TPU v7x, 512 devices: a whole 4x8x8 slice. The times are simulated.
512 devices in a mesh: dp: 64 (over x, z, y_lo), tensor: 8 (over y_hi, core).
Axes of the slice: x: 4, y: 8 (y_hi: 4, y_lo: 2; y = y_hi * 2 + y_lo), z: 8, core: 2. Of those that a mesh axis runs over, the one named last changes fastest.
Arguments:
- pooled: bfloat16 [8192, 1536], P('dp', 'tensor'), may hold values from -16 to 16
- ln_gain: float32 [1536], replicated, may hold values from 0.5 to 1.5
- ln_bias: float32 [1536], replicated, may hold values from -4 to 4
- w_up: bfloat16 [1536, 3072], P(None, 'tensor'), may hold values from -0.15625 to 0.15625
- b_up: float32 [3072], P('tensor'), may hold values from -4 to 4
- w_down: bfloat16 [3072, 1536], P('tensor'), may hold values from -0.21875 to 0.21875
- b_down: float32 [1536], P('tensor'), may hold values from -4 to 4
- text_embed: bfloat16 [8192, 1536], P('dp', 'tensor'), may hold values from -16 to 16
- image_ids: int32 [8192], P('dp'), may hold values from 0 to 8191, as said below
- text_ids: int32 [8192], P('dp'), may hold values from 0 to 8191, as said below
- logit_scale: float32 [1], replicated, may hold values from 9 to 11
- logit_bias: float32 [1], replicated, may hold values from -10.5 to -9.5
- loss_scale: float32 [1], replicated, may hold values from 524288 to 2097152
Outputs:
- loss: float32 [1], replicated
- grad_pooled: bfloat16 [8192, 1536], P('dp', 'tensor')
- grad_down: float32 [3072, 1536], P('tensor', 'dp')
Inputs may be any that keep to these rules, and one draw needn't show every extreme that they name: `image_ids`: each holds every pair id of the batch exactly once, so each image has exactly one positive text. `text_ids`: each holds every pair id of the batch exactly once.
All inputs are finite; a program needn't handle non-finite values.
Results may differ from a plain program's by a relative error of at most 0.0074.
The roundings to bfloat16 on the way count: a program that leaves them out, or rounds other values in their place, can miss the bound.
Values may be sent and summed in bfloat16 or wider, within the bound.
No kernel may reach another device: no remote copies, remote signals or barrier semaphores. Data moves between devices by JAX's collectives and lax.ppermute only.
A program may use at most 128 MiB of HBM per device.

v0:
```python
import jax
import jax.numpy as jnp
from jax import lax
from jax.sharding import PartitionSpec as P


def gelu_fn(values):
    return jax.nn.gelu(values, approximate=True)


def normalize_rows(rows):
    wide = rows.astype(jnp.float32)
    average = jnp.mean(wide, axis=1, keepdims=True)
    centered = wide - average
    inverse = lax.rsqrt(jnp.mean(centered * centered, axis=1, keepdims=True) + 1e-06)
    return (centered * inverse, inverse)


def pair_terms(img_rows, row_ids, txt_rows, txt_ids, temper, offset, factor):
    scores = lax.dot_general(
        img_rows, txt_rows, (((1,), (1,)), ((), ())), preferred_element_type=jnp.float32
    )
    positive = row_ids[:, None] == txt_ids[None, :]
    signs = jnp.where(positive, 1.0, -1.0).astype(jnp.float32)
    logits = temper * scores + offset
    margin = -signs * logits
    row_loss = jnp.sum(jax.nn.softplus(margin), axis=1)
    weights = (-signs * temper * factor * jax.nn.sigmoid(margin)).astype(jnp.bfloat16)
    grad_part = jnp.dot(weights, txt_rows, preferred_element_type=jnp.float32)
    return (grad_part, row_loss)


def shards(
    pooled,
    ln_gain,
    ln_bias,
    w_up,
    b_up,
    w_down,
    b_down,
    text_embed,
    image_ids,
    text_ids,
    logit_scale,
    logit_bias,
    loss_scale,
):
    tensor_count = lax.axis_size("tensor")
    data_count = lax.axis_size("dp")
    local_rows = pooled.shape[0]
    slices = pooled.shape[1]
    batch_total = local_rows * data_count
    offset_cols = lax.axis_index("tensor") * slices
    share_rows = local_rows // tensor_count
    share_start = lax.axis_index("tensor") * share_rows
    rows_full = lax.all_gather(pooled, "tensor", axis=1, tiled=True)
    scaled, inverse = normalize_rows(rows_full)
    normed = (scaled * ln_gain + ln_bias).astype(jnp.bfloat16)
    preact = jnp.dot(normed, w_up, preferred_element_type=jnp.float32) + b_up
    hidden = gelu_fn(preact).astype(jnp.bfloat16)
    partial_out = jnp.dot(hidden, w_down, preferred_element_type=jnp.float32)
    mixed = lax.psum_scatter(partial_out, "tensor", scatter_dimension=1, tiled=True)
    summed = pooled.astype(jnp.float32) + mixed + b_down
    txt_wide = text_embed.astype(jnp.float32)
    img_sq, txt_sq = lax.psum(
        (jnp.sum(summed * summed, axis=1), jnp.sum(txt_wide * txt_wide, axis=1)), "tensor"
    )
    img_norm = jnp.sqrt(img_sq + 1e-06)[:, None]
    img_unit = summed / img_norm
    img_low = img_unit.astype(jnp.bfloat16)
    txt_low = (txt_wide / jnp.sqrt(txt_sq + 1e-06)[:, None]).astype(jnp.bfloat16)
    temper = logit_scale[0]
    offset = logit_bias[0]
    factor = loss_scale[0] / batch_total
    img_full = lax.all_gather(img_low, "tensor", axis=1, tiled=True)
    txt_share = lax.all_to_all(txt_low, "tensor", split_axis=0, concat_axis=1, tiled=True)
    ids_share = lax.dynamic_slice_in_dim(text_ids, share_start, share_rows, 0)
    grad_part, row_loss = pair_terms(
        img_full,
        image_ids,
        lax.all_gather(txt_share, "dp", axis=0, tiled=True),
        lax.all_gather(ids_share, "dp", axis=0, tiled=True),
        temper,
        offset,
        factor,
    )
    grad_unit = lax.psum_scatter(grad_part, "tensor", scatter_dimension=1, tiled=True)
    loss = (lax.psum(jnp.sum(row_loss), ("dp", "tensor")) / batch_total).reshape(1)
    tangent = lax.psum(jnp.sum(img_unit * grad_unit, axis=1), "tensor")
    grad_sum = (grad_unit - img_unit * tangent[:, None]) / img_norm
    grad_low = grad_sum.astype(jnp.bfloat16)
    grad_full = lax.all_gather(grad_low, "tensor", axis=1, tiled=True)
    grad_down = lax.psum_scatter(
        lax.dot_general(
            grad_full, hidden, (((0,), (0,)), ((), ())), preferred_element_type=jnp.float32
        ),
        "dp",
        scatter_dimension=0,
        tiled=True,
    ).T
    grad_hidden = lax.dot_general(
        grad_full, w_down, (((1,), (1,)), ((), ())), preferred_element_type=jnp.float32
    )
    grad_pre = jax.vjp(gelu_fn, preact)[1](grad_hidden)[0].astype(jnp.bfloat16)
    normed_part = lax.dot_general(
        grad_pre, w_up, (((1,), (1,)), ((), ())), preferred_element_type=jnp.float32
    )
    whole_grad = lax.psum(normed_part, "tensor")
    scaled_grad = whole_grad * ln_gain
    centre = jnp.mean(scaled_grad, axis=1, keepdims=True)
    along = jnp.mean(scaled_grad * scaled, axis=1, keepdims=True)
    whole_input = inverse * (scaled_grad - centre - scaled * along)
    grad_input = lax.dynamic_slice_in_dim(whole_input, offset_cols, slices, 1)
    grad_pooled = (grad_sum + grad_input).astype(jnp.bfloat16)
    return (loss, grad_pooled, grad_down)


def solution(mesh):
    placed = (
        P("dp", "tensor"),
        P(),
        P(),
        P(None, "tensor"),
        P("tensor"),
        P("tensor", None),
        P("tensor"),
        P("dp", "tensor"),
        P("dp"),
        P("dp"),
        P(),
        P(),
        P(),
    )
    return jax.shard_map(
        shards,
        mesh=mesh,
        in_specs=placed,
        out_specs=(P(), P("dp", "tensor"), P("tensor", "dp")),
        check_vma=False,
    )
```

profile of v0, /device:TPU:16, one launch (start us, length us, event | category | flops | bytes accessed | tf_op | source)
XLA Modules:
  0.0 901.7 jit_solution(12533611391330237429)
XLA Ops:
  7.2 0.0 copy-start
  7.2 0.0 copy-start.3
  7.2 0.0 copy-start.7
  7.2 0.0 copy-start.11
  7.2 0.0 copy-start.10
  7.2 0.0 reduce-scatter.7.cloned.1.call-start
  7.3 17.3 %all_gather.16 = bf16[128,1536]{0,1:T(8,128)(2,1)S(1)} all-gather(bf16[128,192]{0,1:T(8,128)(2,1)} %param.13), channel_id=1, replica_groups=mesh['dp'=64,'tensor'=8] {'tensor'}, dimensions={1}, use_global_device_ids=true | all-gather | bytes 442368 | tf_op jit(solution)/shard_map/all_gather | solution.py:56
  24.5 0.2 convert_reduce_fusion
  24.8 0.2 fusion.4
  25.0 0.0 copy-done.3
  25.0 0.0 copy-done.7
  25.0 0.0 copy-done.11
  25.0 0.0 copy-done.10
  25.0 1.0 convolution_add_fusion
  26.0 0.0 copy-done
  26.0 0.0 copy-start.5
  26.0 0.0 copy-start.2
  26.0 0.0 copy-start.6
  26.0 1.5 fusion.48
  27.5 0.0 reduce-scatter.7.cloned.1.call-update
  27.5 0.0 all-gather.2.cloned.1.call-start
  27.6 0.0 copy-done.5
  27.6 0.1 copy.20
  27.7 0.1 fusion.23
  27.8 39.2 %reduce-scatter.7.cloned.1.call-done = f32[128,192]{0,1:T(8,128)} async-done(((f32[128,1536]{0,1:T(8,128)}), f32[128,192]{0,1:T(8,128)}) %reduce-scatter.7.cloned.1.call-update) | async-done | bytes 98320 | tf_op jit(solution)/shard_map/reduce_scatter | solution.py:62
  67.0 0.0 copy-done.2
  67.0 0.0 copy-done.6
  67.0 1.0 multiply_reduce_fusion.2
  68.0 17.0 %all-reduce.2 = (f32[128]{0:T(128)S(1)}, f32[128]{0:T(128)S(1)}) all-reduce(f32[128]{0:T(128)S(1)} %multiply_reduce_fusion.2, f32[128]{0:T(128)S(1)} %fusion.23), channel_id=1, replica_groups=mesh['dp'=64,'tensor'=8] {'tensor'}, use_global_device_ids=true, to_apply=%region_4.0 | all-reduce | flops 256 | bytes 2048 | tf_op jit(solution)/shard_map/psum | solution.py:65
  85.0 0.1 fusion.24
  85.1 15.0 %all_to_all.19 = bf16[8,16,192]{2,1,0:T(8,128)(2,1)S(1)} all-to-all(bf16[8,16,192]{2,1,0:T(8,128)(2,1)S(1)} %bitcast.21), channel_id=1, replica_groups=mesh['dp'=64,'tensor'=8] {'tensor'}, dimensions={0} | all-to-all | bytes 98304 | tf_op jit(solution)/shard_map/all_to_all | solution.py:76
  100.1 0.7 all_to_all.17
  100.8 0.0 all-gather.2.cloned.1.call-update
  100.9 0.0 reduce-scatter.9.cloned.1.call-start
  102.9 1.3 dynamic-slice
  104.7 0.0 copy-done.8
  104.7 0.2 dynamic-slice_dynamic-update-slice_fusion
  104.9 24.2 %all-reduce = s32[1024]{0:T(1024)S(1)} all-reduce(s32[1024]{0:T(1024)S(1)} %dynamic-slice_dynamic-update-slice_fusion), channel_id=1, replica_groups=mesh['dp'=64,'tensor'=8] {'dp'}, use_global_device_ids=true, to_apply=%add | all-reduce | flops 1024 | bytes 8192
  129.1 1.0 fusion.49
  130.1 15.0 %all_gather.17 = bf16[128,1536]{0,1:T(8,128)(2,1)S(1)} all-gather(bf16[128,192]{0,1:T(8,128)(2,1)S(1)} %fusion.49), channel_id=1, replica_groups=mesh['dp'=64,'tensor'=8] {'tensor'}, dimensions={1}, use_global_device_ids=true | all-gather | bytes 442368 | tf_op jit(solution)/shard_map/all_gather | solution.py:75
  145.1 262.7 %all-gather.2.cloned.1.call-done = bf16[1024,1536]{1,0:T(8,128)(2,1)} async-done(((bf16[16,1536]{1,0:T(8,128)(2,1)}), bf16[1024,1536]{1,0:T(8,128)(2,1)}) %all-gather.2.cloned.1.call-update) | async-done | bytes 3145744 | tf_op jit(solution)/shard_map/all_gather | solution.py:81
  407.8 0.0 copy-done.12
  407.8 4.0 fusion.5
  411.9 0.0 copy-done.9
  411.9 2.3 fusion.8
  414.2 0.0 reduce-scatter.9.cloned.1.call-update
  414.2 0.0 all-reduce.5.cloned.1.call-start
  414.3 32.5 %reduce-scatter.9.cloned.1.call-done = f32[128,192]{0,1:T(8,128)} async-done(((f32[128,1536]{0,1:T(8,128)}), f32[128,192]{0,1:T(8,128)}) %reduce-scatter.9.cloned.1.call-update) | async-done | bytes 98320 | tf_op jit(solution)/shard_map/reduce_scatter | solution.py:87
  446.8 0.0 copy-done.1
  446.8 1.0 multiply_reduce_fusion.1
  447.8 16.9 %psum.38 = f32[128]{0:T(128)S(1)} all-reduce(f32[128]{0:T(128)S(1)} %multiply_reduce_fusion.1), channel_id=1, replica_groups=mesh['dp'=64,'tensor'=8] {'tensor'}, use_global_device_ids=true, to_apply=%region_11.12 | all-reduce | flops 128 | bytes 1024 | tf_op jit(solution)/shard_map/psum | solution.py:89
  464.7 1.0 fusion.46
  465.7 16.4 %all_gather.19 = bf16[128,1536]{0,1:T(8,128)(2,1)S(1)} all-gather(bf16[128,192]{0,1:T(8,128)(2,1)S(1)} %fusion.46), channel_id=1, replica_groups=mesh['dp'=64,'tensor'=8] {'tensor'}, dimensions={1}, use_global_device_ids=true | all-gather | bytes 442368 | tf_op jit(solution)/shard_map/all_gather | solution.py:92
  482.2 2.0 fusion.25
  484.2 0.0 all-reduce.5.cloned.1.call-update
  484.2 0.0 reduce-scatter.11.cloned.1.call-start
  484.2 1.9 fusion.47
  486.1 0.0 reduce-scatter.11.cloned.1.call-update
  486.2 101.2 %psum.37 = f32[]{:T(128)} all-reduce(f32[]{:T(128)} %get-tuple-element.9), channel_id=1, replica_groups=mesh['dp'=64,'tensor'=8] {'dp','tensor'}, use_global_device_ids=true, to_apply=%region_8.9 | all-reduce | flops 1 | bytes 8 | tf_op jit(solution)/shard_map/psum | solution.py:88
  588.1 0.0 all-reduce.5.cloned.1.call-done
  588.1 1.5 fusion.50
  589.6 0.0 copy-done.4
  589.6 0.7 fusion.30
  590.3 303.7 %reduce-scatter.11.cloned.1.call-done = f32[24,384]{1,0:T(8,128)} async-done(((f32[1536,384]{1,0:T(8,128)}), f32[24,384]{1,0:T(8,128)}) %reduce-scatter.11.cloned.1.call-update) | async-done | bytes 36880
  (12 shorter events, 0.1 us)
Async XLA Ops:
  7.2 18.8 %copy-start = (bf16[384,1536]{1,0:T(8,128)(2,1)S(1)}, bf16[384,1536]{1,0:T(8,128)(2,1)}, u32[]{:S(2)}) copy-start(bf16[384,1536]{1,0:T(8,128)(2,1)} %param.18) | copy-start | bytes 3538948
  7.2 17.8 %copy-start.3 = (bf16[1536,384]{1,0:T(8,128)(2,1)S(1)}, bf16[1536,384]{1,0:T(8,128)(2,1)}, u32[]{:S(2)}) copy-start(bf16[1536,384]{1,0:T(8,128)(2,1)} %param.16) | copy-start | bytes 3538948
  7.2 17.8 %copy-start.7 = (f32[1536]{0:T(1024)S(1)}, f32[1536]{0:T(1024)}, u32[]{:S(2)}) copy-start(f32[1536]{0:T(1024)} %param.14) | copy-start | bytes 18436
  7.2 17.8 %copy-start.11 = (f32[384]{0:T(512)S(1)}, f32[384]{0:T(512)}, u32[]{:S(2)}) copy-start(f32[384]{0:T(512)} %param.17) | copy-start | bytes 4612
  7.2 17.8 %copy-start.10 = (f32[1536]{0:T(1024)S(1)}, f32[1536]{0:T(1024)}, u32[]{:S(2)}) copy-start(f32[1536]{0:T(1024)} %param.15) | copy-start | bytes 18436
  7.2 59.8 %reduce-scatter.7.cloned.1.call-start = ((), (), s32[]{:S(2)}) async-start(), calls=%async_computation.4 | async-start | bytes 884736 | tf_op jit(solution)/shard_map/reduce_scatter | solution.py:62
  26.0 1.6 copy-start.5
  26.0 41.0 %copy-start.2 = (bf16[128,192]{0,1:T(8,128)(2,1)S(1)}, bf16[128,192]{0,1:T(8,128)(2,1)}, u32[]{:S(2)}) copy-start(bf16[128,192]{0,1:T(8,128)(2,1)} %param.13) | copy-start | bytes 147460
  26.0 41.0 %copy-start.6 = (f32[192]{0:T(256)S(1)}, f32[192]{0:T(256)}, u32[]{:S(2)}) copy-start(f32[192]{0:T(256)} %param.19) | copy-start | bytes 2308
  27.5 77.2 %copy-start.8 = (s32[128]{0:T(128)S(1)}, s32[128]{0:T(128)}, u32[]{:S(2)}) copy-start(s32[128]{0:T(128)} %param.22) | copy-start | bytes 1540
  27.5 380.3 %copy-start.12 = (s32[128]{0:T(128)S(1)}, s32[128]{0:T(128)}, u32[]{:S(2)}) copy-start(s32[128]{0:T(128)} %param.21) | copy-start | bytes 1540
  27.5 380.3 %all-gather.2.cloned.1.call-start = ((), (), s32[]{:S(2)}) async-start(), calls=%async_computation.5 | async-start | bytes 3194880 | tf_op jit(solution)/shard_map/all_gather | solution.py:81
  100.9 346.0 %reduce-scatter.9.cloned.1.call-start = ((), (), s32[]{:S(2)}) async-start(), calls=%async_computation.6 | async-start | bytes 884736 | tf_op jit(solution)/shard_map/reduce_scatter | solution.py:87
  407.8 4.0 copy-start.9
  411.9 34.9 %copy-start.1 = (f32[128,192]{0,1:T(8,128)S(1)}, f32[128,192]{0,1:T(8,128)}, u32[]{:S(2)}) copy-start(f32[128,192]{0,1:T(8,128)} %reduce-scatter.7.cloned.1.call-done) | copy-start | bytes 294916
  414.2 173.9 %all-reduce.5.cloned.1.call-start = ((), (), s32[]{:S(2)}) async-start(), calls=%async_computation.7 | async-start | bytes 1572864 | tf_op jit(solution)/shard_map/psum | solution.py:108
  484.2 409.8 %reduce-scatter.11.cloned.1.call-start = ((), (), s32[]{:S(2)}) async-start(), calls=%async_computation.8 | async-start | bytes 2396160
  588.0 1.5 copy-start.4
Sparse Core Ops, SparseCore 0:
  27.7 39.3 reduce-scatter.6
  101.0 306.8 all-gather.1
  414.3 32.4 reduce-scatter.8
  484.3 79.7 all-reduce.4
  567.6 326.3 reduce-scatter.10
where the time goes:
time: 902 us
  waiting for transfers between devices  638 us (71%)
  blocking collectives  223 us (25%)
  between operations  18.3 us (2%)
  matrix products  12.7 us (1%)
    unnamed x6, waiting for transfers between devices  304 us
    all_gather x1, waiting for transfers between devices, shards(): lax.all_gather(txt_share, 'dp', axis=0, tiled=True)  263 us
    psum x1, blocking collectives, shards(): lax.psum(jnp.sum(row_loss), ('dp', 'tensor')) / batch_total  101 us
    reduce_scatter x1, waiting for transfers between devices, shards(): lax.psum_scatter(partial_out, 'tensor', scatter_dimension=1, tiled=True)  39.2 us
    reduce_scatter x1, waiting for transfers between devices, shards(): lax.psum_scatter(grad_part, 'tensor', scatter_dimension=1, tiled=True)  32.5 us
    unnamed x1, blocking collectives  24.2 us
  transfers between devices with their start and end apart: 5, of which 4 were waited for; matrix products, arithmetic and copies ran while one was open for 1% of the time, Pallas kernels for 0%

commit v1 on v0

v1 whole, which is shorter than its diff:
```python
import jax
import jax.numpy as jnp
from jax import lax
from jax.sharding import Mesh, PartitionSpec as P

ROWS = 128
WIDE = 1536
SLICE = 192
EXTRA = 128
IMG = 16
DATA = ("x", "z", "ylo")
TENS = ("yhi", "core")
RING = ("ylo", "yhi", "core")
DIGITS = 8
SPAN = 2.0**26


def gelu_fn(values):
    return jax.nn.gelu(values, approximate=True)


def id_columns(ids):
    high = (ids // 128).astype(jnp.bfloat16)
    low = (ids % 128).astype(jnp.bfloat16)
    pair = jnp.stack([high, low], axis=1)
    return jnp.pad(pair, ((0, 0), (0, EXTRA - 2)))


def read_ids(block):
    wide = block[:, WIDE : WIDE + 2].astype(jnp.float32)
    return wide[:, 0] * 128.0 + wide[:, 1]


def to_digits(value):
    rest = value / SPAN
    digits = []
    for _ in range(DIGITS):
        rest = rest * 64.0
        digit = jnp.floor(rest)
        rest = rest - digit
        digits.append(digit)
    return jnp.stack(digits)


def from_digits(digits):
    total = jnp.float32(0.0)
    for place in range(DIGITS):
        total = total + digits[place] * (SPAN / 64.0 ** (place + 1))
    return total


def halves(values):
    high = values.astype(jnp.bfloat16)
    low = (values - high.astype(jnp.float32)).astype(jnp.bfloat16)
    return high, low


def shards(
    pooled,
    ln_gain,
    ln_bias,
    w_up,
    b_up,
    w_down,
    b_down,
    text_embed,
    image_ids,
    text_ids,
    logit_scale,
    logit_bias,
    loss_scale,
):
    tens = lax.axis_index(TENS)
    row0 = tens * IMG
    col0 = tens * SLICE
    batch = ROWS * 64

    both = lax.all_gather(
        jnp.concatenate([pooled, text_embed], axis=0), TENS, axis=1, tiled=True
    )
    txt_rows = lax.dynamic_slice_in_dim(both, ROWS + row0, IMG, 0).astype(jnp.float32)
    txt_norm = jnp.sqrt(jnp.sum(txt_rows * txt_rows, axis=1, keepdims=True) + 1e-06)
    txt_low = (txt_rows / txt_norm).astype(jnp.bfloat16)
    txt_ids = lax.dynamic_slice_in_dim(text_ids, row0, IMG, 0)
    txt_send = jnp.concatenate([txt_low, id_columns(txt_ids)], axis=1)
    txt_x = lax.all_gather(txt_send, "x", axis=0, tiled=True)
    txt_x, both = lax.optimization_barrier((txt_x, both))
    txt_all = lax.all_gather(txt_x, "z", axis=0, tiled=True)

    wide = both[:ROWS].astype(jnp.float32)
    average = jnp.mean(wide, axis=1, keepdims=True)
    centered = wide - average
    inverse = lax.rsqrt(jnp.mean(centered * centered, axis=1, keepdims=True) + 1e-06)
    scaled = centered * inverse
    normed = (scaled * ln_gain + ln_bias).astype(jnp.bfloat16)
    preact = jnp.dot(normed, w_up, preferred_element_type=jnp.float32) + b_up
    hidden = gelu_fn(preact).astype(jnp.bfloat16)
    bias_row = lax.dynamic_update_slice_in_dim(
        jnp.zeros((WIDE,), jnp.float32), b_down, col0, 0
    )
    part = jnp.dot(hidden, w_down, preferred_element_type=jnp.float32) + bias_row
    parts = lax.all_to_all(
        part.astype(jnp.bfloat16), TENS, split_axis=0, concat_axis=0, tiled=True
    )
    mixed = jnp.sum(parts.reshape(8, IMG, WIDE).astype(jnp.float32), axis=0)
    own = lax.dynamic_slice_in_dim(both, row0, IMG, 0).astype(jnp.float32)
    summed = own + mixed
    img_norm = jnp.sqrt(jnp.sum(summed * summed, axis=1, keepdims=True) + 1e-06)
    img_unit = summed / img_norm
    img_ids = lax.dynamic_slice_in_dim(image_ids, row0, IMG, 0)
    img_send = jnp.concatenate([img_unit.astype(jnp.bfloat16), id_columns(img_ids)], axis=1)
    img_all = lax.all_gather(img_send, RING, axis=0, tiled=True)

    temper = logit_scale[0]
    offset = logit_bias[0]
    factor = loss_scale[0] / batch
    txt_full = txt_all[:, :WIDE]
    scores = lax.dot_general(
        img_all[:, :WIDE], txt_full, (((1,), (1,)), ((), ())), preferred_element_type=jnp.float32
    )
    positive = read_ids(img_all)[:, None] == read_ids(txt_all)[None, :]
    signs = jnp.where(positive, 1.0, -1.0).astype(jnp.float32)
    margin = -signs * (temper * scores + offset)
    loss_part = jnp.sum(jax.nn.softplus(margin))
    weights = (-signs * temper * factor * jax.nn.sigmoid(margin)).astype(jnp.bfloat16)
    unit_part = jnp.dot(weights, txt_full, preferred_element_type=jnp.float32)
    unit_parts = lax.all_to_all(
        unit_part.astype(jnp.bfloat16), RING, split_axis=0, concat_axis=0, tiled=True
    )
    grad_unit = jnp.sum(unit_parts.reshape(16, IMG, WIDE).astype(jnp.float32), axis=0)
    tangent = jnp.sum(img_unit * grad_unit, axis=1, keepdims=True)
    grad_low = ((grad_unit - img_unit * tangent) / img_norm).astype(jnp.bfloat16)
    loss_row = jnp.pad(to_digits(loss_part).astype(jnp.bfloat16), (0, EXTRA - DIGITS))
    grad_send = jnp.concatenate([grad_low, jnp.broadcast_to(loss_row, (IMG, EXTRA))], axis=1)
    grad_all = lax.all_gather(grad_send, TENS, axis=0, tiled=True)
    grad_full = grad_all[:, :WIDE]

    group_digits = jnp.sum(
        grad_all.reshape(8, IMG, WIDE + EXTRA)[:, 0, WIDE : WIDE + DIGITS].astype(jnp.float32), axis=0
    )
    group_loss = from_digits(group_digits)
    down_part = lax.dot_general(
        grad_full, hidden, (((0,), (0,)), ((), ())), preferred_element_type=jnp.float32
    ).astype(jnp.bfloat16)
    loss_block = jnp.zeros((16, 384), jnp.bfloat16) + jnp.pad(
        to_digits(group_loss).astype(jnp.bfloat16), (0, 384 - DIGITS)
    )
    down_send = jnp.concatenate(
        [down_part.reshape(4, 384, 384), jnp.broadcast_to(loss_block, (4, 16, 384))], axis=1
    ).reshape(1600, 384)
    down_x = lax.psum_scatter(down_send, "x", scatter_dimension=0, tiled=True)

    grad_hidden = lax.dot_general(
        grad_full, w_down, (((1,), (1,)), ((), ())), preferred_element_type=jnp.float32
    )
    grad_pre = jax.vjp(gelu_fn, preact)[1](grad_hidden)[0].astype(jnp.bfloat16)
    normed_part = lax.dot_general(
        w_up, grad_pre, (((1,), (1,)), ((), ())), preferred_element_type=jnp.float32
    )
    gained = normed_part * ln_gain[:, None]
    sum_h = jnp.sum(gained, axis=0)
    sum_hs = jnp.sum(gained * scaled.T, axis=0)
    h_hi, h_lo = halves(sum_h)
    s_hi, s_lo = halves(sum_hs)
    stats = jnp.pad(jnp.stack([h_hi, h_lo, s_hi, s_lo]), ((0, 12), (0, 0)))
    norm_send = jnp.concatenate(
        [
            normed_part.astype(jnp.bfloat16).reshape(8, SLICE, ROWS),
            jnp.broadcast_to(stats, (8, 16, ROWS)),
        ],
        axis=1,
    )
    norm_parts = lax.all_to_all(norm_send, TENS, split_axis=0, concat_axis=0, tiled=True)
    norm_sum = jnp.sum(norm_parts.astype(jnp.float32), axis=0)
    centre = (norm_sum[SLICE] + norm_sum[SLICE + 1]) / WIDE
    along = (norm_sum[SLICE + 2] + norm_sum[SLICE + 3]) / WIDE
    gain_own = lax.dynamic_slice_in_dim(ln_gain, col0, SLICE, 0)
    scaled_own = (pooled.astype(jnp.float32) - average) * inverse
    h_own = norm_sum[:SLICE].T * gain_own[None, :]
    grad_own = lax.dynamic_slice_in_dim(grad_full, col0, SLICE, 1).astype(jnp.float32)
    grad_input = inverse * (h_own - centre[:, None] - scaled_own * along[:, None])
    grad_pooled = (grad_own + grad_input).astype(jnp.bfloat16)

    digits_x = down_x[384, :DIGITS].astype(jnp.float32)
    loss_x = from_digits(digits_x)
    loss_tail = jnp.pad(
        jnp.stack([*three(loss_x)]), (0, 384 - 3)
    )
    last_send = jnp.concatenate(
        [
            down_x[:384].reshape(16, 24, 384),
            jnp.broadcast_to(loss_tail, (16, 8, 384)),
        ],
        axis=1,
    )
    last = lax.all_to_all(last_send, ("z", "ylo"), split_axis=0, concat_axis=0, tiled=True)
    last_sum = jnp.sum(last.astype(jnp.float32), axis=0)
    grad_down = last_sum[:24].T
    loss = (jnp.sum(last_sum[24, :3]) / batch).reshape(1)
    return (loss, grad_pooled, grad_down)


def three(value):
    first = value.astype(jnp.bfloat16)
    rest = value - first.astype(jnp.float32)
    second = rest.astype(jnp.bfloat16)
    third = (rest - second.astype(jnp.float32)).astype(jnp.bfloat16)
    return first, second, third


def solution(mesh):
    inner = Mesh(mesh.devices.reshape(4, 8, 2, 4, 2), ("x", "z", "ylo", "yhi", "core"))
    placed = (
        P(DATA, TENS),
        P(),
        P(),
        P(None, TENS),
        P(TENS),
        P(TENS, None),
        P(TENS),
        P(DATA, TENS),
        P(DATA),
        P(DATA),
        P(),
        P(),
        P(),
    )
    return jax.shard_map(
        shards,
        mesh=inner,
        in_specs=placed,
        out_specs=(P(), P(DATA, TENS), P(TENS, DATA)),
        check_vma=False,
    )
```

time: 902 us -> 213 us (0.24)
  the two profiles are of different devices: /device:TPU:16 before, /device:TPU:1 now
where the time goes in v1:
time: 213 us; the launch traced here: 212 us
  blocking collectives  65.9 us (31%)
  waiting for transfers between devices  60.7 us (28%)
  starting transfers between devices  29.7 us (14%)
  between operations  29 us (14%)
  matrix products  10.5 us (5%)
  other arithmetic  10.1 us (5%)
  local copies, waits for them, and re-layouts  6.11 us (3%)
    all_gather x1, blocking collectives, shards(): lax.all_gather(jnp.concatenate([pooled, text_embed], axis=0), TENS, axis=...  22.2 us
    all_to_all x1, waiting for transfers between devices, shards(): lax.all_to_all(unit_part.astype(jnp.bfloat16), RING, split_axis=0, concat...  21.8 us
    all_gather x1, blocking collectives, shards(): img_all = lax.all_gather(img_send, RING, axis=0, tiled=True)  19.9 us
    reduce_scatter x1, waiting for transfers between devices, shards(): down_x = lax.psum_scatter(down_send, 'x', scatter_dimension=0, tiled=True)  16.7 us
    all_gather x1, blocking collectives, shards(): grad_all = lax.all_gather(grad_send, TENS, axis=0, tiled=True)  13.8 us
    all_to_all x1, waiting for transfers between devices, shards(): lax.all_to_all(last_send, ('z', 'ylo'), split_axis=0, concat_axis=0, tile...  11.3 us
    all_to_all x1, waiting for transfers between devices, shards(): lax.all_to_all(part.astype(jnp.bfloat16), TENS, split_axis=0, concat_axis...  10.7 us
    all_to_all x1, starting transfers between devices, shards(): lax.all_to_all(unit_part.astype(jnp.bfloat16), RING, split_axis=0, concat...  10 us
  transfers between devices with their start and end apart: 6, of which 4 were waited for; matrix products, arithmetic and copies ran while one was open for 6% of the time, Pallas kernels for 0%

profile of v1, /device:TPU:1, one launch (start us, length us, event | category | flops | bytes accessed | tf_op | source)
XLA Modules:
  0.0 212.0 jit_solution(17473926050176859577)
XLA Ops:
  7.2 0.0 all-gather.2.cloned.1.call-start
  7.2 0.8 convert_bitcast_fusion.1
  8.1 0.7 convert_bitcast_fusion.2
  8.8 0.1 copy.56
  8.9 0.8 pad_maximum_fusion.3
  9.8 22.2 %all_gather.15 = bf16[256,1536]{0,1:T(8,128)(2,1)S(1)} all-gather(bf16[256,192]{0,1:T(8,128)(2,1)S(1)} %pad_maximum_fusion.3), channel_id=1, replica_groups=mesh['x'=4,'z'=8,'ylo'=2,'yhi'=4,'core'=2] {'yhi','core'}, dimensions={1}, use_global_device_ids=true | all-gather | bytes 884736 | tf_op jit(solution)/shard_map/all_gather | solution.py:78
  31.9 0.2 constant_dynamic-slice_fusion.1
  32.1 0.1 copy.54
  32.2 0.1 fusion.46
  32.4 0.1 fusion.47
  32.5 10.0 %all_gather.16 = bf16[64,1664]{1,0:T(8,128)(2,1)} all-gather(bf16[16,1664]{1,0:T(8,128)(2,1)S(1)} %fusion.63), channel_id=1, replica_groups=mesh['x'=4,'z'=8,'ylo'=2,'yhi'=4,'core'=2] {'x'}, dimensions={0}, use_global_device_ids=true | all-gather | bytes 266240 | tf_op jit(solution)/shard_map/all_gather | solution.py:86
  42.6 0.3 copy.49
  42.9 0.1 convert_reduce_fusion.1
  43.0 0.3 fusion.20
  43.3 1.7 convolution_add_fusion.1
  45.0 0.3 dynamic_update_slice.5
  45.3 1.1 fusion
  46.5 6.7 %all-to-all-start = ((bf16[8,16,1536]{2,1,0:T(8,128)(2,1)}), bf16[8,16,1536]{2,1,0:T(8,128)(2,1)S(1)}, u32[]{:S(2)}, u32[]{:S(2)}) async-start(bf16[8,16,1536]{2,1,0:T(8,128)(2,1)} %bitcast.2), calls=%async_computation | async-start | bytes 786432 | tf_op jit(solution)/shard_map/all_to_all | solution.py:102
  53.2 0.1 copy.57
  55.2 10.7 %all-to-all-done = bf16[8,16,1536]{2,1,0:T(8,128)(2,1)S(1)} async-done(((bf16[8,16,1536]{2,1,0:T(8,128)(2,1)}), bf16[8,16,1536]{2,1,0:T(8,128)(2,1)S(1)}, u32[]{:S(2)}, u32[]{:S(2)}) %all-to-all-start) | async-done | bytes 393248 | tf_op jit(solution)/shard_map/all_to_all | solution.py:102
  65.9 0.1 convert_reduce_fusion.4
  66.0 0.1 multiply_reduce_fusion.2
  66.2 0.1 fusion.104
  66.3 19.9 %all_gather.17 = bf16[256,1664]{1,0:T(8,128)(2,1)S(1)} all-gather(bf16[16,1664]{1,0:T(8,128)(2,1)S(1)} %fusion.64), channel_id=1, replica_groups=mesh['x'=4,'z'=8,'ylo'=2,'yhi'=4,'core'=2] {'ylo','yhi','core'}, dimensions={0}, use_global_device_ids=true | all-gather | bytes 905216 | tf_op jit(solution)/shard_map/all_gather | solution.py:112
  86.2 0.2 fusion.43
  86.4 0.0 all-gather.2.cloned.1.call-done
  86.4 0.9 slice_convert_fusion
  87.3 0.2 fusion.28
  87.6 3.1 %fusion.22 = (f32[]{:T(128)}, f32[256,512]{1,0:T(8,128)S(1)}) fusion(f32[]{:T(128)} %bitcast.78, bf16[512,1664]{1,0:T(8,128)(2,1)} %all-gather.2.cloned.1.call-done, bf16[256,1664]{1,0:T(8,128)(2,1)S(1)} %all_gather.17, f32[]{:T(128)} %bitcast.77, f32[512]{0:T(512)S(1)} %fusion.28, f32[256]{0:T(256)S(1)} %fusion.43), kind=kOutput, calls=%fused_computation.29 | convolution fusion | flops 404357120 | bytes 2887684 | tf_op jit(solution)/shard_map/dot_general | solution.py:118
  90.7 1.6 convolution_convert_fusion.1
  92.2 10.0 %all-to-all-start.1 = ((bf16[16,16,1536]{2,1,0:T(8,128)(2,1)}), bf16[16,16,1536]{2,1,0:T(8,128)(2,1)S(1)}, u32[]{:S(2)}, u32[]{:S(2)}) async-start(bf16[16,16,1536]{2,1,0:T(8,128)(2,1)} %bitcast.84), calls=%async_computation.1 | async-start | bytes 1572864 | tf_op jit(solution)/shard_map/all_to_all | solution.py:127
  102.3 0.0 reduce-scatter.2.cloned.1.call-start
  103.0 0.1 stack.123
  103.1 21.8 %all-to-all-done.1 = bf16[16,16,1536]{2,1,0:T(8,128)(2,1)S(1)} async-done(((bf16[16,16,1536]{2,1,0:T(8,128)(2,1)}), bf16[16,16,1536]{2,1,0:T(8,128)(2,1)S(1)}, u32[]{:S(2)}, u32[]{:S(2)}) %all-to-all-start.1) | async-done | bytes 786464 | tf_op jit(solution)/shard_map/all_to_all | solution.py:127
  125.0 0.1 convert_reduce_fusion
  125.1 0.2 multiply_reduce_fusion.1
  125.3 0.1 divide_convert_fusion
  125.4 13.8 %all_gather.19 = bf16[128,1664]{1,0:T(8,128)(2,1)S(1)} all-gather(bf16[16,1664]{1,0:T(8,128)(2,1)S(1)} %pad_maximum_fusion.4), channel_id=1, replica_groups=mesh['x'=4,'z'=8,'ylo'=2,'yhi'=4,'core'=2] {'yhi','core'}, dimensions={0}, use_global_device_ids=true | all-gather | bytes 479232 | tf_op jit(solution)/shard_map/all_gather | solution.py:135
  139.2 0.5 convolution_convert_fusion
  139.7 0.3 copy-done.1
  140.0 0.7 fusion.106
  145.8 0.1 stack.132
  146.0 1.2 pad_maximum_fusion
  147.1 1.0 copy-done.2
  148.1 2.5 %multiply_reduce_fusion = (f32[128]{0:T(128)S(1)}, f32[128]{0:T(128)S(1)}, bf16[1536,128]{0,1:T(8,128)(2,1)S(1)}) fusion(f32[1536]{0:T(1024)S(1)} %copy-done.6, f32[128]{0:T(128)S(1)} %add_rsqrt_fusion, f32[128]{0:T(128)S(1)} %broadcast_multiply_fusion, bf16[256,1536]{1,0:T(8,128)(2,1)S(1)} %copy.49, bf16[1536,384]{1,0:T(8,128)(2,1)} %param.16, ...), kind=kOutput, calls=%fused_computation.28 | convolution fusion | flops 304545536 | bytes 3745792 | tf_op jit(solution)/shard_map/dot_general | solution.py:157
  150.6 0.2 copy.53
  150.9 0.8 pad_maximum_fusion.1
  151.7 4.6 %all-to-all-start.3 = ((bf16[8,208,128]{2,1,0:T(8,128)(2,1)}), bf16[8,208,128]{2,1,0:T(8,128)(2,1)S(1)}, u32[]{:S(2)}, u32[]{:S(2)}) async-start(bf16[8,208,128]{2,1,0:T(8,128)(2,1)} %pad_maximum_fusion.1), calls=%async_computation.4 | async-start | bytes 851968 | tf_op jit(solution)/shard_map/all_to_all | solution.py:173
  156.3 16.7 %reduce-scatter.2.cloned.1.call-done = bf16[400,384]{1,0:T(8,128)(2,1)} async-done(((bf16[1600,384]{1,0:T(8,128)(2,1)}), bf16[400,384]{1,0:T(8,128)(2,1)}) %reduce-scatter.2.cloned.1.call-update) | async-done | bytes 307216 | tf_op jit(solution)/shard_map/reduce_scatter | solution.py:151
  173.0 0.7 slice_convert_fusion.3
  173.7 0.7 fusion.105
  179.4 1.0 slice.163
  180.4 0.1 fusion.78
  180.5 0.8 pad_maximum_fusion.2
  181.3 8.3 %all-to-all-start.2 = ((bf16[16,32,384]{2,1,0:T(8,128)(2,1)}), bf16[16,32,384]{2,1,0:T(8,128)(2,1)S(1)}, u32[]{:S(2)}, u32[]{:S(2)}) async-start(bf16[16,32,384]{2,1,0:T(8,128)(2,1)} %pad_maximum_fusion.2), calls=%async_computation.3 | async-start | bytes 786432 | tf_op jit(solution)/shard_map/all_to_all | solution.py:196
  189.6 0.1 dynamic_slice.23
  189.7 0.1 constant_dynamic-slice_fusion
  189.8 0.1 copy.58
  189.9 0.1 convert_reduce_fusion.2
  190.0 0.7 fusion.55
  190.8 11.3 %all-to-all-done.2 = bf16[16,32,384]{2,1,0:T(8,128)(2,1)S(1)} async-done(((bf16[16,32,384]{2,1,0:T(8,128)(2,1)}), bf16[16,32,384]{2,1,0:T(8,128)(2,1)S(1)}, u32[]{:S(2)}, u32[]{:S(2)}) %all-to-all-start.2) | async-done | bytes 393248 | tf_op jit(solution)/shard_map/all_to_all | solution.py:196
  202.1 0.1 convert_reduce_fusion.3
  202.2 0.6 slice_bitcast_fusion
  202.8 0.6 slice_reduce_fusion
  (44 shorter events, 0.3 us)
Async XLA Ops:
  7.2 38.2 %copy-start = (bf16[384,1536]{1,0:T(8,128)(2,1)S(1)}, bf16[384,1536]{1,0:T(8,128)(2,1)}, u32[]{:S(2)}) copy-start(bf16[384,1536]{1,0:T(8,128)(2,1)} %param.18) | copy-start | bytes 3538948
  7.2 79.2 %all-gather.2.cloned.1.call-start = ((), (), s32[]{:S(2)}) async-start(), calls=%async_computation.5 | async-start | bytes 1916928 | tf_op jit(solution)/shard_map/all_gather | solution.py:88
  42.5 0.7 copy-start.6
  42.5 0.7 copy-start.7
  42.6 0.7 copy-start.8
  43.3 1.8 copy-start.5
  46.5 19.5 %all-to-all-start = ((bf16[8,16,1536]{2,1,0:T(8,128)(2,1)}), bf16[8,16,1536]{2,1,0:T(8,128)(2,1)S(1)}, u32[]{:S(2)}, u32[]{:S(2)}) async-start(bf16[8,16,1536]{2,1,0:T(8,128)(2,1)} %bitcast.2), calls=%async_computation | async-start | bytes 786432 | tf_op jit(solution)/shard_map/all_to_all | solution.py:102
  87.6 3.1 %copy-start.4 = (bf16[512,1664]{1,0:T(8,128)(2,1)S(1)}, bf16[512,1664]{1,0:T(8,128)(2,1)}, u32[]{:S(2)}) copy-start(bf16[512,1664]{1,0:T(8,128)(2,1)} %all-gather.2.cloned.1.call-done) | copy-start | bytes 5111812
  92.2 32.7 %all-to-all-start.1 = ((bf16[16,16,1536]{2,1,0:T(8,128)(2,1)}), bf16[16,16,1536]{2,1,0:T(8,128)(2,1)S(1)}, u32[]{:S(2)}, u32[]{:S(2)}) async-start(bf16[16,16,1536]{2,1,0:T(8,128)(2,1)} %bitcast.84), calls=%async_computation.1 | async-start | bytes 1572864 | tf_op jit(solution)/shard_map/all_to_all | solution.py:127
  102.3 70.7 %reduce-scatter.2.cloned.1.call-start = ((), (), s32[]{:S(2)}) async-start(), calls=%async_computation.6 | async-start | bytes 1536000 | tf_op jit(solution)/shard_map/reduce_scatter | solution.py:151
  139.2 0.8 copy-start.1
  147.1 1.0 copy-start.2
  151.7 29.6 %all-to-all-start.3 = ((bf16[8,208,128]{2,1,0:T(8,128)(2,1)}), bf16[8,208,128]{2,1,0:T(8,128)(2,1)S(1)}, u32[]{:S(2)}, u32[]{:S(2)}) async-start(bf16[8,208,128]{2,1,0:T(8,128)(2,1)} %pad_maximum_fusion.1), calls=%async_computation.4 | async-start | bytes 851968 | tf_op jit(solution)/shard_map/all_to_all | solution.py:173
  181.3 8.7 %copy-start.3 = (bf16[128,192]{0,1:T(8,128)(2,1)S(1)}, bf16[128,192]{0,1:T(8,128)(2,1)}, u32[]{:S(2)}) copy-start(bf16[128,192]{0,1:T(8,128)(2,1)} %param.13) | copy-start | bytes 147460
  181.3 20.8 %all-to-all-start.2 = ((bf16[16,32,384]{2,1,0:T(8,128)(2,1)}), bf16[16,32,384]{2,1,0:T(8,128)(2,1)S(1)}, u32[]{:S(2)}, u32[]{:S(2)}) async-start(bf16[16,32,384]{2,1,0:T(8,128)(2,1)} %pad_maximum_fusion.2), calls=%async_computation.3 | async-start | bytes 786432 | tf_op jit(solution)/shard_map/all_to_all | solution.py:196
Sparse Core Ops, SparseCore 0:
  42.7 42.4 all-gather.1
  147.3 25.6 reduce-scatter.1

commit v2 on v1

--- a/solution.py
+++ b/solution.py
@@ -11,8 +11,9 @@
 DATA = ("x", "z", "ylo")
 TENS = ("yhi", "core")
 RING = ("ylo", "yhi", "core")
-DIGITS = 8
-SPAN = 2.0**26
+LANES = 64
+DIGITS = 16
+SPAN = 2.0**16
 
 
 def gelu_fn(values):
@@ -31,28 +32,32 @@
     return wide[:, 0] * 128.0 + wide[:, 1]
 
 
-def to_digits(value):
-    rest = value / SPAN
-    digits = []
-    for _ in range(DIGITS):
-        rest = rest * 64.0
-        digit = jnp.floor(rest)
-        rest = rest - digit
-        digits.append(digit)
-    return jnp.stack(digits)
+def to_digits(values):
+    places = 4.0 ** jnp.arange(1, DIGITS + 1, dtype=jnp.float32)[:, None]
+    upper = jnp.floor(values[None, :] * (places / SPAN))
+    lower = jnp.floor(values[None, :] * (places / (4.0 * SPAN)))
+    return (upper - 4.0 * lower).astype(jnp.bfloat16)
 
 
 def from_digits(digits):
-    total = jnp.float32(0.0)
-    for place in range(DIGITS):
-        total = total + digits[place] * (SPAN / 64.0 ** (place + 1))
-    return total
-
-
-def halves(values):
-    high = values.astype(jnp.bfloat16)
-    low = (values - high.astype(jnp.float32)).astype(jnp.bfloat16)
-    return high, low
+    places = SPAN / 4.0 ** jnp.arange(1, DIGITS + 1, dtype=jnp.float32)[:, None]
+    return jnp.sum(digits.astype(jnp.float32) * places, axis=0)
+
+
+def pieces(values, count):
+    parts = []
+    for _ in range(count):
+        part = lax.reduce_precision(values, 8, 7)
+        parts.append(part.astype(jnp.bfloat16))
+        values = values - part
+    return jnp.stack(parts)
+
+
+def spread(block, axis, count):
+    send = jnp.broadcast_to(block[None], (count,) + block.shape)
+    return lax.all_to_all(send, axis, split_axis=0, concat_axis=0, tiled=True).reshape(
+        count * block.shape[0], block.shape[1]
+    )
 
 
 def shards(
@@ -82,9 +87,7 @@
     txt_norm = jnp.sqrt(jnp.sum(txt_rows * txt_rows, axis=1, keepdims=True) + 1e-06)
     txt_low = (txt_rows / txt_norm).astype(jnp.bfloat16)
     txt_ids = lax.dynamic_slice_in_dim(text_ids, row0, IMG, 0)
-    txt_send = jnp.concatenate([txt_low, id_columns(txt_ids)], axis=1)
-    txt_x = lax.all_gather(txt_send, "x", axis=0, tiled=True)
-    txt_x, both = lax.optimization_barrier((txt_x, both))
+    txt_x = spread(jnp.concatenate([txt_low, id_columns(txt_ids)], axis=1), "x", 4)
     txt_all = lax.all_gather(txt_x, "z", axis=0, tiled=True)
 
     wide = both[:ROWS].astype(jnp.float32)
@@ -95,6 +98,7 @@
     normed = (scaled * ln_gain + ln_bias).astype(jnp.bfloat16)
     preact = jnp.dot(normed, w_up, preferred_element_type=jnp.float32) + b_up
     hidden = gelu_fn(preact).astype(jnp.bfloat16)
+    hidden_other = lax.ppermute(hidden, "ylo", [(0, 1), (1, 0)])
     bias_row = lax.dynamic_update_slice_in_dim(
         jnp.zeros((WIDE,), jnp.float32), b_down, col0, 0
     )
@@ -121,7 +125,7 @@
     positive = read_ids(img_all)[:, None] == read_ids(txt_all)[None, :]
     signs = jnp.where(positive, 1.0, -1.0).astype(jnp.float32)
     margin = -signs * (temper * scores + offset)
-    loss_part = jnp.sum(jax.nn.softplus(margin))
+    loss_part = jnp.sum(jnp.sum(jax.nn.softplus(margin), axis=0).reshape(8, LANES), axis=0)
     weights = (-signs * temper * factor * jax.nn.sigmoid(margin)).astype(jnp.bfloat16)
     unit_part = jnp.dot(weights, txt_full, preferred_element_type=jnp.float32)
     unit_parts = lax.all_to_all(
@@ -130,24 +134,32 @@
     grad_unit = jnp.sum(unit_parts.reshape(16, IMG, WIDE).astype(jnp.float32), axis=0)
     tangent = jnp.sum(img_unit * grad_unit, axis=1, keepdims=True)
     grad_low = ((grad_unit - img_unit * tangent) / img_norm).astype(jnp.bfloat16)
-    loss_row = jnp.pad(to_digits(loss_part).astype(jnp.bfloat16), (0, EXTRA - DIGITS))
-    grad_send = jnp.concatenate([grad_low, jnp.broadcast_to(loss_row, (IMG, EXTRA))], axis=1)
-    grad_all = lax.all_gather(grad_send, TENS, axis=0, tiled=True)
-    grad_full = grad_all[:, :WIDE]
-
-    group_digits = jnp.sum(
-        grad_all.reshape(8, IMG, WIDE + EXTRA)[:, 0, WIDE : WIDE + DIGITS].astype(jnp.float32), axis=0
-    )
-    group_loss = from_digits(group_digits)
+    loss_block = jnp.pad(to_digits(loss_part), ((0, 0), (0, EXTRA - LANES)))
+    grad_all = lax.all_gather(
+        jnp.concatenate([grad_low, loss_block], axis=1), RING, axis=0, tiled=True
+    )
+    ylo = lax.axis_index("ylo")
+    grad_full = lax.dynamic_slice(grad_all, (ylo * ROWS, 0), (ROWS, WIDE))
+    grad_other = lax.dynamic_slice(grad_all, ((1 - ylo) * ROWS, 0), (ROWS, WIDE))
     down_part = lax.dot_general(
-        grad_full, hidden, (((0,), (0,)), ((), ())), preferred_element_type=jnp.float32
+        jnp.concatenate([grad_full, grad_other], axis=0),
+        jnp.concatenate([hidden, hidden_other], axis=0),
+        (((0,), (0,)), ((), ())),
+        preferred_element_type=jnp.float32,
+    )
+    down_part = lax.dynamic_index_in_dim(
+        down_part.reshape(4, 8, 2, 24, 384), ylo, 2, keepdims=False
     ).astype(jnp.bfloat16)
-    loss_block = jnp.zeros((16, 384), jnp.bfloat16) + jnp.pad(
-        to_digits(group_loss).astype(jnp.bfloat16), (0, 384 - DIGITS)
-    )
+    ring_digits = jnp.sum(
+        grad_all.reshape(16, IMG, WIDE + EXTRA)[:, :, WIDE:].astype(jnp.float32), axis=0
+    ).astype(jnp.bfloat16)
     down_send = jnp.concatenate(
-        [down_part.reshape(4, 384, 384), jnp.broadcast_to(loss_block, (4, 16, 384))], axis=1
-    ).reshape(1600, 384)
+        [
+            down_part.reshape(4, 192, 384),
+            jnp.broadcast_to(jnp.pad(ring_digits, ((0, 0), (0, 256))), (4, IMG, 384)),
+        ],
+        axis=1,
+    ).reshape(832, 384)
     down_x = lax.psum_scatter(down_send, "x", scatter_dimension=0, tiled=True)
 
     grad_hidden = lax.dot_general(
@@ -160,9 +172,9 @@
     gained = normed_part * ln_gain[:, None]
     sum_h = jnp.sum(gained, axis=0)
     sum_hs = jnp.sum(gained * scaled.T, axis=0)
-    h_hi, h_lo = halves(sum_h)
-    s_hi, s_lo = halves(sum_hs)
-    stats = jnp.pad(jnp.stack([h_hi, h_lo, s_hi, s_lo]), ((0, 12), (0, 0)))
+    stats = jnp.pad(
+        pieces(jnp.stack([sum_h, sum_hs]), 2).reshape(4, ROWS), ((0, 12), (0, 0))
+    )
     norm_send = jnp.concatenate(
         [
             normed_part.astype(jnp.bfloat16).reshape(8, SLICE, ROWS),
@@ -172,8 +184,8 @@
     )
     norm_parts = lax.all_to_all(norm_send, TENS, split_axis=0, concat_axis=0, tiled=True)
     norm_sum = jnp.sum(norm_parts.astype(jnp.float32), axis=0)
-    centre = (norm_sum[SLICE] + norm_sum[SLICE + 1]) / WIDE
-    along = (norm_sum[SLICE + 2] + norm_sum[SLICE + 3]) / WIDE
+    centre = (norm_sum[SLICE] + norm_sum[SLICE + 2]) / WIDE
+    along = (norm_sum[SLICE + 1] + norm_sum[SLICE + 3]) / WIDE
     gain_own = lax.dynamic_slice_in_dim(ln_gain, col0, SLICE, 0)
     scaled_own = (pooled.astype(jnp.float32) - average) * inverse
     h_own = norm_sum[:SLICE].T * gain_own[None, :]
@@ -181,35 +193,21 @@
     grad_input = inverse * (h_own - centre[:, None] - scaled_own * along[:, None])
     grad_pooled = (grad_own + grad_input).astype(jnp.bfloat16)
 
-    digits_x = down_x[384, :DIGITS].astype(jnp.float32)
-    loss_x = from_digits(digits_x)
     loss_tail = jnp.pad(
-        jnp.stack([*three(loss_x)]), (0, 384 - 3)
+        pieces(from_digits(down_x[192:, :LANES]), 3), ((0, 5), (0, 384 - LANES))
     )
     last_send = jnp.concatenate(
-        [
-            down_x[:384].reshape(16, 24, 384),
-            jnp.broadcast_to(loss_tail, (16, 8, 384)),
-        ],
-        axis=1,
-    )
-    last = lax.all_to_all(last_send, ("z", "ylo"), split_axis=0, concat_axis=0, tiled=True)
+        [down_x[:192].reshape(8, 24, 384), jnp.broadcast_to(loss_tail, (8, 8, 384))], axis=1
+    )
+    last = lax.all_to_all(last_send, "z", split_axis=0, concat_axis=0, tiled=True)
     last_sum = jnp.sum(last.astype(jnp.float32), axis=0)
     grad_down = last_sum[:24].T
-    loss = (jnp.sum(last_sum[24, :3]) / batch).reshape(1)
+    loss = (jnp.sum(last_sum[24:27, :LANES]) / batch).reshape(1)
     return (loss, grad_pooled, grad_down)
 
 
-def three(value):
-    first = value.astype(jnp.bfloat16)
-    rest = value - first.astype(jnp.float32)
-    second = rest.astype(jnp.bfloat16)
-    third = (rest - second.astype(jnp.float32)).astype(jnp.bfloat16)
-    return first, second, third
-
-
 def solution(mesh):
-    inner = Mesh(mesh.devices.reshape(4, 8, 2, 4, 2), ("x", "z", "ylo", "yhi", "core"))
+    inner = Mesh(mesh.devices.reshape(4, 8, 2, 4, 2), DATA + TENS)
     placed = (
         P(DATA, TENS),
         P(),

time: 213 us -> 200 us (0.939)
  between operations: 29 us -> 18.1 us
  waiting for transfers between devices: 60.7 us -> 56.9 us
  starting transfers between devices: 29.7 us -> 32.1 us
    reduce_scatter x1, waiting for transfers between devices: 16.7 us -> 1.96 us  [shards(): down_x = lax.psum_scatter(down_send, 'x', scatter_dimension=0, tiled=True)]
    all_to_all x1, waiting for transfers between devices: 0.01 us -> 11.8 us  [shards(): lax.all_to_all(norm_send, TENS, split_axis=0, concat_axis=0, tiled=True)]
    ppermute x0 -> x1, starting transfers between devices: none -> 3.3 us  [shards(): hidden_other = lax.ppermute(hidden, 'ylo', [(0, 1), (1, 0)])]
    all_to_all x1, waiting for transfers between devices: 21.8 us -> 19.1 us  [shards(): lax.all_to_all(unit_part.astype(jnp.bfloat16), RING, split_axis=0, concat...]
    all_to_all x1 -> x2, starting transfers between devices: 8.28 us -> 10.7 us  [the longest x1 7.28 us: shards(): lax.all_to_all(last_send, 'z', split_axis=0, concat_axis=0, tiled=True)]
    all_to_all x1 -> x2, waiting for transfers between devices: 11.3 us -> 13.1 us  [the longest x1 8.01 us: shards(): lax.all_to_all(last_send, 'z', split_axis=0, concat_axis=0, tiled=True)]
    all_gather x2 -> x1, blocking collectives: 23.8 us -> 22.9 us  [shards(): lax.all_gather(jnp.concatenate([grad_low, loss_block], axis=1), RING, axi...]
  transfers between devices with their start and end apart: 6 -> 8, of which waited for: 4 -> 6; matrix products, arithmetic and copies ran while one was open for 6% -> 5% of each run, Pallas kernels for 0% -> 0%
where the time goes in v2:
time: 200 us; the launch traced here: 197 us
  blocking collectives  65 us (32%)
  waiting for transfers between devices  56.9 us (28%)
  starting transfers between devices  32.1 us (16%)
  between operations  18.1 us (9%)
  matrix products  10 us (5%)
  other arithmetic  9.85 us (5%)
  local copies, waits for them, and re-layouts  4.97 us (2%)
    all_gather x1, blocking collectives, shards(): lax.all_gather(jnp.concatenate([grad_low, loss_block], axis=1), RING, axi...  22.9 us
    all_gather x1, blocking collectives, shards(): lax.all_gather(jnp.concatenate([pooled, text_embed], axis=0), TENS, axis=...  22.2 us
    all_gather x1, blocking collectives, shards(): img_all = lax.all_gather(img_send, RING, axis=0, tiled=True)  19.9 us
    all_to_all x1, waiting for transfers between devices, shards(): lax.all_to_all(unit_part.astype(jnp.bfloat16), RING, split_axis=0, concat...  19.1 us
    all_to_all x1, waiting for transfers between devices, shards(): lax.all_to_all(norm_send, TENS, split_axis=0, concat_axis=0, tiled=True)  11.8 us
    all_to_all x1, waiting for transfers between devices, shards(): lax.all_to_all(part.astype(jnp.bfloat16), TENS, split_axis=0, concat_axis...  10.9 us
    all_to_all x1, starting transfers between devices, shards(): lax.all_to_all(unit_part.astype(jnp.bfloat16), RING, split_axis=0, concat...  9.5 us
    all_to_all x1, waiting for transfers between devices, shards(): lax.all_to_all(last_send, 'z', split_axis=0, concat_axis=0, tiled=True)  8.01 us
  transfers between devices with their start and end apart: 8, of which 6 were waited for; matrix products, arithmetic and copies ran while one was open for 5% of the time, Pallas kernels for 0%

profile of v2, /device:TPU:1, one launch (start us, length us, event | category | flops | bytes accessed | tf_op | source)
XLA Modules:
  0.0 197.0 jit_solution(1722711869759492591)
XLA Ops:
  7.2 0.9 pad_maximum_fusion.3
  8.1 22.2 %all_gather.12 = bf16[256,1536]{0,1:T(8,128)(2,1)S(1)} all-gather(bf16[256,192]{0,1:T(8,128)(2,1)S(1)} %pad_maximum_fusion.3), channel_id=1, replica_groups=mesh['x'=4,'z'=8,'ylo'=2,'yhi'=4,'core'=2] {'yhi','core'}, dimensions={1}, use_global_device_ids=true | all-gather | bytes 884736 | tf_op jit(solution)/shard_map/all_gather | solution.py:83
  30.3 0.7 convert_bitcast_fusion.2
  31.0 0.7 convert_bitcast_fusion.1
  31.8 0.3 constant_dynamic-slice_fusion.3
  32.0 0.1 copy.76
  32.2 0.1 fusion.53
  32.3 0.1 fusion.54
  32.5 0.1 copy.79
  32.6 0.7 broadcast_in_dim.14
  33.3 3.4 %all-to-all-start.1 = ((bf16[4,16,1664]{2,1,0:T(8,128)(2,1)}), bf16[4,16,1664]{2,1,0:T(8,128)(2,1)S(1)}, u32[]{:S(2)}, u32[]{:S(2)}) async-start(bf16[4,16,1664]{2,1,0:T(8,128)(2,1)} %broadcast_in_dim.14), calls=%async_computation.1 | async-start | bytes 425984 | tf_op jit(solution)/shard_map/all_to_all | solution.py:58
  36.7 0.0 all-gather.2.cloned.1.call-start
  36.8 0.2 copy.75
  36.9 0.1 convert_reduce_fusion.1
  37.1 0.3 fusion.20
  37.4 5.1 %all-to-all-done.1 = bf16[4,16,1664]{2,1,0:T(8,128)(2,1)S(1)} async-done(((bf16[4,16,1664]{2,1,0:T(8,128)(2,1)}), bf16[4,16,1664]{2,1,0:T(8,128)(2,1)S(1)}, u32[]{:S(2)}, u32[]{:S(2)}) %all-to-all-start.1) | async-done | bytes 213024 | tf_op jit(solution)/shard_map/all_to_all | solution.py:58
  42.4 0.7 copy-done.1
  43.2 1.8 multiply_convert_fusion.2
  45.0 0.3 dynamic_update_slice.5
  45.3 1.1 fusion
  46.4 4.9 %all-to-all-start = ((bf16[8,16,1536]{2,1,0:T(8,128)(2,1)}), bf16[8,16,1536]{2,1,0:T(8,128)(2,1)S(1)}, u32[]{:S(2)}, u32[]{:S(2)}) async-start(bf16[8,16,1536]{2,1,0:T(8,128)(2,1)} %bitcast), calls=%async_computation | async-start | bytes 786432 | tf_op jit(solution)/shard_map/all_to_all | solution.py:106
  51.3 0.1 copy.74
  51.5 0.1 copy.78
  53.5 10.9 %all-to-all-done = bf16[8,16,1536]{2,1,0:T(8,128)(2,1)S(1)} async-done(((bf16[8,16,1536]{2,1,0:T(8,128)(2,1)}), bf16[8,16,1536]{2,1,0:T(8,128)(2,1)S(1)}, u32[]{:S(2)}, u32[]{:S(2)}) %all-to-all-start) | async-done | bytes 393248 | tf_op jit(solution)/shard_map/all_to_all | solution.py:106
  64.4 0.1 convert_reduce_fusion.3
  64.5 0.1 multiply_reduce_fusion.2
  64.6 0.1 fusion.106
  64.7 19.9 %all_gather.13 = bf16[256,1664]{1,0:T(8,128)(2,1)S(1)} all-gather(bf16[16,1664]{1,0:T(8,128)(2,1)S(1)} %fusion.70), channel_id=1, replica_groups=mesh['x'=4,'z'=8,'ylo'=2,'yhi'=4,'core'=2] {'ylo','yhi','core'}, dimensions={0}, use_global_device_ids=true | all-gather | bytes 905216 | tf_op jit(solution)/shard_map/all_gather | solution.py:116
  84.6 0.2 fusion.49
  84.8 0.9 slice_convert_fusion
  85.8 0.2 fusion.32
  86.0 2.5 %fusion.26 = (f32[512]{0:T(512)S(1)}, f32[256,512]{1,0:T(8,128)S(1)}) fusion(f32[]{:T(128)} %bitcast.57, bf16[512,1664]{1,0:T(8,128)(2,1)} %all-gather.2.cloned.1.call-done, bf16[256,1664]{1,0:T(8,128)(2,1)S(1)} %all_gather.13, f32[]{:T(128)} %bitcast.56, f32[512]{0:T(512)S(1)} %fusion.32, f32[256]{0:T(256)S(1)} %fusion.49), kind=kOutput, calls=%fused_computation.32 | convolution fusion | flops 404356608 | bytes 2889728 | tf_op jit(solution)/shard_map/dot_general | solution.py:122
  88.5 1.6 convolution_convert_fusion
  90.1 9.5 %all-to-all-start.2 = ((bf16[16,16,1536]{2,1,0:T(8,128)(2,1)}), bf16[16,16,1536]{2,1,0:T(8,128)(2,1)S(1)}, u32[]{:S(2)}, u32[]{:S(2)}) async-start(bf16[16,16,1536]{2,1,0:T(8,128)(2,1)} %bitcast.9), calls=%async_computation.2 | async-start | bytes 1572864 | tf_op jit(solution)/shard_map/all_to_all | solution.py:131
  99.6 3.3 %collective-permute-start = (bf16[128,384]{1,0:T(8,128)(2,1)S(1)}, bf16[128,384]{1,0:T(8,128)(2,1)S(1)}, u32[]{:S(2)}, u32[]{:S(2)}) collective-permute-start(bf16[128,384]{1,0:T(8,128)(2,1)S(1)} %get-tuple-element.30), channel_id=1, source_target_pairs={{0,8},{8,0},{1,9},{9,1},{2,10},{10,2},{3,11},{11,3},{4,12},{12,4},... | collective-permute-start | bytes 294920 | tf_op jit(solution)/shard_map/ppermute | solution.py:101
  103.0 0.1 reshape.262
  103.1 0.1 subtract_convert_fusion
  103.2 19.1 %all-to-all-done.2 = bf16[16,16,1536]{2,1,0:T(8,128)(2,1)S(1)} async-done(((bf16[16,16,1536]{2,1,0:T(8,128)(2,1)}), bf16[16,16,1536]{2,1,0:T(8,128)(2,1)S(1)}, u32[]{:S(2)}, u32[]{:S(2)}) %all-to-all-start.2) | async-done | bytes 786464 | tf_op jit(solution)/shard_map/all_to_all | solution.py:131
  122.3 0.1 convert_reduce_fusion
  122.4 0.2 multiply_reduce_fusion.1
  122.6 0.1 divide_convert_fusion
  122.7 22.9 %all_gather.15 = bf16[256,1664]{1,0:T(8,128)(2,1)S(1)} all-gather(bf16[16,1664]{1,0:T(8,128)(2,1)S(1)} %fusion.72), channel_id=1, replica_groups=mesh['x'=4,'z'=8,'ylo'=2,'yhi'=4,'core'=2] {'ylo','yhi','core'}, dimensions={0}, use_global_device_ids=true | all-gather | bytes 905216 | tf_op jit(solution)/shard_map/all_gather | solution.py:138
  145.6 0.1 constant_dynamic-slice_fusion.1
  145.7 0.6 fusion.22
  146.3 0.1 dynamic-slice_convert_fusion
  146.4 0.9 pad_maximum_fusion
  147.3 2.5 %multiply_reduce_fusion = (f32[128]{0:T(128)S(1)}, f32[128]{0:T(128)S(1)}, bf16[1536,128]{0,1:T(8,128)(2,1)S(1)}) fusion(f32[1536]{0:T(1024)S(1)} %copy-done.5, f32[128]{0:T(128)S(1)} %add_rsqrt_fusion, f32[128]{0:T(128)S(1)} %broadcast_multiply_fusion, bf16[128,1536]{1,0:T(8,128)(2,1)S(1)} %copy.75, bf16[1536,384]{1,0:T(8,128)(2,1)} %param.16, ...), kind=kOutput, calls=%fused_computation.30 | convolution fusion | flops 304545536 | bytes 3743744 | tf_op jit(solution)/shard_map/dot_general | solution.py:169
  149.8 0.2 copy.73
  150.1 0.8 pad_maximum_fusion.1
  150.9 3.7 %all-to-all-start.4 = ((bf16[8,208,128]{2,1,0:T(8,128)(2,1)}), bf16[8,208,128]{2,1,0:T(8,128)(2,1)S(1)}, u32[]{:S(2)}, u32[]{:S(2)}) async-start(bf16[8,208,128]{2,1,0:T(8,128)(2,1)} %pad_maximum_fusion.1), calls=%async_computation.5 | async-start | bytes 851968 | tf_op jit(solution)/shard_map/all_to_all | solution.py:185
  154.5 0.1 dynamic_slice.36
  154.6 0.1 dynamic_slice.35
  154.7 0.1 copy.77
  154.9 11.8 %all-to-all-done.4 = bf16[8,208,128]{2,1,0:T(8,128)(2,1)S(1)} async-done(((bf16[8,208,128]{2,1,0:T(8,128)(2,1)}), bf16[8,208,128]{2,1,0:T(8,128)(2,1)S(1)}, u32[]{:S(2)}, u32[]{:S(2)}) %all-to-all-start.4) | async-done | bytes 426016 | tf_op jit(solution)/shard_map/all_to_all | solution.py:185
  166.6 0.1 convert_reduce_fusion.2
  166.7 2.0 reduce-scatter.2.cloned.1.call-done
  168.7 0.8 multiply_reduce_fusion.3
  169.4 0.9 slice.86
  170.4 0.7 pad_maximum_fusion.2
  171.1 7.3 %all-to-all-start.3 = ((bf16[8,32,384]{2,1,0:T(8,128)(2,1)}), bf16[8,32,384]{2,1,0:T(8,128)(2,1)S(1)}, u32[]{:S(2)}, u32[]{:S(2)}) async-start(bf16[8,32,384]{2,1,0:T(8,128)(2,1)} %pad_maximum_fusion.2), calls=%async_computation.4 | async-start | bytes 393216 | tf_op jit(solution)/shard_map/all_to_all | solution.py:202
  178.4 0.7 fusion.62
  179.1 8.0 %all-to-all-done.3 = bf16[8,32,384]{2,1,0:T(8,128)(2,1)S(1)} async-done(((bf16[8,32,384]{2,1,0:T(8,128)(2,1)}), bf16[8,32,384]{2,1,0:T(8,128)(2,1)S(1)}, u32[]{:S(2)}, u32[]{:S(2)}) %all-to-all-start.3) | async-done | bytes 196640 | tf_op jit(solution)/shard_map/all_to_all | solution.py:202
  187.1 0.6 slice_bitcast_fusion
  187.8 0.6 slice_reduce_fusion.1
  (48 shorter events, 0.5 us)
Async XLA Ops:
  7.2 38.1 %copy-start = (bf16[384,1536]{1,0:T(8,128)(2,1)S(1)}, bf16[384,1536]{1,0:T(8,128)(2,1)}, u32[]{:S(2)}) copy-start(bf16[384,1536]{1,0:T(8,128)(2,1)} %param.18) | copy-start | bytes 3538948
  33.3 9.2 %all-to-all-start.1 = ((bf16[4,16,1664]{2,1,0:T(8,128)(2,1)}), bf16[4,16,1664]{2,1,0:T(8,128)(2,1)S(1)}, u32[]{:S(2)}, u32[]{:S(2)}) async-start(bf16[4,16,1664]{2,1,0:T(8,128)(2,1)} %broadcast_in_dim.14), calls=%async_computation.1 | async-start | bytes 425984 | tf_op jit(solution)/shard_map/all_to_all | solution.py:58
  36.6 6.5 %copy-start.5 = (f32[1536]{0:T(1024)S(1)}, f32[1536]{0:T(1024)}, u32[]{:S(2)}) copy-start(f32[1536]{0:T(1024)} %param.14) | copy-start | bytes 18436
  36.6 6.5 %copy-start.6 = (f32[1536]{0:T(1024)S(1)}, f32[1536]{0:T(1024)}, u32[]{:S(2)}) copy-start(f32[1536]{0:T(1024)} %param.15) | copy-start | bytes 18436
  36.7 6.5 %copy-start.7 = (f32[384]{0:T(512)S(1)}, f32[384]{0:T(512)}, u32[]{:S(2)}) copy-start(f32[384]{0:T(512)} %param.17) | copy-start | bytes 4612
  36.7 48.2 %all-gather.2.cloned.1.call-start = ((), (), s32[]{:S(2)}) async-start(), calls=%async_computation.6 | async-start | bytes 1916928 | tf_op jit(solution)/shard_map/all_gather | solution.py:91
  42.4 0.7 copy-start.1
  43.2 1.8 copy-start.4
  46.4 18.0 %all-to-all-start = ((bf16[8,16,1536]{2,1,0:T(8,128)(2,1)}), bf16[8,16,1536]{2,1,0:T(8,128)(2,1)S(1)}, u32[]{:S(2)}, u32[]{:S(2)}) async-start(bf16[8,16,1536]{2,1,0:T(8,128)(2,1)} %bitcast), calls=%async_computation | async-start | bytes 786432 | tf_op jit(solution)/shard_map/all_to_all | solution.py:106
  86.0 2.5 %copy-start.3 = (bf16[512,1664]{1,0:T(8,128)(2,1)S(1)}, bf16[512,1664]{1,0:T(8,128)(2,1)}, u32[]{:S(2)}) copy-start(bf16[512,1664]{1,0:T(8,128)(2,1)} %all-gather.2.cloned.1.call-done) | copy-start | bytes 5111812
  90.1 32.2 %all-to-all-start.2 = ((bf16[16,16,1536]{2,1,0:T(8,128)(2,1)}), bf16[16,16,1536]{2,1,0:T(8,128)(2,1)S(1)}, u32[]{:S(2)}, u32[]{:S(2)}) async-start(bf16[16,16,1536]{2,1,0:T(8,128)(2,1)} %bitcast.9), calls=%async_computation.2 | async-start | bytes 1572864 | tf_op jit(solution)/shard_map/all_to_all | solution.py:131
  99.6 69.1 %reduce-scatter.2.cloned.1.call-start = ((), (), s32[]{:S(2)}) async-start(), calls=%async_computation.7 | async-start | bytes 798720 | tf_op jit(solution)/shard_map/reduce_scatter | solution.py:163
  99.6 46.1 %collective-permute-start = (bf16[128,384]{1,0:T(8,128)(2,1)S(1)}, bf16[128,384]{1,0:T(8,128)(2,1)S(1)}, u32[]{:S(2)}, u32[]{:S(2)}) collective-permute-start(bf16[128,384]{1,0:T(8,128)(2,1)S(1)} %get-tuple-element.30), channel_id=1, source_target_pairs={{0,8},{8,0},{1,9},{9,1},{2,10},{10,2},{3,11},{11,3},{4,12},{12,4},... | collective-permute-start | bytes 294920 | tf_op jit(solution)/shard_map/ppermute | solution.py:101
  150.9 27.5 %copy-start.2 = (bf16[128,192]{0,1:T(8,128)(2,1)S(1)}, bf16[128,192]{0,1:T(8,128)(2,1)}, u32[]{:S(2)}) copy-start(bf16[128,192]{0,1:T(8,128)(2,1)} %param.13) | copy-start | bytes 147460
  150.9 15.7 %all-to-all-start.4 = ((bf16[8,208,128]{2,1,0:T(8,128)(2,1)}), bf16[8,208,128]{2,1,0:T(8,128)(2,1)S(1)}, u32[]{:S(2)}, u32[]{:S(2)}) async-start(bf16[8,208,128]{2,1,0:T(8,128)(2,1)} %pad_maximum_fusion.1), calls=%async_computation.5 | async-start | bytes 851968 | tf_op jit(solution)/shard_map/all_to_all | solution.py:185
  171.1 16.0 %all-to-all-start.3 = ((bf16[8,32,384]{2,1,0:T(8,128)(2,1)}), bf16[8,32,384]{2,1,0:T(8,128)(2,1)S(1)}, u32[]{:S(2)}, u32[]{:S(2)}) async-start(bf16[8,32,384]{2,1,0:T(8,128)(2,1)} %pad_maximum_fusion.2), calls=%async_computation.4 | async-start | bytes 393216 | tf_op jit(solution)/shard_map/all_to_all | solution.py:202
Sparse Core Ops, SparseCore 0:
  43.3 39.5 all-gather.1
  147.5 21.1 reduce-scatter.1

commit v3 on v2

v3 whole, which is shorter than its diff:
```python
import jax
import jax.numpy as jnp
from jax import lax
from jax.experimental import pallas as pl
from jax.experimental.pallas import tpu as pltpu
from jax.sharding import Mesh, PartitionSpec as P

ROWS = 128
WIDE = 1536
SLICE = 192
EXTRA = 128
IMG = 16
DATA = ("x", "z", "ylo")
TENS = ("yhi", "core")
RING = ("ylo", "yhi", "core")


def gelu_fn(values):
    return jax.nn.gelu(values, approximate=True)


def id_columns(ids, start):
    lanes = lax.broadcasted_iota(jnp.int32, (IMG, ROWS), 1)
    rows = lax.broadcasted_iota(jnp.int32, (IMG, ROWS), 0)
    own = jnp.sum(
        jnp.where(lanes == rows + start, ids[None, :], 0).astype(jnp.float32), axis=1, keepdims=True
    )
    high = jnp.floor(own / 128.0)
    low = own - 128.0 * high
    place = lax.broadcasted_iota(jnp.int32, (IMG, EXTRA), 1)
    return jnp.where(place == 0, high, jnp.where(place == 1, low, 0.0)).astype(jnp.bfloat16)


def pieces(values, count):
    parts = []
    for _ in range(count):
        part = lax.reduce_precision(values, 8, 7)
        parts.append(part.astype(jnp.bfloat16))
        values = values - part
    return jnp.stack(parts)


def spread(block, axis, count):
    send = jnp.broadcast_to(block[None], (count,) + block.shape)
    return lax.all_to_all(send, axis, split_axis=0, concat_axis=0, tiled=True).reshape(
        count * block.shape[0], block.shape[1]
    )


VMEM = pl.BlockSpec(memory_space=pltpu.VMEM)
SMEM = pl.BlockSpec(memory_space=pltpu.SMEM)


def call(kernel, outs, n_smem, flops, moved, *args):
    return pl.pallas_call(
        kernel,
        out_shape=[jax.ShapeDtypeStruct(shape, kind) for shape, kind in outs],
        in_specs=[SMEM] * n_smem + [VMEM] * (len(args) - n_smem),
        out_specs=[VMEM] * len(outs),
        compiler_params=pltpu.CompilerParams(vmem_limit_bytes=32 * 2**20),
        cost_estimate=pl.CostEstimate(flops=flops, bytes_accessed=moved, transcendentals=0),
    )(*args)


def split_two(values):
    first = values.astype(jnp.bfloat16).astype(jnp.float32)
    return first, values - first


def pair_kernel(which_ref, scalar_ref, img_ref, txt_ref, out_ref, loss_ref):
    img = img_ref[:, which_ref[0]].reshape(ROWS, WIDE + EXTRA)
    txt = txt_ref[:, :WIDE]
    across = (((1,), (1,)), ((), ()))
    scores = lax.dot_general(img[:, :WIDE], txt, across, preferred_element_type=jnp.float32)
    place = lax.broadcasted_iota(jnp.int32, (8, EXTRA), 1)
    pick = jnp.where(place == 0, 128.0, jnp.where(place == 1, 1.0, 0.0))
    txt_ids = lax.dot_general(
        pick.astype(jnp.bfloat16), txt_ref[:, WIDE:], across, preferred_element_type=jnp.float32
    )[:1]
    img_ids = jnp.sum(img[:, WIDE:].astype(jnp.float32) * pick[:1], axis=1, keepdims=True)
    logits = scalar_ref[0] * scores + scalar_ref[1]
    positive = img_ids == txt_ids
    margin = jnp.where(positive, -logits, logits)
    shrunk = jnp.exp(-jnp.abs(margin))
    losses = jnp.maximum(margin, 0.0) + jnp.log1p(shrunk)
    sigmoid = jnp.where(margin >= 0.0, 1.0, shrunk) / (1.0 + shrunk)
    scale = scalar_ref[2]
    weights = (jnp.where(positive, -scale, scale) * sigmoid).astype(jnp.bfloat16)
    out_ref[...] = jnp.dot(weights, txt, preferred_element_type=jnp.float32).astype(out_ref.dtype)
    folded = losses[:, :128] + losses[:, 128:256] + losses[:, 256:384] + losses[:, 384:]
    loss_ref[...] = jnp.sum(folded.reshape(16, 8, 128), axis=0)


def pair_rows(which, scalars, img_all, txt_all, kind):
    return call(
        pair_kernel,
        [((ROWS, WIDE), kind), ((8, 128), jnp.float32)],
        2,
        4 * ROWS * 512 * WIDE,
        3000000,
        which.reshape(1).astype(jnp.int32),
        scalars,
        img_all.reshape(8, 2, IMG, WIDE + EXTRA),
        txt_all,
    )


def gelu_slope(values):
    root = 0.7978845608028654
    inner = jnp.tanh(root * (values + 0.044715 * (values * values * values)))
    return 0.5 * (1.0 + inner) + 0.5 * values * (1.0 - inner * inner) * root * (
        1.0 + 3.0 * 0.044715 * (values * values)
    )


def back_kernel(
    where_ref, grad_ref, down_ref, pre_ref, up_ref, gain_ref, gs_ref, send_ref, own_ref, sum_ref, hold_ref
):
    across = (((1,), (1,)), ((), ()))
    core = where_ref[1]
    grad = grad_ref[where_ref[0]][:, :WIDE]
    grad_hidden = lax.dot_general(grad, down_ref[...], across, preferred_element_type=jnp.float32)
    grad_pre = (grad_hidden * gelu_slope(pre_ref[...])).astype(jnp.bfloat16)
    part = lax.dot_general(up_ref[...], grad_pre, across, preferred_element_type=jnp.float32)
    hold_ref[...] = part.reshape(4, 2, SLICE, ROWS)
    sum_h = jnp.sum(part * gain_ref[...], axis=0, keepdims=True)
    sum_hs = jnp.sum(part * gs_ref[...], axis=0, keepdims=True)
    send_ref[: 4 * SLICE] = hold_ref[:, 1 - core].reshape(4 * SLICE, ROWS).astype(jnp.bfloat16)
    own_ref[...] = hold_ref[:, core]
    write_sums(send_ref, 4 * SLICE, sum_h, sum_hs)
    sum_ref[...] = jnp.concatenate([sum_h, sum_hs, jnp.zeros((6, ROWS), jnp.float32)], axis=0)


def write_sums(ref, start, sum_h, sum_hs):
    h_hi, h_lo = split_two(sum_h)
    s_hi, s_lo = split_two(sum_hs)
    ref[start:] = jnp.concatenate(
        [h_hi, s_hi, h_lo, s_lo, jnp.zeros((12, ROWS), jnp.float32)], axis=0
    ).astype(jnp.bfloat16)


def read_sums(ref, start):
    block = ref[start:].astype(jnp.float32)
    return block[0:1] + block[2:3], block[1:2] + block[3:4]


def back_rows(where, grad_all, w_down, preact, w_up, gain_t, gs_t):
    return pl.pallas_call(
        back_kernel,
        out_shape=[
            jax.ShapeDtypeStruct((4 * SLICE + 16, ROWS), jnp.bfloat16),
            jax.ShapeDtypeStruct((4, SLICE, ROWS), jnp.float32),
            jax.ShapeDtypeStruct((8, ROWS), jnp.float32),
        ],
        in_specs=[SMEM] + [VMEM] * 6,
        out_specs=[VMEM] * 3,
        scratch_shapes=[pltpu.VMEM((4, 2, SLICE, ROWS), jnp.float32)],
        compiler_params=pltpu.CompilerParams(vmem_limit_bytes=32 * 2**20),
        cost_estimate=pl.CostEstimate(
            flops=4 * ROWS * 384 * WIDE, bytes_accessed=4000000, transcendentals=0
        ),
    )(where, grad_all.reshape(2, ROWS, WIDE + EXTRA), w_down, preact, w_up, gain_t, gs_t)


def chip_kernel(where_ref, own_ref, sums_ref, got_ref, one_ref, two_ref, three_ref, keep_ref, all_ref, hold_ref):
    yhi = where_ref[2]
    hold_ref[...] = own_ref[...] + got_ref[: 4 * SLICE].astype(jnp.float32).reshape(4, SLICE, ROWS)
    got_h, got_hs = read_sums(got_ref, 4 * SLICE)
    sum_h = sums_ref[0:1] + got_h
    sum_hs = sums_ref[1:2] + got_hs
    for step, ref in enumerate((one_ref, two_ref, three_ref), 1):
        ref[:SLICE] = hold_ref[lax.rem(yhi + step, 4)].astype(jnp.bfloat16)
        write_sums(ref, SLICE, sum_h, sum_hs)
    keep_ref[...] = hold_ref[yhi]
    all_ref[...] = jnp.concatenate([sum_h, sum_hs, jnp.zeros((6, ROWS), jnp.float32)], axis=0)


def chip_rows(where, own_blocks, own_sums, got):
    return pl.pallas_call(
        chip_kernel,
        out_shape=[jax.ShapeDtypeStruct((SLICE + 16, ROWS), jnp.bfloat16)] * 3
        + [
            jax.ShapeDtypeStruct((SLICE, ROWS), jnp.float32),
            jax.ShapeDtypeStruct((8, ROWS), jnp.float32),
        ],
        in_specs=[SMEM] + [VMEM] * 3,
        out_specs=[VMEM] * 5,
        scratch_shapes=[pltpu.VMEM((4, SLICE, ROWS), jnp.float32)],
        compiler_params=pltpu.CompilerParams(vmem_limit_bytes=16 * 2**20),
        cost_estimate=pl.CostEstimate(flops=1000000, bytes_accessed=1000000, transcendentals=0),
    )(where, own_blocks, own_sums, got)


def last_kernel(
    keep_ref, all_ref, one_ref, two_ref, three_ref, inv_ref, invgain_ref, invscaled_ref, grad_ref, out_ref
):
    total = keep_ref[...]
    sum_h = all_ref[0:1]
    sum_hs = all_ref[1:2]
    for ref in (one_ref, two_ref, three_ref):
        total = total + ref[:SLICE].astype(jnp.float32)
        got_h, got_hs = read_sums(ref, SLICE)
        sum_h = sum_h + got_h
        sum_hs = sum_hs + got_hs
    side = (
        invgain_ref[...] * total
        - inv_ref[:1] * (sum_h / WIDE)
        - invscaled_ref[...] * (sum_hs / WIDE)
    )
    out_ref[...] = (grad_ref[...].astype(jnp.float32) + side.T).astype(jnp.bfloat16)


def last_rows(keep, sums, gots, inverse_t, invgain, invscaled, grad_own):
    return call(
        last_kernel,
        [((ROWS, SLICE), jnp.bfloat16)],
        0,
        1000000,
        800000,
        keep,
        sums,
        *gots,
        inverse_t,
        invgain,
        invscaled,
        grad_own,
    )[0]


def down_kernel(ylo_ref, grad_ref, hidden_ref, out_ref):
    even = ylo_ref[0] == 0
    rows = grad_ref[:, :WIDE]
    for piece in range(3):
        part = lax.dot_general(
            rows,
            hidden_ref[:, piece * 128 : (piece + 1) * 128],
            (((0,), (0,)), ((), ())),
            preferred_element_type=jnp.float32,
        ).reshape(32, 2, 24, 128)
        out_ref[:, piece * 24 : (piece + 1) * 24, :] = jnp.where(
            even, part[:, 0], part[:, 1]
        ).astype(jnp.bfloat16)
    tail = grad_ref[:, WIDE:].astype(jnp.float32)
    total = jnp.sum(tail, axis=0, keepdims=True)
    first = total.astype(jnp.bfloat16).astype(jnp.float32)
    second = (total - first).astype(jnp.bfloat16).astype(jnp.float32)
    third = total - first - second
    place = lax.broadcasted_iota(jnp.int32, (8, 128), 0)
    block = jnp.where(
        place == 0, first, jnp.where(place == 1, second, jnp.where(place == 2, third, 0.0))
    )
    out_ref[:, 72:, :] = jnp.broadcast_to(block[None], (32, 8, 128)).astype(jnp.bfloat16)


def down_block(ylo, grad_all, hidden_pair):
    return pl.pallas_call(
        down_kernel,
        out_shape=jax.ShapeDtypeStruct((32, 80, 128), jnp.bfloat16),
        in_specs=[
            pl.BlockSpec(memory_space=pltpu.SMEM),
            pl.BlockSpec(memory_space=pltpu.VMEM),
            pl.BlockSpec(memory_space=pltpu.VMEM),
        ],
        out_specs=pl.BlockSpec(memory_space=pltpu.VMEM),
        compiler_params=pltpu.CompilerParams(vmem_limit_bytes=24 * 2**20),
        cost_estimate=pl.CostEstimate(
            flops=2 * 256 * WIDE * 384, bytes_accessed=1700000, transcendentals=0
        ),
    )(ylo.reshape(1).astype(jnp.int32), grad_all, hidden_pair)


def turn(step):
    return [(at, (at + step) % 4) for at in range(4)]


def shards(
    pooled,
    ln_gain,
    ln_bias,
    w_up,
    b_up,
    w_down,
    b_down,
    text_embed,
    image_ids,
    text_ids,
    logit_scale,
    logit_bias,
    loss_scale,
):
    tens = lax.axis_index(TENS)
    row0 = tens * IMG
    col0 = tens * SLICE
    batch = ROWS * 64

    both = lax.all_gather(
        jnp.concatenate([pooled, text_embed], axis=0), TENS, axis=1, tiled=True
    )
    txt_rows = lax.dynamic_slice_in_dim(both, ROWS + row0, IMG, 0).astype(jnp.float32)
    txt_norm = jnp.sqrt(jnp.sum(txt_rows * txt_rows, axis=1, keepdims=True) + 1e-06)
    txt_low = (txt_rows / txt_norm).astype(jnp.bfloat16)
    txt_z = spread(jnp.concatenate([txt_low, id_columns(text_ids, row0)], axis=1), "z", 8)

    wide = both[:ROWS].astype(jnp.float32)
    average = jnp.mean(wide, axis=1, keepdims=True)
    centered = wide - average
    inverse = lax.rsqrt(jnp.mean(centered * centered, axis=1, keepdims=True) + 1e-06)
    scaled = centered * inverse
    normed = (scaled * ln_gain + ln_bias).astype(jnp.bfloat16)
    preact = jnp.dot(normed, w_up, preferred_element_type=jnp.float32) + b_up
    hidden = gelu_fn(preact).astype(jnp.bfloat16)
    hidden_other = lax.ppermute(hidden, "ylo", [(0, 1), (1, 0)])
    ylo = lax.axis_index("ylo")
    hidden_pair = jnp.concatenate(
        [jnp.where(ylo == 0, hidden, hidden_other), jnp.where(ylo == 0, hidden_other, hidden)],
        axis=0,
    )
    bias_row = lax.dynamic_update_slice_in_dim(
        jnp.zeros((WIDE,), jnp.float32), b_down, col0, 0
    )
    part = jnp.dot(hidden, w_down, preferred_element_type=jnp.float32) + bias_row
    core = lax.axis_index("core")
    yhi = lax.axis_index("yhi")
    part = part.reshape(4, 2, IMG, WIDE)
    core_got = lax.ppermute(
        lax.dynamic_index_in_dim(part, 1 - core, 1, keepdims=False).astype(jnp.bfloat16),
        "core",
        [(0, 1), (1, 0)],
    )
    chip = lax.dynamic_index_in_dim(part, core, 1, keepdims=False) + core_got.astype(jnp.float32)
    mixed = lax.dynamic_index_in_dim(chip, yhi, 0, keepdims=False)
    for step in range(1, 4):
        block = lax.dynamic_index_in_dim(chip, (yhi + step) % 4, 0, keepdims=False)
        got = lax.ppermute(block.astype(jnp.bfloat16), "yhi", turn(step))
        mixed = mixed + got.astype(jnp.float32)
    own = lax.dynamic_slice_in_dim(both, row0, IMG, 0).astype(jnp.float32)
    summed = own + mixed
    img_norm = jnp.sqrt(jnp.sum(summed * summed, axis=1, keepdims=True) + 1e-06)
    img_unit = summed / img_norm
    txt_all = spread(txt_z, "x", 4)
    img_send = jnp.concatenate(
        [img_unit.astype(jnp.bfloat16), id_columns(image_ids, row0)], axis=1
    )
    img_all = lax.all_gather(img_send, RING, axis=0, tiled=True)

    temper = logit_scale[0]
    offset = logit_bias[0]
    factor = loss_scale[0] / batch
    scalars = jnp.stack([temper, offset, temper * factor])
    other_part, other_loss = pair_rows(1 - core, scalars, img_all, txt_all, jnp.bfloat16)
    from_other = lax.ppermute(other_part, "core", [(0, 1), (1, 0)])
    own_part, own_loss = pair_rows(core, scalars, img_all, txt_all, jnp.float32)
    loss_part = jnp.sum(other_loss + own_loss, axis=0)
    chip_part = (own_part + from_other.astype(jnp.float32)).astype(jnp.bfloat16)
    unit_parts = lax.all_to_all(
        chip_part, ("ylo", "yhi"), split_axis=0, concat_axis=0, tiled=True
    )
    grad_unit = jnp.sum(unit_parts.reshape(8, IMG, WIDE).astype(jnp.float32), axis=0)
    tangent = jnp.sum(img_unit * grad_unit, axis=1, keepdims=True)
    grad_low = ((grad_unit - img_unit * tangent) / img_norm).astype(jnp.bfloat16)
    loss_block = jnp.pad(pieces(loss_part, 3), ((0, IMG - 3), (0, 0)))
    grad_all = lax.all_gather(
        jnp.concatenate([grad_low, loss_block], axis=1), RING, axis=0, tiled=True
    )
    down_send = down_block(ylo, grad_all, hidden_pair)
    down_got = lax.all_to_all(down_send, ("x", "z"), split_axis=0, concat_axis=0, tiled=True)

    where = jnp.stack([ylo, core, yhi]).astype(jnp.int32)
    gain_t = jnp.broadcast_to(ln_gain[:, None], (WIDE, ROWS))
    send, own_blocks, own_sums = back_rows(
        where, grad_all, w_down, preact, w_up, gain_t, gain_t * scaled.T
    )
    got = lax.ppermute(send, "core", [(0, 1), (1, 0)])
    sends = chip_rows(where, own_blocks, own_sums, got)
    gots = [lax.ppermute(sends[step - 1], "yhi", turn(step)) for step in range(1, 4)]
    gain_own = lax.dynamic_slice_in_dim(ln_gain, col0, SLICE, 0)
    scaled_own = ((pooled.astype(jnp.float32) - average) * inverse).T
    inverse_t = jnp.broadcast_to(inverse.reshape(1, ROWS), (8, ROWS))
    grad_own = lax.dynamic_slice(grad_all, (ylo * ROWS, col0), (ROWS, SLICE))
    grad_pooled = last_rows(
        sends[3], sends[4], gots, inverse_t, inverse_t[:1] * gain_own[:, None],
        inverse_t[:1] * scaled_own, grad_own,
    )

    down_sum = jnp.sum(down_got.astype(jnp.float32), axis=0)
    grad_down = down_sum[:72].reshape(3, 24, 128).transpose(0, 2, 1).reshape(384, 24)
    loss = (jnp.sum(down_sum[72:75]) / batch).reshape(1)
    return (loss, grad_pooled, grad_down)


def solution(mesh):
    inner = Mesh(mesh.devices.reshape(4, 8, 2, 4, 2), DATA + TENS)
    placed = (
        P(DATA, TENS),
        P(),
        P(),
        P(None, TENS),
        P(TENS),
        P(TENS, None),
        P(TENS),
        P(DATA, TENS),
        P(DATA),
        P(DATA),
        P(),
        P(),
        P(),
    )
    return jax.shard_map(
        shards,
        mesh=inner,
        in_specs=placed,
        out_specs=(P(), P(DATA, TENS), P(TENS, DATA)),
        check_vma=False,
    )
```

time: 200 us -> 179 us (0.90); the launches traced: 197 us -> 178 us
  waiting for transfers between devices: 56.9 us -> 19 us
  starting transfers between devices: 32.1 us -> 62.5 us
  between operations: 18.1 us -> 4.86 us
  matrix products: 10 us -> 1.37 us
  Pallas kernels: 0 us -> 7.6 us
  blocking collectives: 65 us -> 70.3 us
  other arithmetic: 9.85 us -> 6.75 us
    all_to_all x4 -> x2, waiting for transfers between devices: 49.8 us -> 10.5 us  [the longest x1 10.5 us: shards(): lax.all_to_all(chip_part, ('ylo', 'yhi'), split_axis=0, concat_axis=0, ti...]
    ppermute x0 -> x9, starting transfers between devices: none -> 31.3 us  [the longest x3 12.6 us: shards(): got = lax.ppermute(block.astype(jnp.bfloat16), 'yhi', turn(step))]
    all_to_all x4 -> x2, starting transfers between devices: 25.3 us -> 13.2 us  [the longest x1 9.6 us: shards(): lax.all_to_all(down_send, ('x', 'z'), split_axis=0, concat_axis=0, tiled=...]
    all_to_all x1 -> x2, starting transfers between devices: 3.37 us -> 12.1 us  [spread(): lax.all_to_all(send, axis, split_axis=0, concat_axis=0, tiled=True)]
    ppermute x0 -> x9, waiting for transfers between devices: none -> 8.55 us  [the longest x3 5.64 us: shards(): lax.ppermute(sends[step - 1], 'yhi', turn(step))]
    pallas_call x0 -> x6, Pallas kernels: none -> 7.6 us  [the longest x3 3.59 us: call(): pl.pallas_call(kernel, out_shape=[jax.ShapeDtypeStruct(shape, kind) for s...]
    dot_general x4 -> x0, matrix products: 7.14 us -> none  [the longest x1 2.49 us: shards(): lax.dot_general(img_all[:, :WIDE], txt_full, (((1,), (1,)), ((), ())), pr...]
    all_to_all x1 -> x2, waiting for transfers between devices: 5.08 us -> 0.01 us  [spread(): lax.all_to_all(send, axis, split_axis=0, concat_axis=0, tiled=True)]
  transfers between devices with their start and end apart: 8 -> 14, of which waited for: 6 -> 5; matrix products, arithmetic and copies ran while one was open for 5% -> 3% of each run, Pallas kernels for 0% -> 2%
where the time goes in v3:
time: 179 us; the launch traced here: 178 us
  blocking collectives  70.3 us (39%)
  starting transfers between devices  62.5 us (35%)
  waiting for transfers between devices  19 us (11%)
  Pallas kernels  7.6 us (4%)
  other arithmetic  6.75 us (4%)
  local copies, waits for them, and re-layouts  5.71 us (3%)
  between operations  4.86 us (3%)
    all_gather x1, blocking collectives, shards(): lax.all_gather(jnp.concatenate([grad_low, loss_block], axis=1), RING, axi...  25.3 us
    all_gather x1, blocking collectives, shards(): img_all = lax.all_gather(img_send, RING, axis=0, tiled=True)  22.9 us
    all_gather x1, blocking collectives, shards(): lax.all_gather(jnp.concatenate([pooled, text_embed], axis=0), TENS, axis=...  22.2 us
    ppermute x3, starting transfers between devices, shards(): got = lax.ppermute(block.astype(jnp.bfloat16), 'yhi', turn(step))  12.6 us
    ppermute x3, starting transfers between devices, shards(): lax.ppermute(sends[step - 1], 'yhi', turn(step))  12.2 us
    all_to_all x2, starting transfers between devices, spread(): lax.all_to_all(send, axis, split_axis=0, concat_axis=0, tiled=True)  12.1 us
    all_to_all x1, waiting for transfers between devices, shards(): lax.all_to_all(chip_part, ('ylo', 'yhi'), split_axis=0, concat_axis=0, ti...  10.5 us
    all_to_all x1, starting transfers between devices, shards(): lax.all_to_all(down_send, ('x', 'z'), split_axis=0, concat_axis=0, tiled=...  9.6 us
  transfers between devices with their start and end apart: 14, of which 5 were waited for; matrix products, arithmetic and copies ran while one was open for 3% of the time, Pallas kernels for 2%

profile of v3, /device:TPU:1, one launch (start us, length us, event | category | flops | bytes accessed | tf_op | source)
XLA Modules:
  0.0 178.2 jit_solution(16846187590471030422)
XLA Ops:
  0.7 0.9 pad_maximum_fusion.1
  1.6 22.2 %all_gather.9 = bf16[256,1536]{0,1:T(8,128)(2,1)S(1)} all-gather(bf16[256,192]{0,1:T(8,128)(2,1)S(1)} %pad_maximum_fusion.1), channel_id=1, replica_groups=mesh['x'=4,'z'=8,'ylo'=2,'yhi'=4,'core'=2] {'yhi','core'}, dimensions={1}, use_global_device_ids=true | all-gather | bytes 884736 | tf_op jit(solution)/shard_map/all_gather | solution.py:296
  23.8 0.2 convert_reduce_fusion.1
  24.0 0.2 fusion.2
  24.3 0.3 dynamic_update_slice.5
  24.6 1.0 fusion.20
  25.6 0.3 copy-done
  25.8 0.4 convolution_add_fusion
  26.3 2.1 %collective-permute-start = (bf16[4,16,1536]{2,1,0:T(8,128)(2,1)S(1)}, bf16[4,16,1536]{2,1,0:T(8,128)(2,1)S(1)}, u32[]{:S(2)}, u32[]{:S(2)}) collective-permute-start(bf16[4,16,1536]{2,1,0:T(8,128)(2,1)S(1)} %fusion.21), channel_id=1, source_target_pairs={{0,1},{1,0},{2,3},{3,2},{4,5},{5,4},{6,7},{7,6},{8,9},{9,8},{10,11... | collective-permute-start | bytes 589832 | tf_op jit(solution)/shard_map/ppermute | solution.py:325
  28.4 0.3 constant_dynamic-slice_fusion
  28.7 0.1 copy.51
  28.8 0.1 fusion.22
  29.0 0.1 fusion.23
  29.1 0.0 copy-done.9
  29.1 0.2 convert_reduce_fusion.3
  29.3 0.1 select_convert_fusion
  29.4 0.8 broadcast_in_dim.93
  30.2 8.1 %all-to-all-start = ((bf16[8,16,1664]{2,1,0:T(8,128)(2,1)}), bf16[8,16,1664]{2,1,0:T(8,128)(2,1)S(1)}, u32[]{:S(2)}, u32[]{:S(2)}) async-start(bf16[8,16,1664]{2,1,0:T(8,128)(2,1)} %broadcast_in_dim.93), calls=%async_computation | async-start | bytes 851968 | tf_op jit(solution)/shard_map/all_to_all | solution.py:45
  40.3 1.9 %collective-permute-start.1 = (bf16[16,1536]{1,0:T(8,128)(2,1)S(1)}, bf16[16,1536]{1,0:T(8,128)(2,1)S(1)}, u32[]{:S(2)}, u32[]{:S(2)}) collective-permute-start(bf16[16,1536]{1,0:T(8,128)(2,1)S(1)} %get-tuple-element.51), channel_id=1, source_target_pairs={{0,2},{2,4},{4,6},{6,0},{1,3},{3,5},{5,7},{7,1},{8,10},{10,12},{12... | collective-permute-start | bytes 147464 | tf_op jit(solution)/shard_map/ppermute | solution.py:334
  42.3 5.2 %collective-permute-start.2 = (bf16[16,1536]{1,0:T(8,128)(2,1)S(1)}, bf16[16,1536]{1,0:T(8,128)(2,1)S(1)}, u32[]{:S(2)}, u32[]{:S(2)}) collective-permute-start(bf16[16,1536]{1,0:T(8,128)(2,1)S(1)} %get-tuple-element.53), channel_id=1, source_target_pairs={{0,4},{2,6},{4,0},{6,2},{1,5},{3,7},{5,1},{7,3},{8,12},{10,14},{12... | collective-permute-start | bytes 147464 | tf_op jit(solution)/shard_map/ppermute | solution.py:334
  47.5 5.5 %collective-permute-start.3 = (bf16[16,1536]{1,0:T(8,128)(2,1)S(1)}, bf16[16,1536]{1,0:T(8,128)(2,1)S(1)}, u32[]{:S(2)}, u32[]{:S(2)}) collective-permute-start(bf16[16,1536]{1,0:T(8,128)(2,1)S(1)} %get-tuple-element.52), channel_id=1, source_target_pairs={{0,6},{2,0},{4,2},{6,4},{1,7},{3,1},{5,3},{7,5},{8,14},{10,8},{12,... | collective-permute-start | bytes 147464 | tf_op jit(solution)/shard_map/ppermute | solution.py:334
  53.0 0.1 pad_maximum_fusion.5.scalar_ref
  53.0 0.1 copy.49
  53.2 0.0 collective-permute-done.2
  53.2 1.9 %collective-permute-done.3 = bf16[16,1536]{1,0:T(8,128)(2,1)S(1)} collective-permute-done((bf16[16,1536]{1,0:T(8,128)(2,1)S(1)}, bf16[16,1536]{1,0:T(8,128)(2,1)S(1)}, u32[]{:S(2)}, u32[]{:S(2)}) %collective-permute-start.3) | collective-permute-done | bytes 49184 | tf_op jit(solution)/shard_map/ppermute | solution.py:334
  55.1 0.1 multiply_reduce_fusion.1
  55.2 1.3 broadcast_in_dim.95
  56.6 4.0 %all-to-all-start.1 = ((bf16[4,128,1664]{2,1,0:T(8,128)(2,1)}), bf16[4,128,1664]{2,1,0:T(8,128)(2,1)S(1)}, u32[]{:S(2)}, u32[]{:S(2)}) async-start(bf16[4,128,1664]{2,1,0:T(8,128)(2,1)} %broadcast_in_dim.95), calls=%async_computation.1 | async-start | bytes 3407872 | tf_op jit(solution)/shard_map/all_to_all | solution.py:45
  60.6 0.1 fusion.37
  60.7 22.9 %all_gather.10 = bf16[256,1664]{1,0:T(8,128)(2,1)S(1)} all-gather(bf16[16,1664]{1,0:T(8,128)(2,1)S(1)} %pad_maximum_fusion.2), channel_id=1, replica_groups=mesh['x'=4,'z'=8,'ylo'=2,'yhi'=4,'core'=2] {'ylo','yhi','core'}, dimensions={0}, use_global_device_ids=true | all-gather | bytes 905216 | tf_op jit(solution)/shard_map/all_gather | solution.py:344
  83.6 1.7 shard_map.149
  85.3 2.1 %collective-permute-start.4 = (bf16[128,1536]{1,0:T(8,128)(2,1)S(1)}, bf16[128,1536]{1,0:T(8,128)(2,1)}, u32[]{:S(2)}, u32[]{:S(2)}) collective-permute-start(bf16[128,1536]{1,0:T(8,128)(2,1)S(1)} %get-tuple-element.16), channel_id=1, source_target_pairs={{0,1},{1,0},{2,3},{3,2},{4,5},{5,4},{6,7},{7,6},{8,9},{9,8},{10,11... | collective-permute-start | bytes 1179656 | tf_op jit(solution)/shard_map/ppermute | solution.py:351
  87.4 5.9 %collective-permute-start.5 = (bf16[128,384]{1,0:T(8,128)(2,1)S(1)}, bf16[128,384]{1,0:T(8,128)(2,1)S(1)}, u32[]{:S(2)}, u32[]{:S(2)}) collective-permute-start(bf16[128,384]{1,0:T(8,128)(2,1)S(1)} %get-tuple-element.65), channel_id=1, source_target_pairs={{0,8},{8,0},{1,9},{9,1},{2,10},{10,2},{3,11},{11,3},{4,12},{12,4},... | collective-permute-start | bytes 294920 | tf_op jit(solution)/shard_map/ppermute | solution.py:312
  93.3 1.7 shard_map.148
  95.1 1.8 %add_convert_fusion = bf16[128,1536]{1,0:T(8,128)(2,1)} fusion(f32[128,1536]{1,0:T(8,128)S(1)} %get-tuple-element.15, bf16[128,1536]{1,0:T(8,128)(2,1)} %collective-permute-done.4), kind=kLoop, calls=%fused_computation.13 | loop fusion | flops 589824 | bytes 1572864 | tf_op jit(solution)/shard_map/convert_element_type | solution.py:354
  96.9 3.6 %all-to-all-start.2 = ((bf16[8,16,1536]{2,1,0:T(8,128)(2,1)}), bf16[8,16,1536]{2,1,0:T(8,128)(2,1)S(1)}, u32[]{:S(2)}, u32[]{:S(2)}) async-start(bf16[8,16,1536]{2,1,0:T(8,128)(2,1)} %bitcast.13), calls=%async_computation.2 | async-start | bytes 786432 | tf_op jit(solution)/shard_map/all_to_all | solution.py:355
  100.6 10.5 %all-to-all-done.2 = bf16[8,16,1536]{2,1,0:T(8,128)(2,1)S(1)} async-done(((bf16[8,16,1536]{2,1,0:T(8,128)(2,1)}), bf16[8,16,1536]{2,1,0:T(8,128)(2,1)S(1)}, u32[]{:S(2)}, u32[]{:S(2)}) %all-to-all-start.2) | async-done | bytes 393248 | tf_op jit(solution)/shard_map/all_to_all | solution.py:355
  111.0 0.1 convert_reduce_fusion.2
  111.1 0.2 multiply_reduce_fusion
  111.3 0.1 divide_convert_fusion
  111.4 25.3 %all_gather.11.grad_ref = bf16[256,1664]{1,0:T(8,128)(2,1)S(1)} all-gather(bf16[16,1664]{1,0:T(8,128)(2,1)S(1)} %pad_maximum_fusion.4), channel_id=1, replica_groups=mesh['x'=4,'z'=8,'ylo'=2,'yhi'=4,'core'=2] {'ylo','yhi','core'}, dimensions={0}, use_global_device_ids=true | all-gather | bytes 905216 | tf_op jit(solution)/shard_map/all_gather | solution.py:362
  136.7 1.7 shard_map.150
  138.4 9.6 %all-to-all-start.3 = ((bf16[32,80,128]{2,1,0:T(8,128)(2,1)}), bf16[32,80,128]{2,1,0:T(8,128)(2,1)}, u32[]{:S(2)}, u32[]{:S(2)}) async-start(bf16[32,80,128]{2,1,0:T(8,128)(2,1)} %shard_map.150), calls=%async_computation.3 | async-start | bytes 1310720 | tf_op jit(solution)/shard_map/all_to_all | solution.py:366
  148.0 0.1 dynamic_slice.40
  148.1 0.1 pad_add_fusion.where_ref
  148.2 0.3 fusion.4.gs_ref
  148.4 0.3 broadcast_in_dim.96.gain_ref
  148.7 0.6 copy-done.1
  149.3 1.7 shard_map.151
  151.0 2.3 %collective-permute-start.6 = (bf16[784,128]{1,0:T(8,128)(2,1)S(1)}, bf16[784,128]{1,0:T(8,128)(2,1)S(1)}, u32[]{:S(2)}, u32[]{:S(2)}) collective-permute-start(bf16[784,128]{1,0:T(8,128)(2,1)S(1)} %get-tuple-element.21), channel_id=1, source_target_pairs={{0,1},{1,0},{2,3},{3,2},{4,5},{5,4},{6,7},{7,6},{8,9},{9,8},{10,11... | collective-permute-start | bytes 602120 | tf_op jit(solution)/shard_map/ppermute | solution.py:373
  153.4 1.0 collective-permute-done.6.got_ref
  154.4 0.6 shard_map.152
  155.0 4.0 %collective-permute-start.7 = (bf16[208,128]{1,0:T(8,128)(2,1)S(1)}, bf16[208,128]{1,0:T(8,128)(2,1)S(1)}, u32[]{:S(2)}, u32[]{:S(2)}) collective-permute-start(bf16[208,128]{1,0:T(8,128)(2,1)S(1)} %get-tuple-element.24), channel_id=1, source_target_pairs={{0,2},{2,4},{4,6},{6,0},{1,3},{3,5},{5,7},{7,1},{8,10},{10,12},{12... | collective-permute-start | bytes 159752 | tf_op jit(solution)/shard_map/ppermute | solution.py:375
  159.0 6.0 %collective-permute-start.8 = (bf16[208,128]{1,0:T(8,128)(2,1)S(1)}, bf16[208,128]{1,0:T(8,128)(2,1)S(1)}, u32[]{:S(2)}, u32[]{:S(2)}) collective-permute-start(bf16[208,128]{1,0:T(8,128)(2,1)S(1)} %get-tuple-element.25), channel_id=1, source_target_pairs={{0,4},{2,6},{4,0},{6,2},{1,5},{3,7},{5,1},{7,3},{8,12},{10,14},{12... | collective-permute-start | bytes 159752 | tf_op jit(solution)/shard_map/ppermute | solution.py:375
  165.1 2.2 %collective-permute-start.9 = (bf16[208,128]{1,0:T(8,128)(2,1)S(1)}, bf16[208,128]{1,0:T(8,128)(2,1)S(1)}, u32[]{:S(2)}, u32[]{:S(2)}) collective-permute-start(bf16[208,128]{1,0:T(8,128)(2,1)S(1)} %get-tuple-element.26), channel_id=1, source_target_pairs={{0,6},{2,0},{4,2},{6,4},{1,7},{3,1},{5,3},{7,5},{8,14},{10,8},{12,... | collective-permute-start | bytes 159752 | tf_op jit(solution)/shard_map/ppermute | solution.py:375
  167.3 0.1 broadcast_multiply_fusion.invgain_ref
  167.4 0.1 dynamic_slice.41.grad_ref
  167.5 0.7 collective-permute-done.8.two_ref
  168.2 4.9 %collective-permute-done.9.three_ref = bf16[208,128]{1,0:T(8,128)(2,1)S(1)} collective-permute-done((bf16[208,128]{1,0:T(8,128)(2,1)S(1)}, bf16[208,128]{1,0:T(8,128)(2,1)S(1)}, u32[]{:S(2)}, u32[]{:S(2)}) %collective-permute-start.9) | collective-permute-done | bytes 53280 | tf_op jit(solution)/shard_map/ppermute | solution.py:375
  173.1 0.1 shard_map.153
  173.3 0.7 copy.48
  174.0 1.2 convert_reduce_fusion
  175.2 0.6 slice_reduce_fusion
  175.8 0.6 copy.54
  (53 shorter events, 0.4 us)
Async XLA Ops:
  0.6 23.6 %copy-start.8 = (f32[192]{0:T(256)S(1)}, f32[192]{0:T(256)}, u32[]{:S(2)}) copy-start(f32[192]{0:T(256)} %param.19) | copy-start | bytes 2308
  0.6 23.9 %copy-start.7 = (f32[1536]{0:T(1024)S(1)}, f32[1536]{0:T(1024)}, u32[]{:S(2)}) copy-start(f32[1536]{0:T(1024)} %param.14) | copy-start | bytes 18436
  0.7 23.9 %copy-start.11 = (f32[1536]{0:T(1024)S(1)}, f32[1536]{0:T(1024)}, u32[]{:S(2)}) copy-start(f32[1536]{0:T(1024)} %param.15) | copy-start | bytes 18436
  0.7 23.9 %copy-start.2 = (bf16[1536,384]{1,0:T(8,128)(2,1)S(1)}, bf16[1536,384]{1,0:T(8,128)(2,1)}, u32[]{:S(2)}) copy-start(bf16[1536,384]{1,0:T(8,128)(2,1)} %up_ref.1) | copy-start | bytes 3538948
  0.7 23.9 %copy-start.12 = (f32[384]{0:T(512)S(1)}, f32[384]{0:T(512)}, u32[]{:S(2)}) copy-start(f32[384]{0:T(512)} %param.17) | copy-start | bytes 4612
  23.8 4.6 %copy-start.4 = (bf16[256,1536]{0,1:T(8,128)(2,1)}, bf16[256,1536]{0,1:T(8,128)(2,1)S(1)}, u32[]{:S(2)}) copy-start(bf16[256,1536]{0,1:T(8,128)(2,1)S(1)} %all_gather.9) | copy-start | bytes 2359300
  24.6 1.3 copy-start
  26.3 2.8 %copy-start.9 = (s32[128]{0:T(128)S(1)}, s32[128]{0:T(128)}, u32[]{:S(2)}) copy-start(s32[128]{0:T(128)} %param.22) | copy-start | bytes 1540
  26.3 2.8 %copy-start.10 = (s32[128]{0:T(128)S(1)}, s32[128]{0:T(128)}, u32[]{:S(2)}) copy-start(s32[128]{0:T(128)} %param.21) | copy-start | bytes 1540
  26.3 14.0 %collective-permute-start = (bf16[4,16,1536]{2,1,0:T(8,128)(2,1)S(1)}, bf16[4,16,1536]{2,1,0:T(8,128)(2,1)S(1)}, u32[]{:S(2)}, u32[]{:S(2)}) collective-permute-start(bf16[4,16,1536]{2,1,0:T(8,128)(2,1)S(1)} %fusion.21), channel_id=1, source_target_pairs={{0,1},{1,0},{2,3},{3,2},{4,5},{5,4},{6,7},{7,6},{8,9},{9,8},{10,11... | collective-permute-start | bytes 589832 | tf_op jit(solution)/shard_map/ppermute | solution.py:325
  30.2 25.1 %all-to-all-start = ((bf16[8,16,1664]{2,1,0:T(8,128)(2,1)}), bf16[8,16,1664]{2,1,0:T(8,128)(2,1)S(1)}, u32[]{:S(2)}, u32[]{:S(2)}) async-start(bf16[8,16,1664]{2,1,0:T(8,128)(2,1)} %broadcast_in_dim.93), calls=%async_computation | async-start | bytes 851968 | tf_op jit(solution)/shard_map/all_to_all | solution.py:45
  40.3 12.8 %collective-permute-start.1 = (bf16[16,1536]{1,0:T(8,128)(2,1)S(1)}, bf16[16,1536]{1,0:T(8,128)(2,1)S(1)}, u32[]{:S(2)}, u32[]{:S(2)}) collective-permute-start(bf16[16,1536]{1,0:T(8,128)(2,1)S(1)} %get-tuple-element.51), channel_id=1, source_target_pairs={{0,2},{2,4},{4,6},{6,0},{1,3},{3,5},{5,7},{7,1},{8,10},{10,12},{12... | collective-permute-start | bytes 147464 | tf_op jit(solution)/shard_map/ppermute | solution.py:334
  42.3 10.9 %collective-permute-start.2 = (bf16[16,1536]{1,0:T(8,128)(2,1)S(1)}, bf16[16,1536]{1,0:T(8,128)(2,1)S(1)}, u32[]{:S(2)}, u32[]{:S(2)}) collective-permute-start(bf16[16,1536]{1,0:T(8,128)(2,1)S(1)} %get-tuple-element.53), channel_id=1, source_target_pairs={{0,4},{2,6},{4,0},{6,2},{1,5},{3,7},{5,1},{7,3},{8,12},{10,14},{12... | collective-permute-start | bytes 147464 | tf_op jit(solution)/shard_map/ppermute | solution.py:334
  47.5 7.6 %collective-permute-start.3 = (bf16[16,1536]{1,0:T(8,128)(2,1)S(1)}, bf16[16,1536]{1,0:T(8,128)(2,1)S(1)}, u32[]{:S(2)}, u32[]{:S(2)}) collective-permute-start(bf16[16,1536]{1,0:T(8,128)(2,1)S(1)} %get-tuple-element.52), channel_id=1, source_target_pairs={{0,6},{2,0},{4,2},{6,4},{1,7},{3,1},{5,3},{7,5},{8,14},{10,8},{12,... | collective-permute-start | bytes 147464 | tf_op jit(solution)/shard_map/ppermute | solution.py:334
  56.6 27.0 %all-to-all-start.1 = ((bf16[4,128,1664]{2,1,0:T(8,128)(2,1)}), bf16[4,128,1664]{2,1,0:T(8,128)(2,1)S(1)}, u32[]{:S(2)}, u32[]{:S(2)}) async-start(bf16[4,128,1664]{2,1,0:T(8,128)(2,1)} %broadcast_in_dim.95), calls=%async_computation.1 | async-start | bytes 3407872 | tf_op jit(solution)/shard_map/all_to_all | solution.py:45
  85.3 9.8 %collective-permute-start.4 = (bf16[128,1536]{1,0:T(8,128)(2,1)S(1)}, bf16[128,1536]{1,0:T(8,128)(2,1)}, u32[]{:S(2)}, u32[]{:S(2)}) collective-permute-start(bf16[128,1536]{1,0:T(8,128)(2,1)S(1)} %get-tuple-element.16), channel_id=1, source_target_pairs={{0,1},{1,0},{2,3},{3,2},{4,5},{5,4},{6,7},{7,6},{8,9},{9,8},{10,11... | collective-permute-start | bytes 1179656 | tf_op jit(solution)/shard_map/ppermute | solution.py:351
  87.4 13.0 %collective-permute-start.5 = (bf16[128,384]{1,0:T(8,128)(2,1)S(1)}, bf16[128,384]{1,0:T(8,128)(2,1)S(1)}, u32[]{:S(2)}, u32[]{:S(2)}) collective-permute-start(bf16[128,384]{1,0:T(8,128)(2,1)S(1)} %get-tuple-element.65), channel_id=1, source_target_pairs={{0,8},{8,0},{1,9},{9,1},{2,10},{10,2},{3,11},{11,3},{4,12},{12,4},... | collective-permute-start | bytes 294920 | tf_op jit(solution)/shard_map/ppermute | solution.py:312
  96.9 14.1 %all-to-all-start.2 = ((bf16[8,16,1536]{2,1,0:T(8,128)(2,1)}), bf16[8,16,1536]{2,1,0:T(8,128)(2,1)S(1)}, u32[]{:S(2)}, u32[]{:S(2)}) async-start(bf16[8,16,1536]{2,1,0:T(8,128)(2,1)} %bitcast.13), calls=%async_computation.2 | async-start | bytes 786432 | tf_op jit(solution)/shard_map/all_to_all | solution.py:355
  136.7 11.5 %copy-start.5 = (bf16[256,1536]{0,1:T(8,128)(2,1)S(1)}, bf16[256,1536]{0,1:T(8,128)(2,1)}, u32[]{:S(2)}) copy-start(bf16[256,1536]{0,1:T(8,128)(2,1)} %copy-done.4) | copy-start | bytes 2359300
  138.4 10.3 %copy-start.3 = (bf16[1536,384]{1,0:T(8,128)(2,1)S(1)}, bf16[1536,384]{1,0:T(8,128)(2,1)}, u32[]{:S(2)}) copy-start(bf16[1536,384]{1,0:T(8,128)(2,1)} %up_ref.1) | copy-start | bytes 3538948
  138.4 35.6 %all-to-all-start.3 = ((bf16[32,80,128]{2,1,0:T(8,128)(2,1)}), bf16[32,80,128]{2,1,0:T(8,128)(2,1)}, u32[]{:S(2)}, u32[]{:S(2)}) async-start(bf16[32,80,128]{2,1,0:T(8,128)(2,1)} %shard_map.150), calls=%async_computation.3 | async-start | bytes 1310720 | tf_op jit(solution)/shard_map/all_to_all | solution.py:366
  148.0 1.3 copy-start.1
  149.3 4.1 %copy-start.6 = (bf16[128,192]{0,1:T(8,128)(2,1)S(1)}, bf16[128,192]{0,1:T(8,128)(2,1)}, u32[]{:S(2)}) copy-start(bf16[128,192]{0,1:T(8,128)(2,1)} %param.13) | copy-start | bytes 147460
  151.0 3.4 %collective-permute-start.6 = (bf16[784,128]{1,0:T(8,128)(2,1)S(1)}, bf16[784,128]{1,0:T(8,128)(2,1)S(1)}, u32[]{:S(2)}, u32[]{:S(2)}) collective-permute-start(bf16[784,128]{1,0:T(8,128)(2,1)S(1)} %get-tuple-element.21), channel_id=1, source_target_pairs={{0,1},{1,0},{2,3},{3,2},{4,5},{5,4},{6,7},{7,6},{8,9},{9,8},{10,11... | collective-permute-start | bytes 602120 | tf_op jit(solution)/shard_map/ppermute | solution.py:373
  155.0 12.5 %collective-permute-start.7 = (bf16[208,128]{1,0:T(8,128)(2,1)S(1)}, bf16[208,128]{1,0:T(8,128)(2,1)S(1)}, u32[]{:S(2)}, u32[]{:S(2)}) collective-permute-start(bf16[208,128]{1,0:T(8,128)(2,1)S(1)} %get-tuple-element.24), channel_id=1, source_target_pairs={{0,2},{2,4},{4,6},{6,0},{1,3},{3,5},{5,7},{7,1},{8,10},{10,12},{12... | collective-permute-start | bytes 159752 | tf_op jit(solution)/shard_map/ppermute | solution.py:375
  159.0 9.2 %collective-permute-start.8 = (bf16[208,128]{1,0:T(8,128)(2,1)S(1)}, bf16[208,128]{1,0:T(8,128)(2,1)S(1)}, u32[]{:S(2)}, u32[]{:S(2)}) collective-permute-start(bf16[208,128]{1,0:T(8,128)(2,1)S(1)} %get-tuple-element.25), channel_id=1, source_target_pairs={{0,4},{2,6},{4,0},{6,2},{1,5},{3,7},{5,1},{7,3},{8,12},{10,14},{12... | collective-permute-start | bytes 159752 | tf_op jit(solution)/shard_map/ppermute | solution.py:375
  165.1 8.1 %collective-permute-start.9 = (bf16[208,128]{1,0:T(8,128)(2,1)S(1)}, bf16[208,128]{1,0:T(8,128)(2,1)S(1)}, u32[]{:S(2)}, u32[]{:S(2)}) collective-permute-start(bf16[208,128]{1,0:T(8,128)(2,1)S(1)} %get-tuple-element.26), channel_id=1, source_target_pairs={{0,6},{2,0},{4,2},{6,4},{1,7},{3,1},{5,3},{7,5},{8,14},{10,8},{12,... | collective-permute-start | bytes 159752 | tf_op jit(solution)/shard_map/ppermute | solution.py:375

commit v4 on v3

--- a/solution.py
+++ b/solution.py
@@ -10,6 +10,7 @@
 SLICE = 192
 EXTRA = 128
 IMG = 16
+BATCH = 8192
 DATA = ("x", "z", "ylo")
 TENS = ("yhi", "core")
 RING = ("ylo", "yhi", "core")
@@ -67,7 +68,8 @@
     return first, values - first
 
 
-def pair_kernel(which_ref, scalar_ref, img_ref, txt_ref, out_ref, loss_ref):
+def pair_kernel(which_ref, scalar_ref, img_ref, txt_ref, *refs):
+    out_ref, loss_ref = refs[-2:]
     img = img_ref[:, which_ref[0]].reshape(ROWS, WIDE + EXTRA)
     txt = txt_ref[:, :WIDE]
     across = (((1,), (1,)), ((), ()))
@@ -86,15 +88,18 @@
     sigmoid = jnp.where(margin >= 0.0, 1.0, shrunk) / (1.0 + shrunk)
     scale = scalar_ref[2]
     weights = (jnp.where(positive, -scale, scale) * sigmoid).astype(jnp.bfloat16)
-    out_ref[...] = jnp.dot(weights, txt, preferred_element_type=jnp.float32).astype(out_ref.dtype)
+    part = jnp.dot(weights, txt, preferred_element_type=jnp.float32)
+    if len(refs) == 3:
+        part = part + refs[0][...].astype(jnp.float32)
+    out_ref[...] = part.astype(jnp.bfloat16)
     folded = losses[:, :128] + losses[:, 128:256] + losses[:, 256:384] + losses[:, 384:]
     loss_ref[...] = jnp.sum(folded.reshape(16, 8, 128), axis=0)
 
 
-def pair_rows(which, scalars, img_all, txt_all, kind):
+def pair_rows(which, scalars, img_all, txt_all, *added):
     return call(
         pair_kernel,
-        [((ROWS, WIDE), kind), ((8, 128), jnp.float32)],
+        [((ROWS, WIDE), jnp.bfloat16), ((8, 128), jnp.float32)],
         2,
         4 * ROWS * 512 * WIDE,
         3000000,
@@ -102,6 +107,7 @@
         scalars,
         img_all.reshape(8, 2, IMG, WIDE + EXTRA),
         txt_all,
+        *added,
     )
 
 
@@ -192,7 +198,7 @@
 
 
 def last_kernel(
-    keep_ref, all_ref, one_ref, two_ref, three_ref, inv_ref, invgain_ref, invscaled_ref, grad_ref, out_ref
+    keep_ref, all_ref, one_ref, two_ref, three_ref, inv_ref, invgain_ref, invscaled_ref, grad_ref, got_ref, out_ref, down_ref, loss_ref
 ):
     total = keep_ref[...]
     sum_h = all_ref[0:1]
@@ -208,15 +214,24 @@
         - invscaled_ref[...] * (sum_hs / WIDE)
     )
     out_ref[...] = (grad_ref[...].astype(jnp.float32) + side.T).astype(jnp.bfloat16)
-
-
-def last_rows(keep, sums, gots, inverse_t, invgain, invscaled, grad_own):
+    summed = jnp.sum(got_ref[...].astype(jnp.float32), axis=0)
+    for piece in range(3):
+        down_ref[piece * 128 : (piece + 1) * 128] = summed[piece * 24 : (piece + 1) * 24].T
+    tail = jnp.sum(summed[72:], axis=1, keepdims=True)
+    loss_ref[...] = jnp.sum(tail, axis=0, keepdims=True) / BATCH
+
+
+def last_rows(keep, sums, gots, inverse_t, invgain, invscaled, grad_own, down_got):
     return call(
         last_kernel,
-        [((ROWS, SLICE), jnp.bfloat16)],
+        [
+            ((ROWS, SLICE), jnp.bfloat16),
+            ((384, 24), jnp.float32),
+            ((1, 1), jnp.float32),
+        ],
         0,
         1000000,
-        800000,
+        1600000,
         keep,
         sums,
         *gots,
@@ -224,16 +239,22 @@
         invgain,
         invscaled,
         grad_own,
-    )[0]
-
-
-def down_kernel(ylo_ref, grad_ref, hidden_ref, out_ref):
+        down_got,
+    )
+
+
+def down_kernel(ylo_ref, grad_ref, hidden_ref, other_ref, out_ref):
     even = ylo_ref[0] == 0
     rows = grad_ref[:, :WIDE]
+    mine = hidden_ref[...]
+    other = other_ref[...]
+    hidden = jnp.concatenate(
+        [jnp.where(even, mine, other), jnp.where(even, other, mine)], axis=0
+    )
     for piece in range(3):
         part = lax.dot_general(
             rows,
-            hidden_ref[:, piece * 128 : (piece + 1) * 128],
+            hidden[:, piece * 128 : (piece + 1) * 128],
             (((0,), (0,)), ((), ())),
             preferred_element_type=jnp.float32,
         ).reshape(32, 2, 24, 128)
@@ -252,12 +273,13 @@
     out_ref[:, 72:, :] = jnp.broadcast_to(block[None], (32, 8, 128)).astype(jnp.bfloat16)
 
 
-def down_block(ylo, grad_all, hidden_pair):
+def down_block(ylo, grad_all, hidden, hidden_other):
     return pl.pallas_call(
         down_kernel,
         out_shape=jax.ShapeDtypeStruct((32, 80, 128), jnp.bfloat16),
         in_specs=[
             pl.BlockSpec(memory_space=pltpu.SMEM),
+            pl.BlockSpec(memory_space=pltpu.VMEM),
             pl.BlockSpec(memory_space=pltpu.VMEM),
             pl.BlockSpec(memory_space=pltpu.VMEM),
         ],
@@ -266,7 +288,7 @@
         cost_estimate=pl.CostEstimate(
             flops=2 * 256 * WIDE * 384, bytes_accessed=1700000, transcendentals=0
         ),
-    )(ylo.reshape(1).astype(jnp.int32), grad_all, hidden_pair)
+    )(ylo.reshape(1).astype(jnp.int32), grad_all, hidden, hidden_other)
 
 
 def turn(step):
@@ -291,7 +313,6 @@
     tens = lax.axis_index(TENS)
     row0 = tens * IMG
     col0 = tens * SLICE
-    batch = ROWS * 64
 
     both = lax.all_gather(
         jnp.concatenate([pooled, text_embed], axis=0), TENS, axis=1, tiled=True
@@ -299,7 +320,7 @@
     txt_rows = lax.dynamic_slice_in_dim(both, ROWS + row0, IMG, 0).astype(jnp.float32)
     txt_norm = jnp.sqrt(jnp.sum(txt_rows * txt_rows, axis=1, keepdims=True) + 1e-06)
     txt_low = (txt_rows / txt_norm).astype(jnp.bfloat16)
-    txt_z = spread(jnp.concatenate([txt_low, id_columns(text_ids, row0)], axis=1), "z", 8)
+    txt_send = jnp.concatenate([txt_low, id_columns(text_ids, row0)], axis=1)
 
     wide = both[:ROWS].astype(jnp.float32)
     average = jnp.mean(wide, axis=1, keepdims=True)
@@ -309,12 +330,6 @@
     normed = (scaled * ln_gain + ln_bias).astype(jnp.bfloat16)
     preact = jnp.dot(normed, w_up, preferred_element_type=jnp.float32) + b_up
     hidden = gelu_fn(preact).astype(jnp.bfloat16)
-    hidden_other = lax.ppermute(hidden, "ylo", [(0, 1), (1, 0)])
-    ylo = lax.axis_index("ylo")
-    hidden_pair = jnp.concatenate(
-        [jnp.where(ylo == 0, hidden, hidden_other), jnp.where(ylo == 0, hidden_other, hidden)],
-        axis=0,
-    )
     bias_row = lax.dynamic_update_slice_in_dim(
         jnp.zeros((WIDE,), jnp.float32), b_down, col0, 0
     )
@@ -322,8 +337,11 @@
     core = lax.axis_index("core")
     yhi = lax.axis_index("yhi")
     part = part.reshape(4, 2, IMG, WIDE)
+    part_other = lax.dynamic_index_in_dim(part, 1 - core, 1, keepdims=False).astype(jnp.bfloat16)
+    part_other, txt_send = lax.optimization_barrier((part_other, txt_send))
+    txt_all = spread(txt_send, ("x", "z"), 32)
     core_got = lax.ppermute(
-        lax.dynamic_index_in_dim(part, 1 - core, 1, keepdims=False).astype(jnp.bfloat16),
+        part_other,
         "core",
         [(0, 1), (1, 0)],
     )
@@ -337,7 +355,6 @@
     summed = own + mixed
     img_norm = jnp.sqrt(jnp.sum(summed * summed, axis=1, keepdims=True) + 1e-06)
     img_unit = summed / img_norm
-    txt_all = spread(txt_z, "x", 4)
     img_send = jnp.concatenate(
         [img_unit.astype(jnp.bfloat16), id_columns(image_ids, row0)], axis=1
     )
@@ -345,31 +362,35 @@
 
     temper = logit_scale[0]
     offset = logit_bias[0]
-    factor = loss_scale[0] / batch
+    factor = loss_scale[0] / BATCH
     scalars = jnp.stack([temper, offset, temper * factor])
-    other_part, other_loss = pair_rows(1 - core, scalars, img_all, txt_all, jnp.bfloat16)
+    other_part, other_loss = pair_rows(1 - core, scalars, img_all, txt_all)
     from_other = lax.ppermute(other_part, "core", [(0, 1), (1, 0)])
-    own_part, own_loss = pair_rows(core, scalars, img_all, txt_all, jnp.float32)
-    loss_part = jnp.sum(other_loss + own_loss, axis=0)
-    chip_part = (own_part + from_other.astype(jnp.float32)).astype(jnp.bfloat16)
+    chip_part, own_loss = pair_rows(core, scalars, img_all, txt_all, from_other)
+    scaled_late, own_loss = lax.optimization_barrier((scaled, own_loss))
+    gain_t = jnp.broadcast_to(ln_gain[:, None], (WIDE, ROWS))
+    gs_t = gain_t * scaled_late.T
+    hidden_late, gs_t = lax.optimization_barrier((hidden, gs_t))
+    hidden_other = lax.ppermute(hidden_late, "ylo", [(0, 1), (1, 0)])
+    ylo = lax.axis_index("ylo")
     unit_parts = lax.all_to_all(
         chip_part, ("ylo", "yhi"), split_axis=0, concat_axis=0, tiled=True
     )
     grad_unit = jnp.sum(unit_parts.reshape(8, IMG, WIDE).astype(jnp.float32), axis=0)
     tangent = jnp.sum(img_unit * grad_unit, axis=1, keepdims=True)
     grad_low = ((grad_unit - img_unit * tangent) / img_norm).astype(jnp.bfloat16)
+    loss_part = jnp.sum(other_loss + own_loss, axis=0)
     loss_block = jnp.pad(pieces(loss_part, 3), ((0, IMG - 3), (0, 0)))
     grad_all = lax.all_gather(
         jnp.concatenate([grad_low, loss_block], axis=1), RING, axis=0, tiled=True
     )
-    down_send = down_block(ylo, grad_all, hidden_pair)
+    where = jnp.stack([ylo, core, yhi]).astype(jnp.int32)
+    send, own_blocks, own_sums = back_rows(
+        where, grad_all, w_down, preact, w_up, gain_t, gs_t
+    )
+    grad_late, send = lax.optimization_barrier((grad_all, send))
+    down_send = down_block(ylo, grad_late, hidden, hidden_other)
     down_got = lax.all_to_all(down_send, ("x", "z"), split_axis=0, concat_axis=0, tiled=True)
-
-    where = jnp.stack([ylo, core, yhi]).astype(jnp.int32)
-    gain_t = jnp.broadcast_to(ln_gain[:, None], (WIDE, ROWS))
-    send, own_blocks, own_sums = back_rows(
-        where, grad_all, w_down, preact, w_up, gain_t, gain_t * scaled.T
-    )
     got = lax.ppermute(send, "core", [(0, 1), (1, 0)])
     sends = chip_rows(where, own_blocks, own_sums, got)
     gots = [lax.ppermute(sends[step - 1], "yhi", turn(step)) for step in range(1, 4)]
@@ -377,15 +398,11 @@
     scaled_own = ((pooled.astype(jnp.float32) - average) * inverse).T
     inverse_t = jnp.broadcast_to(inverse.reshape(1, ROWS), (8, ROWS))
     grad_own = lax.dynamic_slice(grad_all, (ylo * ROWS, col0), (ROWS, SLICE))
-    grad_pooled = last_rows(
+    grad_pooled, grad_down, loss = last_rows(
         sends[3], sends[4], gots, inverse_t, inverse_t[:1] * gain_own[:, None],
-        inverse_t[:1] * scaled_own, grad_own,
-    )
-
-    down_sum = jnp.sum(down_got.astype(jnp.float32), axis=0)
-    grad_down = down_sum[:72].reshape(3, 24, 128).transpose(0, 2, 1).reshape(384, 24)
-    loss = (jnp.sum(down_sum[72:75]) / batch).reshape(1)
-    return (loss, grad_pooled, grad_down)
+        inverse_t[:1] * scaled_own, grad_own, down_got,
+    )
+    return (loss.reshape(1), grad_pooled, grad_down)
 
 
 def solution(mesh):

time: 179 us -> 172 us (0.961)
  waiting for transfers between devices: 19 us -> 14 us
    all_to_all x1, starting transfers between devices: 3.55 us -> 7.06 us  [shards(): lax.all_to_all(chip_part, ('ylo', 'yhi'), split_axis=0, concat_axis=0, ti...]
    all_to_all x1, waiting for transfers between devices: 10.5 us -> 7.53 us  [shards(): lax.all_to_all(chip_part, ('ylo', 'yhi'), split_axis=0, concat_axis=0, ti...]
    ppermute x3, waiting for transfers between devices: 5.64 us -> 3.02 us  [shards(): lax.ppermute(sends[step - 1], 'yhi', turn(step))]
    ppermute x2, starting transfers between devices: 7.99 us -> 5.72 us  [the longest x1 3.37 us: shards(): hidden_other = lax.ppermute(hidden_late, 'ylo', [(0, 1), (1, 0)])]
    convert_element_type x1 -> x0, other arithmetic: 1.81 us -> none  [shards(): chip_part = (own_part + from_other.astype(jnp.float32)).astype(jnp.bfloat16)]
    reduce_sum x2 -> x0, other arithmetic: 1.79 us -> none  [the longest x1 1.19 us: shards(): down_sum = jnp.sum(down_got.astype(jnp.float32), axis=0)]
    all_to_all x2 -> x1, starting transfers between devices: 12.1 us -> 11 us  [spread(): lax.all_to_all(send, axis, split_axis=0, concat_axis=0, tiled=True)]
  transfers between devices with their start and end apart: 14 -> 13, of which waited for: 5 -> 6; matrix products, arithmetic and copies ran while one was open for 3% -> 3% of each run, Pallas kernels for 2% -> 1%
where the time goes in v4:
time: 172 us; the launch traced here: 170 us
  blocking collectives  68.9 us (40%)
  starting transfers between devices  62.1 us (36%)
  waiting for transfers between devices  14 us (8%)
  Pallas kernels  8.97 us (5%)
  local copies, waits for them, and re-layouts  6.12 us (4%)
  other arithmetic  5.64 us (3%)
  between operations  3.08 us (2%)
    all_gather x1, blocking collectives, shards(): lax.all_gather(jnp.concatenate([grad_low, loss_block], axis=1), RING, axi...  24.4 us
    all_gather x1, blocking collectives, shards(): img_all = lax.all_gather(img_send, RING, axis=0, tiled=True)  22.3 us
    all_gather x1, blocking collectives, shards(): lax.all_gather(jnp.concatenate([pooled, text_embed], axis=0), TENS, axis=...  22.2 us
    ppermute x3, starting transfers between devices, shards(): got = lax.ppermute(block.astype(jnp.bfloat16), 'yhi', turn(step))  12.6 us
    ppermute x3, starting transfers between devices, shards(): lax.ppermute(sends[step - 1], 'yhi', turn(step))  11.7 us
    all_to_all x1, starting transfers between devices, spread(): lax.all_to_all(send, axis, split_axis=0, concat_axis=0, tiled=True)  11 us
    all_to_all x1, starting transfers between devices, shards(): lax.all_to_all(down_send, ('x', 'z'), split_axis=0, concat_axis=0, tiled=...  9.62 us
    all_to_all x1, waiting for transfers between devices, shards(): lax.all_to_all(chip_part, ('ylo', 'yhi'), split_axis=0, concat_axis=0, ti...  7.53 us
  transfers between devices with their start and end apart: 13, of which 6 were waited for; matrix products, arithmetic and copies ran while one was open for 3% of the time, Pallas kernels for 1%

profile of v4, /device:TPU:1, one launch (start us, length us, event | category | flops | bytes accessed | tf_op | source)
XLA Modules:
  0.0 170.1 jit_solution(7580506520259843260)
XLA Ops:
  0.7 0.8 pad_maximum_fusion
  1.5 22.2 %all_gather.9 = bf16[256,1536]{0,1:T(8,128)(2,1)S(1)} all-gather(bf16[256,192]{0,1:T(8,128)(2,1)S(1)} %pad_maximum_fusion), channel_id=1, replica_groups=mesh['x'=4,'z'=8,'ylo'=2,'yhi'=4,'core'=2] {'yhi','core'}, dimensions={1}, use_global_device_ids=true | all-gather | bytes 884736 | tf_op jit(solution)/shard_map/all_gather | solution.py:317
  23.7 0.2 convert_reduce_fusion
  23.9 0.0 copy-start.11
  23.9 0.0 copy-start.8
  24.0 0.3 constant_dynamic-slice_fusion.1
  24.3 0.1 copy.52
  24.4 0.1 fusion.14
  24.6 0.1 fusion.15
  24.7 0.2 fusion.2
  24.9 0.2 convert_reduce_fusion.3
  25.1 0.1 select_convert_fusion.1
  25.2 0.3 dynamic_update_slice.5
  25.5 1.0 fusion.12
  26.5 0.3 copy-done
  26.8 0.4 convolution_add_fusion
  27.2 0.7 fusion.13
  27.9 1.3 broadcast_in_dim.86
  29.2 11.0 %all-to-all-start = ((bf16[32,16,1664]{2,1,0:T(8,128)(2,1)}), bf16[32,16,1664]{2,1,0:T(8,128)(2,1)S(1)}, u32[]{:S(2)}, u32[]{:S(2)}) async-start(bf16[32,16,1664]{2,1,0:T(8,128)(2,1)} %broadcast_in_dim.86), calls=%async_computation | async-start | bytes 3407872 | tf_op jit(solution)/shard_map/all_to_all | solution.py:46
  40.2 2.3 %collective-permute-start = (bf16[4,16,1536]{2,1,0:T(8,128)(2,1)}, bf16[4,16,1536]{2,1,0:T(8,128)(2,1)S(1)}, u32[]{:S(2)}, u32[]{:S(2)}) collective-permute-start(bf16[4,16,1536]{2,1,0:T(8,128)(2,1)} %fusion.13), channel_id=1, source_target_pairs={{0,1},{1,0},{2,3},{3,2},{4,5},{5,4},{6,7},{7,6},{8,9},{9,8},{10,11... | collective-permute-start | bytes 589832 | tf_op jit(solution)/shard_map/ppermute | solution.py:343
  44.5 0.1 pad_maximum_fusion.4.scalar_ref
  44.6 0.8 bitcast_add_fusion
  45.4 1.0 fusion.20
  46.4 1.9 %collective-permute-start.1 = (bf16[16,1536]{1,0:T(8,128)(2,1)S(1)}, bf16[16,1536]{1,0:T(8,128)(2,1)S(1)}, u32[]{:S(2)}, u32[]{:S(2)}) collective-permute-start(bf16[16,1536]{1,0:T(8,128)(2,1)S(1)} %get-tuple-element.73), channel_id=1, source_target_pairs={{0,2},{2,4},{4,6},{6,0},{1,3},{3,5},{5,7},{7,1},{8,10},{10,12},{12... | collective-permute-start | bytes 147464 | tf_op jit(solution)/shard_map/ppermute | solution.py:352
  48.3 5.2 %collective-permute-start.2 = (bf16[16,1536]{1,0:T(8,128)(2,1)S(1)}, bf16[16,1536]{1,0:T(8,128)(2,1)S(1)}, u32[]{:S(2)}, u32[]{:S(2)}) collective-permute-start(bf16[16,1536]{1,0:T(8,128)(2,1)S(1)} %get-tuple-element.75), channel_id=1, source_target_pairs={{0,4},{2,6},{4,0},{6,2},{1,5},{3,7},{5,1},{7,3},{8,12},{10,14},{12... | collective-permute-start | bytes 147464 | tf_op jit(solution)/shard_map/ppermute | solution.py:352
  53.6 5.5 %collective-permute-start.3 = (bf16[16,1536]{1,0:T(8,128)(2,1)S(1)}, bf16[16,1536]{1,0:T(8,128)(2,1)S(1)}, u32[]{:S(2)}, u32[]{:S(2)}) collective-permute-start(bf16[16,1536]{1,0:T(8,128)(2,1)S(1)} %get-tuple-element.74), channel_id=1, source_target_pairs={{0,6},{2,0},{4,2},{6,4},{1,7},{3,1},{5,3},{7,5},{8,14},{10,8},{12,... | collective-permute-start | bytes 147464 | tf_op jit(solution)/shard_map/ppermute | solution.py:352
  59.0 0.1 pad_add_fusion.where_ref
  59.1 0.1 copy.50
  59.3 0.0 collective-permute-done.2
  59.3 1.9 %collective-permute-done.3 = bf16[16,1536]{1,0:T(8,128)(2,1)S(1)} collective-permute-done((bf16[16,1536]{1,0:T(8,128)(2,1)S(1)}, bf16[16,1536]{1,0:T(8,128)(2,1)S(1)}, u32[]{:S(2)}, u32[]{:S(2)}) %collective-permute-start.3) | collective-permute-done | bytes 49184 | tf_op jit(solution)/shard_map/ppermute | solution.py:352
  61.2 1.0 multiply_reduce_fusion.1
  62.2 0.1 fusion.30
  62.3 22.3 %all_gather.10 = bf16[256,1664]{1,0:T(8,128)(2,1)S(1)} all-gather(bf16[16,1664]{1,0:T(8,128)(2,1)S(1)} %pad_maximum_fusion.2), channel_id=1, replica_groups=mesh['x'=4,'z'=8,'ylo'=2,'yhi'=4,'core'=2] {'ylo','yhi','core'}, dimensions={0}, use_global_device_ids=true | all-gather | bytes 905216 | tf_op jit(solution)/shard_map/all_gather | solution.py:361
  84.6 1.7 %shard_map.148 = (bf16[128,1536]{1,0:T(8,128)(2,1)S(1)}, f32[8,128]{1,0:T(8,128)S(1)}) custom-call(s32[1]{0:T(128)} %bitcast.12.which_ref, f32[3]{0:T(128)S(1)} %pad_maximum_fusion.4.scalar_ref, bf16[8,2,16,1664]{3,2,1,0:T(8,128)(2,1)S(1)} %bitcast.50, bf16[512,1664]{1,0:T(8,128)(2,1)S(1)} %bitcast.47), custom_call_target="tpu_custom_call" | custom-call | flops 402653184 | bytes 3000000 | tf_op jit(solution)/shard_map/pallas_call | solution.py:56
  86.4 2.1 %collective-permute-start.4 = (bf16[128,1536]{1,0:T(8,128)(2,1)S(1)}, bf16[128,1536]{1,0:T(8,128)(2,1)S(1)}, u32[]{:S(2)}, u32[]{:S(2)}) collective-permute-start(bf16[128,1536]{1,0:T(8,128)(2,1)S(1)} %get-tuple-element.28), channel_id=1, source_target_pairs={{0,1},{1,0},{2,3},{3,2},{4,5},{5,4},{6,7},{7,6},{8,9},{9,8},{10,11... | collective-permute-start | bytes 1179656 | tf_op jit(solution)/shard_map/ppermute | solution.py:368
  88.5 1.0 fusion
  89.4 0.6 collective-permute-done.4.refs_0_
  90.0 2.5 %shard_map.149 = (bf16[128,1536]{1,0:T(8,128)(2,1)}, f32[8,128]{1,0:T(8,128)S(1)}) custom-call(s32[1]{0:T(128)} %bitcast.1.which_ref, f32[3]{0:T(128)S(1)} %pad_maximum_fusion.4.scalar_ref, bf16[8,2,16,1664]{3,2,1,0:T(8,128)(2,1)S(1)} %bitcast.51, bf16[512,1664]{1,0:T(8,128)(2,1)S(1)} %bitcast.48, bf16[128,1536]{1,0:T(8,128)(2,1)S(1)} %collective-permute-done.4.refs_0_), custom_call_target="tpu_custom_call" | custom-call | flops 402653184 | bytes 3000000 | tf_op jit(solution)/shard_map/pallas_call | solution.py:56
  92.5 7.1 %all-to-all-start.1 = ((bf16[8,16,1536]{2,1,0:T(8,128)(2,1)}), bf16[8,16,1536]{2,1,0:T(8,128)(2,1)S(1)}, u32[]{:S(2)}, u32[]{:S(2)}) async-start(bf16[8,16,1536]{2,1,0:T(8,128)(2,1)} %bitcast.13), calls=%async_computation.1 | async-start | bytes 786432 | tf_op jit(solution)/shard_map/all_to_all | solution.py:376
  99.6 0.3 multiply_bitcast_fusion.gs_ref
  99.8 3.4 %collective-permute-start.9 = (bf16[128,384]{1,0:T(8,128)(2,1)S(1)}, bf16[128,384]{1,0:T(8,128)(2,1)S(1)}, u32[]{:S(2)}, u32[]{:S(2)}) collective-permute-start(bf16[128,384]{1,0:T(8,128)(2,1)S(1)} %get-tuple-element.45.hidden_ref), channel_id=1, source_target_pairs={{0,8},{8,0},{1,9},{9,1},{2,10},{10,2},{3,11},{11,3},{4,12},{12,4},... | collective-permute-start | bytes 294920 | tf_op jit(solution)/shard_map/ppermute | solution.py:374
  103.3 7.5 %all-to-all-done.1 = bf16[8,16,1536]{2,1,0:T(8,128)(2,1)S(1)} async-done(((bf16[8,16,1536]{2,1,0:T(8,128)(2,1)}), bf16[8,16,1536]{2,1,0:T(8,128)(2,1)S(1)}, u32[]{:S(2)}, u32[]{:S(2)}) %all-to-all-start.1) | async-done | bytes 393248 | tf_op jit(solution)/shard_map/all_to_all | solution.py:376
  110.8 0.1 convert_reduce_fusion.1
  110.9 0.2 multiply_reduce_fusion
  111.1 0.1 divide_convert_fusion
  111.2 24.4 %all_gather.11.grad_ref = bf16[256,1664]{1,0:T(8,128)(2,1)S(1)} all-gather(bf16[16,1664]{1,0:T(8,128)(2,1)S(1)} %pad_maximum_fusion.3), channel_id=1, replica_groups=mesh['x'=4,'z'=8,'ylo'=2,'yhi'=4,'core'=2] {'ylo','yhi','core'}, dimensions={0}, use_global_device_ids=true | all-gather | bytes 905216 | tf_op jit(solution)/shard_map/all_gather | solution.py:384
  135.6 0.3 broadcast_in_dim.87.gain_ref
  135.9 1.7 %shard_map.150 = (bf16[784,128]{1,0:T(8,128)(2,1)S(1)}, f32[4,192,128]{2,1,0:T(8,128)S(1)}, f32[8,128]{1,0:T(8,128)S(1)}) custom-call(s32[3]{0:T(128)S(1)} %pad_add_fusion.where_ref, bf16[2,128,1664]{2,1,0:T(8,128)(2,1)S(1)} %bitcast.49, bf16[384,1536]{1,0:T(8,128)(2,1)S(1)} %copy-done.1, f32[128,384]{1,0:T(8,128)S(1)} %get-tuple-element.86.pre_ref, ...), custom_call_target="tpu_custom_call" | custom-call | flops 301989888 | bytes 4000000 | tf_op jit(solution)/shard_map/pallas_call | solution.py:154
  137.6 1.7 shard_map.152
  139.3 9.6 %all-to-all-start.2 = ((bf16[32,80,128]{2,1,0:T(8,128)(2,1)}), bf16[32,80,128]{2,1,0:T(8,128)(2,1)S(1)}, u32[]{:S(2)}, u32[]{:S(2)}) async-start(bf16[32,80,128]{2,1,0:T(8,128)(2,1)} %shard_map.152), calls=%async_computation.2 | async-start | bytes 1310720 | tf_op jit(solution)/shard_map/all_to_all | solution.py:393
  148.9 0.1 dynamic_slice.40
  149.0 2.3 %collective-permute-start.5 = (bf16[784,128]{1,0:T(8,128)(2,1)S(1)}, bf16[784,128]{1,0:T(8,128)(2,1)S(1)}, u32[]{:S(2)}, u32[]{:S(2)}) collective-permute-start(bf16[784,128]{1,0:T(8,128)(2,1)S(1)} %get-tuple-element.38), channel_id=1, source_target_pairs={{0,1},{1,0},{2,3},{3,2},{4,5},{5,4},{6,7},{7,6},{8,9},{9,8},{10,11... | collective-permute-start | bytes 602120 | tf_op jit(solution)/shard_map/ppermute | solution.py:394
  151.4 1.0 collective-permute-done.5.got_ref
  152.4 0.6 shard_map.151
  153.0 4.5 %collective-permute-start.6 = (bf16[208,128]{1,0:T(8,128)(2,1)S(1)}, bf16[208,128]{1,0:T(8,128)(2,1)S(1)}, u32[]{:S(2)}, u32[]{:S(2)}) collective-permute-start(bf16[208,128]{1,0:T(8,128)(2,1)S(1)} %get-tuple-element.41), channel_id=1, source_target_pairs={{0,2},{2,4},{4,6},{6,0},{1,3},{3,5},{5,7},{7,1},{8,10},{10,12},{12... | collective-permute-start | bytes 159752 | tf_op jit(solution)/shard_map/ppermute | solution.py:396
  157.5 4.0 %collective-permute-start.7 = (bf16[208,128]{1,0:T(8,128)(2,1)S(1)}, bf16[208,128]{1,0:T(8,128)(2,1)S(1)}, u32[]{:S(2)}, u32[]{:S(2)}) collective-permute-start(bf16[208,128]{1,0:T(8,128)(2,1)S(1)} %get-tuple-element.42), channel_id=1, source_target_pairs={{0,4},{2,6},{4,0},{6,2},{1,5},{3,7},{5,1},{7,3},{8,12},{10,14},{12... | collective-permute-start | bytes 159752 | tf_op jit(solution)/shard_map/ppermute | solution.py:396
  161.4 3.3 %collective-permute-start.8 = (bf16[208,128]{1,0:T(8,128)(2,1)S(1)}, bf16[208,128]{1,0:T(8,128)(2,1)S(1)}, u32[]{:S(2)}, u32[]{:S(2)}) collective-permute-start(bf16[208,128]{1,0:T(8,128)(2,1)S(1)} %get-tuple-element.43), channel_id=1, source_target_pairs={{0,6},{2,0},{4,2},{6,4},{1,7},{3,1},{5,3},{7,5},{8,14},{10,8},{12,... | collective-permute-start | bytes 159752 | tf_op jit(solution)/shard_map/ppermute | solution.py:396
  164.7 0.1 broadcast_multiply_fusion.invgain_ref
  164.8 0.1 dynamic_slice.41.grad_ref
  164.9 1.6 collective-permute-done.7.two_ref
  166.6 1.4 collective-permute-done.8.three_ref
  168.0 0.7 shard_map.153
  168.7 0.7 copy.48
  169.4 0.7 copy.49
  (47 shorter events, 0.2 us)
Async XLA Ops:
  23.7 1.8 %copy-start.4 = (bf16[256,1536]{0,1:T(8,128)(2,1)}, bf16[256,1536]{0,1:T(8,128)(2,1)S(1)}, u32[]{:S(2)}) copy-start(bf16[256,1536]{0,1:T(8,128)(2,1)S(1)} %all_gather.9) | copy-start | bytes 2359300
  23.9 1.0 copy-start.10
  23.9 1.0 copy-start.11
  23.9 1.3 copy-start.9
  23.9 1.6 copy-start.2
  23.9 1.6 copy-start.8
  23.9 1.5 copy-start.12
  24.0 1.5 copy-start.13
  25.5 1.3 copy-start
  29.2 55.4 %all-to-all-start = ((bf16[32,16,1664]{2,1,0:T(8,128)(2,1)}), bf16[32,16,1664]{2,1,0:T(8,128)(2,1)S(1)}, u32[]{:S(2)}, u32[]{:S(2)}) async-start(bf16[32,16,1664]{2,1,0:T(8,128)(2,1)} %broadcast_in_dim.86), calls=%async_computation | async-start | bytes 3407872 | tf_op jit(solution)/shard_map/all_to_all | solution.py:46
  40.2 4.4 %collective-permute-start = (bf16[4,16,1536]{2,1,0:T(8,128)(2,1)}, bf16[4,16,1536]{2,1,0:T(8,128)(2,1)S(1)}, u32[]{:S(2)}, u32[]{:S(2)}) collective-permute-start(bf16[4,16,1536]{2,1,0:T(8,128)(2,1)} %fusion.13), channel_id=1, source_target_pairs={{0,1},{1,0},{2,3},{3,2},{4,5},{5,4},{6,7},{7,6},{8,9},{9,8},{10,11... | collective-permute-start | bytes 589832 | tf_op jit(solution)/shard_map/ppermute | solution.py:343
  46.4 12.8 %collective-permute-start.1 = (bf16[16,1536]{1,0:T(8,128)(2,1)S(1)}, bf16[16,1536]{1,0:T(8,128)(2,1)S(1)}, u32[]{:S(2)}, u32[]{:S(2)}) collective-permute-start(bf16[16,1536]{1,0:T(8,128)(2,1)S(1)} %get-tuple-element.73), channel_id=1, source_target_pairs={{0,2},{2,4},{4,6},{6,0},{1,3},{3,5},{5,7},{7,1},{8,10},{10,12},{12... | collective-permute-start | bytes 147464 | tf_op jit(solution)/shard_map/ppermute | solution.py:352
  48.3 10.9 %collective-permute-start.2 = (bf16[16,1536]{1,0:T(8,128)(2,1)S(1)}, bf16[16,1536]{1,0:T(8,128)(2,1)S(1)}, u32[]{:S(2)}, u32[]{:S(2)}) collective-permute-start(bf16[16,1536]{1,0:T(8,128)(2,1)S(1)} %get-tuple-element.75), channel_id=1, source_target_pairs={{0,4},{2,6},{4,0},{6,2},{1,5},{3,7},{5,1},{7,3},{8,12},{10,14},{12... | collective-permute-start | bytes 147464 | tf_op jit(solution)/shard_map/ppermute | solution.py:352
  53.6 7.6 %collective-permute-start.3 = (bf16[16,1536]{1,0:T(8,128)(2,1)S(1)}, bf16[16,1536]{1,0:T(8,128)(2,1)S(1)}, u32[]{:S(2)}, u32[]{:S(2)}) collective-permute-start(bf16[16,1536]{1,0:T(8,128)(2,1)S(1)} %get-tuple-element.74), channel_id=1, source_target_pairs={{0,6},{2,0},{4,2},{6,4},{1,7},{3,1},{5,3},{7,5},{8,14},{10,8},{12,... | collective-permute-start | bytes 147464 | tf_op jit(solution)/shard_map/ppermute | solution.py:352
  84.6 3.8 %copy-start.5 = (bf16[256,1536]{0,1:T(8,128)(2,1)S(1)}, bf16[256,1536]{0,1:T(8,128)(2,1)}, u32[]{:S(2)}) copy-start(bf16[256,1536]{0,1:T(8,128)(2,1)} %copy-done.4) | copy-start | bytes 2359300
  86.4 3.6 %collective-permute-start.4 = (bf16[128,1536]{1,0:T(8,128)(2,1)S(1)}, bf16[128,1536]{1,0:T(8,128)(2,1)S(1)}, u32[]{:S(2)}, u32[]{:S(2)}) collective-permute-start(bf16[128,1536]{1,0:T(8,128)(2,1)S(1)} %get-tuple-element.28), channel_id=1, source_target_pairs={{0,1},{1,0},{2,3},{3,2},{4,5},{5,4},{6,7},{7,6},{8,9},{9,8},{10,11... | collective-permute-start | bytes 1179656 | tf_op jit(solution)/shard_map/ppermute | solution.py:368
  92.5 7.1 %copy-start.6 = (f32[128,1536]{0,1:T(8,128)S(1)}, f32[128,1536]{0,1:T(8,128)}, u32[]{:S(2)}) copy-start(f32[128,1536]{0,1:T(8,128)} %fusion) | copy-start | bytes 2359300
  92.5 18.3 %all-to-all-start.1 = ((bf16[8,16,1536]{2,1,0:T(8,128)(2,1)}), bf16[8,16,1536]{2,1,0:T(8,128)(2,1)S(1)}, u32[]{:S(2)}, u32[]{:S(2)}) async-start(bf16[8,16,1536]{2,1,0:T(8,128)(2,1)} %bitcast.13), calls=%async_computation.1 | async-start | bytes 786432 | tf_op jit(solution)/shard_map/all_to_all | solution.py:376
  99.8 37.8 %collective-permute-start.9 = (bf16[128,384]{1,0:T(8,128)(2,1)S(1)}, bf16[128,384]{1,0:T(8,128)(2,1)S(1)}, u32[]{:S(2)}, u32[]{:S(2)}) collective-permute-start(bf16[128,384]{1,0:T(8,128)(2,1)S(1)} %get-tuple-element.45.hidden_ref), channel_id=1, source_target_pairs={{0,8},{8,0},{1,9},{9,1},{2,10},{10,2},{3,11},{11,3},{4,12},{12,4},... | collective-permute-start | bytes 294920 | tf_op jit(solution)/shard_map/ppermute | solution.py:374
  110.8 25.0 %copy-start.3 = (bf16[1536,384]{1,0:T(8,128)(2,1)S(1)}, bf16[1536,384]{1,0:T(8,128)(2,1)}, u32[]{:S(2)}) copy-start(bf16[1536,384]{1,0:T(8,128)(2,1)} %up_ref.1) | copy-start | bytes 3538948
  110.8 25.0 %copy-start.1 = (bf16[384,1536]{1,0:T(8,128)(2,1)S(1)}, bf16[384,1536]{1,0:T(8,128)(2,1)}, u32[]{:S(2)}) copy-start(bf16[384,1536]{1,0:T(8,128)(2,1)} %down_ref.1) | copy-start | bytes 3538948
  137.6 13.7 %copy-start.7 = (bf16[128,192]{0,1:T(8,128)(2,1)S(1)}, bf16[128,192]{0,1:T(8,128)(2,1)}, u32[]{:S(2)}) copy-start(bf16[128,192]{0,1:T(8,128)(2,1)} %param.13) | copy-start | bytes 147460
  139.3 28.7 %all-to-all-start.2 = ((bf16[32,80,128]{2,1,0:T(8,128)(2,1)}), bf16[32,80,128]{2,1,0:T(8,128)(2,1)S(1)}, u32[]{:S(2)}, u32[]{:S(2)}) async-start(bf16[32,80,128]{2,1,0:T(8,128)(2,1)} %shard_map.152), calls=%async_computation.2 | async-start | bytes 1310720 | tf_op jit(solution)/shard_map/all_to_all | solution.py:393
  149.0 3.4 %collective-permute-start.5 = (bf16[784,128]{1,0:T(8,128)(2,1)S(1)}, bf16[784,128]{1,0:T(8,128)(2,1)S(1)}, u32[]{:S(2)}, u32[]{:S(2)}) collective-permute-start(bf16[784,128]{1,0:T(8,128)(2,1)S(1)} %get-tuple-element.38), channel_id=1, source_target_pairs={{0,1},{1,0},{2,3},{3,2},{4,5},{5,4},{6,7},{7,6},{8,9},{9,8},{10,11... | collective-permute-start | bytes 602120 | tf_op jit(solution)/shard_map/ppermute | solution.py:394
  153.0 11.9 %collective-permute-start.6 = (bf16[208,128]{1,0:T(8,128)(2,1)S(1)}, bf16[208,128]{1,0:T(8,128)(2,1)S(1)}, u32[]{:S(2)}, u32[]{:S(2)}) collective-permute-start(bf16[208,128]{1,0:T(8,128)(2,1)S(1)} %get-tuple-element.41), channel_id=1, source_target_pairs={{0,2},{2,4},{4,6},{6,0},{1,3},{3,5},{5,7},{7,1},{8,10},{10,12},{12... | collective-permute-start | bytes 159752 | tf_op jit(solution)/shard_map/ppermute | solution.py:396
  157.5 9.1 %collective-permute-start.7 = (bf16[208,128]{1,0:T(8,128)(2,1)S(1)}, bf16[208,128]{1,0:T(8,128)(2,1)S(1)}, u32[]{:S(2)}, u32[]{:S(2)}) collective-permute-start(bf16[208,128]{1,0:T(8,128)(2,1)S(1)} %get-tuple-element.42), channel_id=1, source_target_pairs={{0,4},{2,6},{4,0},{6,2},{1,5},{3,7},{5,1},{7,3},{8,12},{10,14},{12... | collective-permute-start | bytes 159752 | tf_op jit(solution)/shard_map/ppermute | solution.py:396
  161.4 6.5 %collective-permute-start.8 = (bf16[208,128]{1,0:T(8,128)(2,1)S(1)}, bf16[208,128]{1,0:T(8,128)(2,1)S(1)}, u32[]{:S(2)}, u32[]{:S(2)}) collective-permute-start(bf16[208,128]{1,0:T(8,128)(2,1)S(1)} %get-tuple-element.43), channel_id=1, source_target_pairs={{0,6},{2,0},{4,2},{6,4},{1,7},{3,1},{5,3},{7,5},{8,14},{10,8},{12,... | collective-permute-start | bytes 159752 | tf_op jit(solution)/shard_map/ppermute | solution.py:396

commit v5 on v4

--- a/solution.py
+++ b/solution.py
@@ -39,13 +39,6 @@
         parts.append(part.astype(jnp.bfloat16))
         values = values - part
     return jnp.stack(parts)
-
-
-def spread(block, axis, count):
-    send = jnp.broadcast_to(block[None], (count,) + block.shape)
-    return lax.all_to_all(send, axis, split_axis=0, concat_axis=0, tiled=True).reshape(
-        count * block.shape[0], block.shape[1]
-    )
 
 
 VMEM = pl.BlockSpec(memory_space=pltpu.VMEM)
@@ -80,13 +73,14 @@
         pick.astype(jnp.bfloat16), txt_ref[:, WIDE:], across, preferred_element_type=jnp.float32
     )[:1]
     img_ids = jnp.sum(img[:, WIDE:].astype(jnp.float32) * pick[:1], axis=1, keepdims=True)
-    logits = scalar_ref[0] * scores + scalar_ref[1]
+    temper = scalar_ref[:, 0:1]
+    logits = temper * scores + scalar_ref[:, 1:2]
     positive = img_ids == txt_ids
     margin = jnp.where(positive, -logits, logits)
     shrunk = jnp.exp(-jnp.abs(margin))
     losses = jnp.maximum(margin, 0.0) + jnp.log1p(shrunk)
     sigmoid = jnp.where(margin >= 0.0, 1.0, shrunk) / (1.0 + shrunk)
-    scale = scalar_ref[2]
+    scale = temper * (scalar_ref[:, 2:3] / BATCH)
     weights = (jnp.where(positive, -scale, scale) * sigmoid).astype(jnp.bfloat16)
     part = jnp.dot(weights, txt, preferred_element_type=jnp.float32)
     if len(refs) == 3:
@@ -100,7 +94,7 @@
     return call(
         pair_kernel,
         [((ROWS, WIDE), jnp.bfloat16), ((8, 128), jnp.float32)],
-        2,
+        1,
         4 * ROWS * 512 * WIDE,
         3000000,
         which.reshape(1).astype(jnp.int32),
@@ -197,6 +191,61 @@
     )(where, own_blocks, own_sums, got)
 
 
+def fore_kernel(where_ref, part_ref, got_ref, one_ref, two_ref, three_ref, keep_ref):
+    core = where_ref[1]
+    yhi = where_ref[2]
+
+    def chip(at):
+        return part_ref[at, core] + got_ref[at].astype(jnp.float32)
+
+    for step, ref in enumerate((one_ref, two_ref, three_ref), 1):
+        ref[...] = chip(lax.rem(yhi + step, 4)).astype(jnp.bfloat16)
+    keep_ref[...] = chip(yhi)
+
+
+def fore_chip(where, part, got):
+    return call(
+        fore_kernel,
+        [((IMG, WIDE), jnp.bfloat16)] * 3 + [((IMG, WIDE), jnp.float32)],
+        1,
+        1000000,
+        1500000,
+        where,
+        part,
+        got,
+    )
+
+
+def img_kernel(keep_ref, one_ref, two_ref, three_ref, own_ref, ids_ref, send_ref, unit_ref, norm_ref):
+    summed = keep_ref[...] + own_ref[...]
+    for ref in (one_ref, two_ref, three_ref):
+        summed = summed + ref[...].astype(jnp.float32)
+    norm = jnp.sqrt(jnp.sum(summed * summed, axis=1, keepdims=True) + 1e-06)
+    unit = summed / norm
+    unit_ref[...] = unit
+    norm_ref[...] = norm
+    send_ref[:, :WIDE] = unit.astype(jnp.bfloat16)
+    send_ref[:, WIDE:] = ids_ref[...]
+
+
+def img_rows(keep, gots, own, ids):
+    return call(
+        img_kernel,
+        [
+            ((IMG, WIDE + EXTRA), jnp.bfloat16),
+            ((IMG, WIDE), jnp.float32),
+            ((IMG, 1), jnp.float32),
+        ],
+        0,
+        200000,
+        500000,
+        keep,
+        *gots,
+        own,
+        ids,
+    )
+
+
 def last_kernel(
     keep_ref, all_ref, one_ref, two_ref, three_ref, inv_ref, invgain_ref, invscaled_ref, grad_ref, got_ref, out_ref, down_ref, loss_ref
 ):
@@ -213,10 +262,10 @@
         - inv_ref[:1] * (sum_h / WIDE)
         - invscaled_ref[...] * (sum_hs / WIDE)
     )
-    out_ref[...] = (grad_ref[...].astype(jnp.float32) + side.T).astype(jnp.bfloat16)
+    out_ref[...] = (grad_ref[...].astype(jnp.float32) + side).astype(jnp.bfloat16)
     summed = jnp.sum(got_ref[...].astype(jnp.float32), axis=0)
     for piece in range(3):
-        down_ref[piece * 128 : (piece + 1) * 128] = summed[piece * 24 : (piece + 1) * 24].T
+        down_ref[:, piece * 128 : (piece + 1) * 128] = summed[piece * 24 : (piece + 1) * 24]
     tail = jnp.sum(summed[72:], axis=1, keepdims=True)
     loss_ref[...] = jnp.sum(tail, axis=0, keepdims=True) / BATCH
 
@@ -225,8 +274,8 @@
     return call(
         last_kernel,
         [
-            ((ROWS, SLICE), jnp.bfloat16),
-            ((384, 24), jnp.float32),
+            ((SLICE, ROWS), jnp.bfloat16),
+            ((24, 384), jnp.float32),
             ((1, 1), jnp.float32),
         ],
         0,
@@ -317,11 +366,13 @@
     both = lax.all_gather(
         jnp.concatenate([pooled, text_embed], axis=0), TENS, axis=1, tiled=True
     )
-    txt_rows = lax.dynamic_slice_in_dim(both, ROWS + row0, IMG, 0).astype(jnp.float32)
+    rows = lax.dynamic_slice_in_dim(
+        both.reshape(2, ROWS, WIDE), row0, IMG, 1
+    ).astype(jnp.float32)
+    own, txt_rows = rows[0], rows[1]
     txt_norm = jnp.sqrt(jnp.sum(txt_rows * txt_rows, axis=1, keepdims=True) + 1e-06)
     txt_low = (txt_rows / txt_norm).astype(jnp.bfloat16)
     txt_send = jnp.concatenate([txt_low, id_columns(text_ids, row0)], axis=1)
-
     wide = both[:ROWS].astype(jnp.float32)
     average = jnp.mean(wide, axis=1, keepdims=True)
     centered = wide - average
@@ -339,31 +390,22 @@
     part = part.reshape(4, 2, IMG, WIDE)
     part_other = lax.dynamic_index_in_dim(part, 1 - core, 1, keepdims=False).astype(jnp.bfloat16)
     part_other, txt_send = lax.optimization_barrier((part_other, txt_send))
-    txt_all = spread(txt_send, ("x", "z"), 32)
     core_got = lax.ppermute(
         part_other,
         "core",
         [(0, 1), (1, 0)],
     )
-    chip = lax.dynamic_index_in_dim(part, core, 1, keepdims=False) + core_got.astype(jnp.float32)
-    mixed = lax.dynamic_index_in_dim(chip, yhi, 0, keepdims=False)
-    for step in range(1, 4):
-        block = lax.dynamic_index_in_dim(chip, (yhi + step) % 4, 0, keepdims=False)
-        got = lax.ppermute(block.astype(jnp.bfloat16), "yhi", turn(step))
-        mixed = mixed + got.astype(jnp.float32)
-    own = lax.dynamic_slice_in_dim(both, row0, IMG, 0).astype(jnp.float32)
-    summed = own + mixed
-    img_norm = jnp.sqrt(jnp.sum(summed * summed, axis=1, keepdims=True) + 1e-06)
-    img_unit = summed / img_norm
-    img_send = jnp.concatenate(
-        [img_unit.astype(jnp.bfloat16), id_columns(image_ids, row0)], axis=1
-    )
+    txt_copies = jnp.broadcast_to(txt_send[None], (32, IMG, WIDE + EXTRA))
+    txt_all = lax.all_to_all(
+        txt_copies, ("x", "z"), split_axis=0, concat_axis=0, tiled=True
+    ).reshape(4 * ROWS, WIDE + EXTRA)
+    where = jnp.stack([lax.axis_index("ylo"), core, yhi]).astype(jnp.int32)
+    sends = fore_chip(where, part, core_got)
+    gots = [lax.ppermute(sends[step - 1], "yhi", turn(step)) for step in range(1, 4)]
+    img_send, img_unit, img_norm = img_rows(sends[3], gots, own, id_columns(image_ids, row0))
     img_all = lax.all_gather(img_send, RING, axis=0, tiled=True)
 
-    temper = logit_scale[0]
-    offset = logit_bias[0]
-    factor = loss_scale[0] / BATCH
-    scalars = jnp.stack([temper, offset, temper * factor])
+    scalars = jnp.concatenate([logit_scale, logit_bias, loss_scale]).reshape(1, 3)
     other_part, other_loss = pair_rows(1 - core, scalars, img_all, txt_all)
     from_other = lax.ppermute(other_part, "core", [(0, 1), (1, 0)])
     chip_part, own_loss = pair_rows(core, scalars, img_all, txt_all, from_other)
@@ -381,10 +423,9 @@
     grad_low = ((grad_unit - img_unit * tangent) / img_norm).astype(jnp.bfloat16)
     loss_part = jnp.sum(other_loss + own_loss, axis=0)
     loss_block = jnp.pad(pieces(loss_part, 3), ((0, IMG - 3), (0, 0)))
-    grad_all = lax.all_gather(
-        jnp.concatenate([grad_low, loss_block], axis=1), RING, axis=0, tiled=True
-    )
-    where = jnp.stack([ylo, core, yhi]).astype(jnp.int32)
+    grad_send = jnp.concatenate([grad_low, loss_block], axis=1)
+    grad_send, hidden_other = lax.optimization_barrier((grad_send, hidden_other))
+    grad_all = lax.all_gather(grad_send, RING, axis=0, tiled=True)
     send, own_blocks, own_sums = back_rows(
         where, grad_all, w_down, preact, w_up, gain_t, gs_t
     )
@@ -400,9 +441,9 @@
     grad_own = lax.dynamic_slice(grad_all, (ylo * ROWS, col0), (ROWS, SLICE))
     grad_pooled, grad_down, loss = last_rows(
         sends[3], sends[4], gots, inverse_t, inverse_t[:1] * gain_own[:, None],
-        inverse_t[:1] * scaled_own, grad_own, down_got,
-    )
-    return (loss.reshape(1), grad_pooled, grad_down)
+        inverse_t[:1] * scaled_own, grad_own.T, down_got,
+    )
+    return (loss.reshape(1), grad_pooled.T, grad_down.T)
 
 
 def solution(mesh):

time: 172 us -> 169 us (0.983)
  local copies, waits for them, and re-layouts: 6.12 us -> 3.46 us
  other arithmetic: 5.64 us -> 3.76 us
    ppermute x3 -> x6, starting transfers between devices: 11.7 us -> 25.2 us  [shards(): lax.ppermute(sends[step - 1], 'yhi', turn(step))]
    ppermute x3 -> x0, starting transfers between devices: 12.6 us -> none  [shards(): got = lax.ppermute(block.astype(jnp.bfloat16), 'yhi', turn(step))]
    ppermute x3 -> x6, waiting for transfers between devices: 3.02 us -> 5.05 us  [shards(): lax.ppermute(sends[step - 1], 'yhi', turn(step))]
    ppermute x3 -> x0, waiting for transfers between devices: 1.89 us -> none  [shards(): got = lax.ppermute(block.astype(jnp.bfloat16), 'yhi', turn(step))]
    pallas_call x3 -> x5, Pallas kernels: 4.98 us -> 5.45 us  [call(): pl.pallas_call(kernel, out_shape=[jax.ShapeDtypeStruct(shape, kind) for s...]
  transfers between devices with their start and end apart: 13 -> 13, of which waited for: 6 -> 7; matrix products, arithmetic and copies ran while one was open for 3% -> 1% of each run, Pallas kernels for 1% -> 1%
where the time goes in v5:
time: 169 us; the launch traced here: 168 us
  blocking collectives  68.2 us (40%)
  starting transfers between devices  63.3 us (37%)
  waiting for transfers between devices  15.1 us (9%)
  Pallas kernels  9.46 us (6%)
  other arithmetic  3.76 us (2%)
  local copies, waits for them, and re-layouts  3.46 us (2%)
  between operations  3 us (2%)
    ppermute x6, starting transfers between devices, shards(): lax.ppermute(sends[step - 1], 'yhi', turn(step))  25.2 us
    all_gather x1, blocking collectives, shards(): grad_all = lax.all_gather(grad_send, RING, axis=0, tiled=True)  23.4 us
    all_gather x1, blocking collectives, shards(): img_all = lax.all_gather(img_send, RING, axis=0, tiled=True)  22.7 us
    all_gather x1, blocking collectives, shards(): lax.all_gather(jnp.concatenate([pooled, text_embed], axis=0), TENS, axis=...  22.2 us
    all_to_all x1, starting transfers between devices, shards(): lax.all_to_all(txt_copies, ('x', 'z'), split_axis=0, concat_axis=0, tiled...  11 us
    all_to_all x1, starting transfers between devices, shards(): lax.all_to_all(down_send, ('x', 'z'), split_axis=0, concat_axis=0, tiled=...  9.92 us
    all_to_all x1, waiting for transfers between devices, shards(): lax.all_to_all(chip_part, ('ylo', 'yhi'), split_axis=0, concat_axis=0, ti...  7.53 us
    all_to_all x1, starting transfers between devices, shards(): lax.all_to_all(chip_part, ('ylo', 'yhi'), split_axis=0, concat_axis=0, ti...  6.67 us
  transfers between devices with their start and end apart: 13, of which 7 were waited for; matrix products, arithmetic and copies ran while one was open for 1% of the time, Pallas kernels for 1%

profile of v5, /device:TPU:1, one launch (start us, length us, event | category | flops | bytes accessed | tf_op | source)
XLA Modules:
  0.0 167.7 jit_solution(8154345354516896884)
XLA Ops:
  0.6 0.8 pad_maximum_fusion
  1.5 22.2 %all_gather.9 = bf16[256,1536]{0,1:T(8,128)(2,1)S(1)} all-gather(bf16[256,192]{0,1:T(8,128)(2,1)S(1)} %pad_maximum_fusion), channel_id=1, replica_groups=mesh['x'=4,'z'=8,'ylo'=2,'yhi'=4,'core'=2] {'yhi','core'}, dimensions={1}, use_global_device_ids=true | all-gather | bytes 884736 | tf_op jit(solution)/shard_map/all_gather | solution.py:366
  23.7 0.0 copy-start.2
  23.7 0.0 copy-start.8
  23.7 0.0 copy-start.12
  23.7 0.0 copy-start.13
  23.7 0.3 copy.40
  24.0 0.2 convert_reduce_fusion
  24.3 0.1 multiply_reduce_fusion.1
  24.4 0.1 divide_convert_fusion.1
  24.5 0.2 fusion.2
  24.7 0.2 convert_reduce_fusion.2
  24.9 0.1 select_convert_fusion
  25.0 0.3 dynamic_update_slice.5
  25.3 0.0 copy-start
  25.4 1.0 fusion.12
  26.4 0.3 copy-done
  26.6 0.4 convolution_add_fusion
  27.0 0.7 fusion.13
  27.7 1.3 broadcast_in_dim.85
  29.0 11.0 %all-to-all-start = ((bf16[32,16,1664]{2,1,0:T(8,128)(2,1)}), bf16[32,16,1664]{2,1,0:T(8,128)(2,1)S(1)}, u32[]{:S(2)}, u32[]{:S(2)}) async-start(bf16[32,16,1664]{2,1,0:T(8,128)(2,1)} %broadcast_in_dim.85), calls=%async_computation | async-start | bytes 3407872 | tf_op jit(solution)/shard_map/all_to_all | solution.py:399
  40.0 2.3 %collective-permute-start = (bf16[4,16,1536]{2,1,0:T(8,128)(2,1)}, bf16[4,16,1536]{2,1,0:T(8,128)(2,1)S(1)}, u32[]{:S(2)}, u32[]{:S(2)}) collective-permute-start(bf16[4,16,1536]{2,1,0:T(8,128)(2,1)} %fusion.13), channel_id=1, source_target_pairs={{0,1},{1,0},{2,3},{3,2},{4,5},{5,4},{6,7},{7,6},{8,9},{9,8},{10,11... | collective-permute-start | bytes 589832 | tf_op jit(solution)/shard_map/ppermute | solution.py:393
  44.3 0.1 pad_add_fusion.where_ref
  44.4 0.6 shard_map.148
  45.0 1.9 %collective-permute-start.1 = (bf16[16,1536]{1,0:T(8,128)(2,1)S(1)}, bf16[16,1536]{1,0:T(8,128)(2,1)S(1)}, u32[]{:S(2)}, u32[]{:S(2)}) collective-permute-start(bf16[16,1536]{1,0:T(8,128)(2,1)S(1)} %get-tuple-element.37), channel_id=1, source_target_pairs={{0,2},{2,4},{4,6},{6,0},{1,3},{3,5},{5,7},{7,1},{8,10},{10,12},{12... | collective-permute-start | bytes 147464 | tf_op jit(solution)/shard_map/ppermute | solution.py:404
  46.9 5.2 %collective-permute-start.2 = (bf16[16,1536]{1,0:T(8,128)(2,1)S(1)}, bf16[16,1536]{1,0:T(8,128)(2,1)S(1)}, u32[]{:S(2)}, u32[]{:S(2)}) collective-permute-start(bf16[16,1536]{1,0:T(8,128)(2,1)S(1)} %get-tuple-element.38), channel_id=1, source_target_pairs={{0,4},{2,6},{4,0},{6,2},{1,5},{3,7},{5,1},{7,3},{8,12},{10,14},{12... | collective-permute-start | bytes 147464 | tf_op jit(solution)/shard_map/ppermute | solution.py:404
  52.1 5.5 %collective-permute-start.3 = (bf16[16,1536]{1,0:T(8,128)(2,1)S(1)}, bf16[16,1536]{1,0:T(8,128)(2,1)S(1)}, u32[]{:S(2)}, u32[]{:S(2)}) collective-permute-start(bf16[16,1536]{1,0:T(8,128)(2,1)S(1)} %get-tuple-element.39), channel_id=1, source_target_pairs={{0,6},{2,0},{4,2},{6,4},{1,7},{3,1},{5,3},{7,5},{8,14},{10,8},{12,... | collective-permute-start | bytes 147464 | tf_op jit(solution)/shard_map/ppermute | solution.py:404
  57.6 0.1 maximum_bitcast_fusion.scalar_ref
  57.7 2.0 %collective-permute-done.3.three_ref = bf16[16,1536]{1,0:T(8,128)(2,1)S(1)} collective-permute-done((bf16[16,1536]{1,0:T(8,128)(2,1)S(1)}, bf16[16,1536]{1,0:T(8,128)(2,1)S(1)}, u32[]{:S(2)}, u32[]{:S(2)}) %collective-permute-start.3) | collective-permute-done | bytes 49184 | tf_op jit(solution)/shard_map/ppermute | solution.py:404
  59.7 0.1 shard_map.149
  59.8 22.7 %all_gather.10 = bf16[256,1664]{1,0:T(8,128)(2,1)S(1)} all-gather(bf16[16,1664]{1,0:T(8,128)(2,1)S(1)} %get-tuple-element.40), channel_id=1, replica_groups=mesh['x'=4,'z'=8,'ylo'=2,'yhi'=4,'core'=2] {'ylo','yhi','core'}, dimensions={0}, use_global_device_ids=true | all-gather | bytes 905216 | tf_op jit(solution)/shard_map/all_gather | solution.py:406
  82.5 2.0 %shard_map.150 = (bf16[128,1536]{1,0:T(8,128)(2,1)}, f32[8,128]{1,0:T(8,128)S(1)}) custom-call(s32[1]{0:T(128)} %bitcast.11.which_ref, f32[1,3]{1,0:T(1,128)S(1)} %maximum_bitcast_fusion.scalar_ref, bf16[8,2,16,1664]{3,2,1,0:T(8,128)(2,1)S(1)} %bitcast.47, bf16[512,1664]{1,0:T(8,128)(2,1)S(1)} %bitcast.44), custom_call_target="tpu_custom_call" | custom-call | flops 402653184 | bytes 3000000 | tf_op jit(solution)/shard_map/pallas_call | solution.py:49
  84.5 2.3 %collective-permute-start.4 = (bf16[128,1536]{1,0:T(8,128)(2,1)}, bf16[128,1536]{1,0:T(8,128)(2,1)S(1)}, u32[]{:S(2)}, u32[]{:S(2)}) collective-permute-start(bf16[128,1536]{1,0:T(8,128)(2,1)} %get-tuple-element.42), channel_id=1, source_target_pairs={{0,1},{1,0},{2,3},{3,2},{4,5},{5,4},{6,7},{7,6},{8,9},{9,8},{10,11... | collective-permute-start | bytes 1179656 | tf_op jit(solution)/shard_map/ppermute | solution.py:410
  86.8 1.0 fusion
  87.8 0.1 reduce
  87.9 0.4 collective-permute-done.4.refs_0_
  88.3 2.0 %shard_map.151 = (bf16[128,1536]{1,0:T(8,128)(2,1)}, f32[8,128]{1,0:T(8,128)S(1)}) custom-call(s32[1]{0:T(128)} %bitcast.1.which_ref, f32[1,3]{1,0:T(1,128)S(1)} %maximum_bitcast_fusion.scalar_ref, bf16[8,2,16,1664]{3,2,1,0:T(8,128)(2,1)S(1)} %bitcast.48, bf16[512,1664]{1,0:T(8,128)(2,1)S(1)} %bitcast.45, bf16[128,1536]{1,0:T(8,128)(2,1)S(1)} %collective-permute-done.4.refs_0_), custom_call_target="tpu_custom_call" | custom-call | flops 402653184 | bytes 3000000 | tf_op jit(solution)/shard_map/pallas_call | solution.py:49
  90.3 6.7 %all-to-all-start.1 = ((bf16[8,16,1536]{2,1,0:T(8,128)(2,1)}), bf16[8,16,1536]{2,1,0:T(8,128)(2,1)S(1)}, u32[]{:S(2)}, u32[]{:S(2)}) async-start(bf16[8,16,1536]{2,1,0:T(8,128)(2,1)} %bitcast.12), calls=%async_computation.1 | async-start | bytes 786432 | tf_op jit(solution)/shard_map/all_to_all | solution.py:418
  97.0 0.3 multiply_bitcast_fusion.gs_ref
  97.3 3.4 %collective-permute-start.5 = (bf16[128,384]{1,0:T(8,128)(2,1)S(1)}, bf16[128,384]{1,0:T(8,128)(2,1)S(1)}, u32[]{:S(2)}, u32[]{:S(2)}) collective-permute-start(bf16[128,384]{1,0:T(8,128)(2,1)S(1)} %get-tuple-element.50.hidden_ref), channel_id=1, source_target_pairs={{0,8},{8,0},{1,9},{9,1},{2,10},{10,2},{3,11},{11,3},{4,12},{12,4},... | collective-permute-start | bytes 294920 | tf_op jit(solution)/shard_map/ppermute | solution.py:416
  100.7 7.5 %all-to-all-done.1 = bf16[8,16,1536]{2,1,0:T(8,128)(2,1)S(1)} async-done(((bf16[8,16,1536]{2,1,0:T(8,128)(2,1)}), bf16[8,16,1536]{2,1,0:T(8,128)(2,1)S(1)}, u32[]{:S(2)}, u32[]{:S(2)}) %all-to-all-start.1) | async-done | bytes 393248 | tf_op jit(solution)/shard_map/all_to_all | solution.py:418
  108.2 0.1 convert_reduce_fusion.1
  108.3 0.0 copy-start.1
  108.3 0.1 multiply_reduce_fusion
  108.4 0.1 divide_convert_fusion
  108.5 1.0 collective-permute-done.5.other_ref
  109.6 23.4 %all_gather.11.grad_ref = bf16[256,1664]{1,0:T(8,128)(2,1)S(1)} all-gather(bf16[16,1664]{1,0:T(8,128)(2,1)S(1)} %pad_maximum_fusion.2), channel_id=1, replica_groups=mesh['x'=4,'z'=8,'ylo'=2,'yhi'=4,'core'=2] {'ylo','yhi','core'}, dimensions={0}, use_global_device_ids=true | all-gather | bytes 905216 | tf_op jit(solution)/shard_map/all_gather | solution.py:428
  133.0 0.3 broadcast_in_dim.86.gain_ref
  133.2 1.7 %shard_map.152 = (bf16[784,128]{1,0:T(8,128)(2,1)S(1)}, f32[4,192,128]{2,1,0:T(8,128)S(1)}, f32[8,128]{1,0:T(8,128)S(1)}) custom-call(s32[3]{0:T(128)S(1)} %pad_add_fusion.where_ref, bf16[2,128,1664]{2,1,0:T(8,128)(2,1)S(1)} %bitcast.46, bf16[384,1536]{1,0:T(8,128)(2,1)S(1)} %copy-done.1, f32[128,384]{1,0:T(8,128)S(1)} %get-tuple-element.79.pre_ref, ...), custom_call_target="tpu_custom_call" | custom-call | flops 301989888 | bytes 4000000 | tf_op jit(solution)/shard_map/pallas_call | solution.py:148
  135.0 1.7 %shard_map.154 = bf16[32,80,128]{2,1,0:T(8,128)(2,1)} custom-call(s32[1]{0:T(128)} %bitcast.ylo_ref, bf16[256,1664]{1,0:T(8,128)(2,1)S(1)} %all_gather.11.grad_ref, bf16[128,384]{1,0:T(8,128)(2,1)S(1)} %get-tuple-element.50.hidden_ref, bf16[128,384]{1,0:T(8,128)(2,1)S(1)} %collective-permute-done.5.other_ref), custom_call_target="tpu_custom_call" | custom-call | flops 301989888 | bytes 1700000 | tf_op jit(solution)/shard_map/pallas_call | solution.py:326
  136.7 9.9 %all-to-all-start.2 = ((bf16[32,80,128]{2,1,0:T(8,128)(2,1)}), bf16[32,80,128]{2,1,0:T(8,128)(2,1)S(1)}, u32[]{:S(2)}, u32[]{:S(2)}) async-start(bf16[32,80,128]{2,1,0:T(8,128)(2,1)} %shard_map.154), calls=%async_computation.2 | async-start | bytes 1310720 | tf_op jit(solution)/shard_map/all_to_all | solution.py:434
  146.6 0.1 dynamic_slice.15
  146.7 2.5 %collective-permute-start.6 = (bf16[784,128]{1,0:T(8,128)(2,1)S(1)}, bf16[784,128]{1,0:T(8,128)(2,1)S(1)}, u32[]{:S(2)}, u32[]{:S(2)}) collective-permute-start(bf16[784,128]{1,0:T(8,128)(2,1)S(1)} %get-tuple-element.56), channel_id=1, source_target_pairs={{0,1},{1,0},{2,3},{3,2},{4,5},{5,4},{6,7},{7,6},{8,9},{9,8},{10,11... | collective-permute-start | bytes 602120 | tf_op jit(solution)/shard_map/ppermute | solution.py:435
  149.3 1.0 collective-permute-done.6.got_ref
  150.3 0.6 shard_map.153
  150.9 5.5 %collective-permute-start.7 = (bf16[208,128]{1,0:T(8,128)(2,1)S(1)}, bf16[208,128]{1,0:T(8,128)(2,1)S(1)}, u32[]{:S(2)}, u32[]{:S(2)}) collective-permute-start(bf16[208,128]{1,0:T(8,128)(2,1)S(1)} %get-tuple-element.59), channel_id=1, source_target_pairs={{0,2},{2,4},{4,6},{6,0},{1,3},{3,5},{5,7},{7,1},{8,10},{10,12},{12... | collective-permute-start | bytes 159752 | tf_op jit(solution)/shard_map/ppermute | solution.py:437
  156.4 2.3 %collective-permute-start.8 = (bf16[208,128]{1,0:T(8,128)(2,1)S(1)}, bf16[208,128]{1,0:T(8,128)(2,1)S(1)}, u32[]{:S(2)}, u32[]{:S(2)}) collective-permute-start(bf16[208,128]{1,0:T(8,128)(2,1)S(1)} %get-tuple-element.60), channel_id=1, source_target_pairs={{0,4},{2,6},{4,0},{6,2},{1,5},{3,7},{5,1},{7,3},{8,12},{10,14},{12... | collective-permute-start | bytes 159752 | tf_op jit(solution)/shard_map/ppermute | solution.py:437
  158.8 4.8 %collective-permute-start.9 = (bf16[208,128]{1,0:T(8,128)(2,1)S(1)}, bf16[208,128]{1,0:T(8,128)(2,1)S(1)}, u32[]{:S(2)}, u32[]{:S(2)}) collective-permute-start(bf16[208,128]{1,0:T(8,128)(2,1)S(1)} %get-tuple-element.61), channel_id=1, source_target_pairs={{0,6},{2,0},{4,2},{6,4},{1,7},{3,1},{5,3},{7,5},{8,14},{10,8},{12,... | collective-permute-start | bytes 159752 | tf_op jit(solution)/shard_map/ppermute | solution.py:437
  163.5 0.1 broadcast_multiply_fusion.invgain_ref
  163.6 0.1 dynamic_slice.16
  163.7 0.1 copy.42
  163.9 1.9 %collective-permute-done.8.two_ref = bf16[208,128]{1,0:T(8,128)(2,1)S(1)} collective-permute-done((bf16[208,128]{1,0:T(8,128)(2,1)S(1)}, bf16[208,128]{1,0:T(8,128)(2,1)S(1)}, u32[]{:S(2)}, u32[]{:S(2)}) %collective-permute-start.8) | collective-permute-done | bytes 53280 | tf_op jit(solution)/shard_map/ppermute | solution.py:437
  165.7 1.1 collective-permute-done.9.three_ref
  166.9 0.8 shard_map.155
  (43 shorter events, 0.2 us)
Async XLA Ops:
  23.7 1.7 copy-start.4
  23.7 1.1 copy-start.10
  23.7 1.1 copy-start.11
  23.7 1.4 copy-start.9
  23.7 1.7 copy-start.2
  23.7 1.7 copy-start.8
  23.7 1.6 copy-start.12
  23.7 1.6 copy-start.13
  25.3 1.3 copy-start
  29.0 53.5 %all-to-all-start = ((bf16[32,16,1664]{2,1,0:T(8,128)(2,1)}), bf16[32,16,1664]{2,1,0:T(8,128)(2,1)S(1)}, u32[]{:S(2)}, u32[]{:S(2)}) async-start(bf16[32,16,1664]{2,1,0:T(8,128)(2,1)} %broadcast_in_dim.85), calls=%async_computation | async-start | bytes 3407872 | tf_op jit(solution)/shard_map/all_to_all | solution.py:399
  40.0 4.4 %collective-permute-start = (bf16[4,16,1536]{2,1,0:T(8,128)(2,1)}, bf16[4,16,1536]{2,1,0:T(8,128)(2,1)S(1)}, u32[]{:S(2)}, u32[]{:S(2)}) collective-permute-start(bf16[4,16,1536]{2,1,0:T(8,128)(2,1)} %fusion.13), channel_id=1, source_target_pairs={{0,1},{1,0},{2,3},{3,2},{4,5},{5,4},{6,7},{7,6},{8,9},{9,8},{10,11... | collective-permute-start | bytes 589832 | tf_op jit(solution)/shard_map/ppermute | solution.py:393
  45.0 12.7 %collective-permute-start.1 = (bf16[16,1536]{1,0:T(8,128)(2,1)S(1)}, bf16[16,1536]{1,0:T(8,128)(2,1)S(1)}, u32[]{:S(2)}, u32[]{:S(2)}) collective-permute-start(bf16[16,1536]{1,0:T(8,128)(2,1)S(1)} %get-tuple-element.37), channel_id=1, source_target_pairs={{0,2},{2,4},{4,6},{6,0},{1,3},{3,5},{5,7},{7,1},{8,10},{10,12},{12... | collective-permute-start | bytes 147464 | tf_op jit(solution)/shard_map/ppermute | solution.py:404
  46.9 10.8 %collective-permute-start.2 = (bf16[16,1536]{1,0:T(8,128)(2,1)S(1)}, bf16[16,1536]{1,0:T(8,128)(2,1)S(1)}, u32[]{:S(2)}, u32[]{:S(2)}) collective-permute-start(bf16[16,1536]{1,0:T(8,128)(2,1)S(1)} %get-tuple-element.38), channel_id=1, source_target_pairs={{0,4},{2,6},{4,0},{6,2},{1,5},{3,7},{5,1},{7,3},{8,12},{10,14},{12... | collective-permute-start | bytes 147464 | tf_op jit(solution)/shard_map/ppermute | solution.py:404
  52.1 7.6 %collective-permute-start.3 = (bf16[16,1536]{1,0:T(8,128)(2,1)S(1)}, bf16[16,1536]{1,0:T(8,128)(2,1)S(1)}, u32[]{:S(2)}, u32[]{:S(2)}) collective-permute-start(bf16[16,1536]{1,0:T(8,128)(2,1)S(1)} %get-tuple-element.39), channel_id=1, source_target_pairs={{0,6},{2,0},{4,2},{6,4},{1,7},{3,1},{5,3},{7,5},{8,14},{10,8},{12,... | collective-permute-start | bytes 147464 | tf_op jit(solution)/shard_map/ppermute | solution.py:404
  82.5 4.3 %copy-start.5 = (bf16[256,1536]{0,1:T(8,128)(2,1)S(1)}, bf16[256,1536]{0,1:T(8,128)(2,1)}, u32[]{:S(2)}) copy-start(bf16[256,1536]{0,1:T(8,128)(2,1)} %copy-done.4) | copy-start | bytes 2359300
  84.5 3.8 %collective-permute-start.4 = (bf16[128,1536]{1,0:T(8,128)(2,1)}, bf16[128,1536]{1,0:T(8,128)(2,1)S(1)}, u32[]{:S(2)}, u32[]{:S(2)}) collective-permute-start(bf16[128,1536]{1,0:T(8,128)(2,1)} %get-tuple-element.42), channel_id=1, source_target_pairs={{0,1},{1,0},{2,3},{3,2},{4,5},{5,4},{6,7},{7,6},{8,9},{9,8},{10,11... | collective-permute-start | bytes 1179656 | tf_op jit(solution)/shard_map/ppermute | solution.py:410
  90.3 6.7 %copy-start.6 = (f32[128,1536]{0,1:T(8,128)S(1)}, f32[128,1536]{0,1:T(8,128)}, u32[]{:S(2)}) copy-start(f32[128,1536]{0,1:T(8,128)} %fusion) | copy-start | bytes 2359300
  90.3 17.9 %all-to-all-start.1 = ((bf16[8,16,1536]{2,1,0:T(8,128)(2,1)}), bf16[8,16,1536]{2,1,0:T(8,128)(2,1)S(1)}, u32[]{:S(2)}, u32[]{:S(2)}) async-start(bf16[8,16,1536]{2,1,0:T(8,128)(2,1)} %bitcast.12), calls=%async_computation.1 | async-start | bytes 786432 | tf_op jit(solution)/shard_map/all_to_all | solution.py:418
  97.3 12.3 %collective-permute-start.5 = (bf16[128,384]{1,0:T(8,128)(2,1)S(1)}, bf16[128,384]{1,0:T(8,128)(2,1)S(1)}, u32[]{:S(2)}, u32[]{:S(2)}) collective-permute-start(bf16[128,384]{1,0:T(8,128)(2,1)S(1)} %get-tuple-element.50.hidden_ref), channel_id=1, source_target_pairs={{0,8},{8,0},{1,9},{9,1},{2,10},{10,2},{3,11},{11,3},{4,12},{12,4},... | collective-permute-start | bytes 294920 | tf_op jit(solution)/shard_map/ppermute | solution.py:416
  108.2 25.0 %copy-start.3 = (bf16[1536,384]{1,0:T(8,128)(2,1)S(1)}, bf16[1536,384]{1,0:T(8,128)(2,1)}, u32[]{:S(2)}) copy-start(bf16[1536,384]{1,0:T(8,128)(2,1)} %up_ref.1) | copy-start | bytes 3538948
  108.3 24.9 %copy-start.1 = (bf16[384,1536]{1,0:T(8,128)(2,1)S(1)}, bf16[384,1536]{1,0:T(8,128)(2,1)}, u32[]{:S(2)}) copy-start(bf16[384,1536]{1,0:T(8,128)(2,1)} %down_ref.1) | copy-start | bytes 3538948
  135.0 14.2 %copy-start.7 = (bf16[128,192]{0,1:T(8,128)(2,1)S(1)}, bf16[128,192]{0,1:T(8,128)(2,1)}, u32[]{:S(2)}) copy-start(bf16[128,192]{0,1:T(8,128)(2,1)} %param.13) | copy-start | bytes 147460
  136.7 30.2 %all-to-all-start.2 = ((bf16[32,80,128]{2,1,0:T(8,128)(2,1)}), bf16[32,80,128]{2,1,0:T(8,128)(2,1)S(1)}, u32[]{:S(2)}, u32[]{:S(2)}) async-start(bf16[32,80,128]{2,1,0:T(8,128)(2,1)} %shard_map.154), calls=%async_computation.2 | async-start | bytes 1310720 | tf_op jit(solution)/shard_map/all_to_all | solution.py:434
  146.7 3.6 %collective-permute-start.6 = (bf16[784,128]{1,0:T(8,128)(2,1)S(1)}, bf16[784,128]{1,0:T(8,128)(2,1)S(1)}, u32[]{:S(2)}, u32[]{:S(2)}) collective-permute-start(bf16[784,128]{1,0:T(8,128)(2,1)S(1)} %get-tuple-element.56), channel_id=1, source_target_pairs={{0,1},{1,0},{2,3},{3,2},{4,5},{5,4},{6,7},{7,6},{8,9},{9,8},{10,11... | collective-permute-start | bytes 602120 | tf_op jit(solution)/shard_map/ppermute | solution.py:435
  150.9 13.0 %collective-permute-start.7 = (bf16[208,128]{1,0:T(8,128)(2,1)S(1)}, bf16[208,128]{1,0:T(8,128)(2,1)S(1)}, u32[]{:S(2)}, u32[]{:S(2)}) collective-permute-start(bf16[208,128]{1,0:T(8,128)(2,1)S(1)} %get-tuple-element.59), channel_id=1, source_target_pairs={{0,2},{2,4},{4,6},{6,0},{1,3},{3,5},{5,7},{7,1},{8,10},{10,12},{12... | collective-permute-start | bytes 159752 | tf_op jit(solution)/shard_map/ppermute | solution.py:437
  156.4 9.3 %collective-permute-start.8 = (bf16[208,128]{1,0:T(8,128)(2,1)S(1)}, bf16[208,128]{1,0:T(8,128)(2,1)S(1)}, u32[]{:S(2)}, u32[]{:S(2)}) collective-permute-start(bf16[208,128]{1,0:T(8,128)(2,1)S(1)} %get-tuple-element.60), channel_id=1, source_target_pairs={{0,4},{2,6},{4,0},{6,2},{1,5},{3,7},{5,1},{7,3},{8,12},{10,14},{12... | collective-permute-start | bytes 159752 | tf_op jit(solution)/shard_map/ppermute | solution.py:437
  158.8 8.1 %collective-permute-start.9 = (bf16[208,128]{1,0:T(8,128)(2,1)S(1)}, bf16[208,128]{1,0:T(8,128)(2,1)S(1)}, u32[]{:S(2)}, u32[]{:S(2)}) collective-permute-start(bf16[208,128]{1,0:T(8,128)(2,1)S(1)} %get-tuple-element.61), channel_id=1, source_target_pairs={{0,6},{2,0},{4,2},{6,4},{1,7},{3,1},{5,3},{7,5},{8,14},{10,8},{12,... | collective-permute-start | bytes 159752 | tf_op jit(solution)/shard_map/ppermute | solution.py:437

commit v6 on v5

--- a/solution.py
+++ b/solution.py
@@ -61,7 +61,7 @@
     return first, values - first
 
 
-def pair_kernel(which_ref, scalar_ref, img_ref, txt_ref, *refs):
+def pair_kernel(which_ref, temper_ref, offset_ref, factor_ref, img_ref, txt_ref, *refs):
     out_ref, loss_ref = refs[-2:]
     img = img_ref[:, which_ref[0]].reshape(ROWS, WIDE + EXTRA)
     txt = txt_ref[:, :WIDE]
@@ -73,14 +73,14 @@
         pick.astype(jnp.bfloat16), txt_ref[:, WIDE:], across, preferred_element_type=jnp.float32
     )[:1]
     img_ids = jnp.sum(img[:, WIDE:].astype(jnp.float32) * pick[:1], axis=1, keepdims=True)
-    temper = scalar_ref[:, 0:1]
-    logits = temper * scores + scalar_ref[:, 1:2]
+    temper = temper_ref[0]
+    logits = temper * scores + offset_ref[0]
     positive = img_ids == txt_ids
     margin = jnp.where(positive, -logits, logits)
     shrunk = jnp.exp(-jnp.abs(margin))
     losses = jnp.maximum(margin, 0.0) + jnp.log1p(shrunk)
     sigmoid = jnp.where(margin >= 0.0, 1.0, shrunk) / (1.0 + shrunk)
-    scale = temper * (scalar_ref[:, 2:3] / BATCH)
+    scale = temper * (factor_ref[0] / BATCH)
     weights = (jnp.where(positive, -scale, scale) * sigmoid).astype(jnp.bfloat16)
     part = jnp.dot(weights, txt, preferred_element_type=jnp.float32)
     if len(refs) == 3:
@@ -94,11 +94,11 @@
     return call(
         pair_kernel,
         [((ROWS, WIDE), jnp.bfloat16), ((8, 128), jnp.float32)],
-        1,
+        4,
         4 * ROWS * 512 * WIDE,
         3000000,
         which.reshape(1).astype(jnp.int32),
-        scalars,
+        *scalars,
         img_all.reshape(8, 2, IMG, WIDE + EXTRA),
         txt_all,
         *added,
@@ -405,7 +405,7 @@
     img_send, img_unit, img_norm = img_rows(sends[3], gots, own, id_columns(image_ids, row0))
     img_all = lax.all_gather(img_send, RING, axis=0, tiled=True)
 
-    scalars = jnp.concatenate([logit_scale, logit_bias, loss_scale]).reshape(1, 3)
+    scalars = (logit_scale, logit_bias, loss_scale)
     other_part, other_loss = pair_rows(1 - core, scalars, img_all, txt_all)
     from_other = lax.ppermute(other_part, "core", [(0, 1), (1, 0)])
     chip_part, own_loss = pair_rows(core, scalars, img_all, txt_all, from_other)

time: 169 us -> 166 us (0.982)
    ppermute x6, waiting for transfers between devices: 5.05 us -> 3.07 us  [shards(): lax.ppermute(sends[step - 1], 'yhi', turn(step))]
where the time goes in v6:
time: 166 us; the launch traced here: 165 us
  blocking collectives  68.2 us (41%)
  starting transfers between devices  62.6 us (38%)
  waiting for transfers between devices  14 us (8%)
  Pallas kernels  9.42 us (6%)
  other arithmetic  3.67 us (2%)
  between operations  3.05 us (2%)
  local copies, waits for them, and re-layouts  2.82 us (2%)
    ppermute x6, starting transfers between devices, shards(): lax.ppermute(sends[step - 1], 'yhi', turn(step))  25.2 us
    all_gather x1, blocking collectives, shards(): grad_all = lax.all_gather(grad_send, RING, axis=0, tiled=True)  23.4 us
    all_gather x1, blocking collectives, shards(): img_all = lax.all_gather(img_send, RING, axis=0, tiled=True)  22.6 us
    all_gather x1, blocking collectives, shards(): lax.all_gather(jnp.concatenate([pooled, text_embed], axis=0), TENS, axis=...  22.2 us
    all_to_all x1, starting transfers between devices, shards(): lax.all_to_all(txt_copies, ('x', 'z'), split_axis=0, concat_axis=0, tiled...  11 us
    all_to_all x1, starting transfers between devices, shards(): lax.all_to_all(down_send, ('x', 'z'), split_axis=0, concat_axis=0, tiled=...  9.49 us
    all_to_all x1, waiting for transfers between devices, shards(): lax.all_to_all(chip_part, ('ylo', 'yhi'), split_axis=0, concat_axis=0, ti...  7.53 us
    pallas_call x5, Pallas kernels, call(): pl.pallas_call(kernel, out_shape=[jax.ShapeDtypeStruct(shape, kind) for s...  5.42 us
  transfers between devices with their start and end apart: 13, of which 7 were waited for; matrix products, arithmetic and copies ran while one was open for 1% of the time, Pallas kernels for 1%

profile of v6, /device:TPU:1, one launch (start us, length us, event | category | flops | bytes accessed | tf_op | source)
XLA Modules:
  0.0 165.2 jit_solution(12979582754531033431)
XLA Ops:
  0.6 0.8 pad_maximum_fusion
  1.5 22.2 %all_gather.9 = bf16[256,1536]{0,1:T(8,128)(2,1)S(1)} all-gather(bf16[256,192]{0,1:T(8,128)(2,1)S(1)} %pad_maximum_fusion), channel_id=1, replica_groups=mesh['x'=4,'z'=8,'ylo'=2,'yhi'=4,'core'=2] {'yhi','core'}, dimensions={1}, use_global_device_ids=true | all-gather | bytes 884736 | tf_op jit(solution)/shard_map/all_gather | solution.py:366
  23.7 0.0 copy-start.2
  23.7 0.0 copy-start.8
  23.7 0.0 copy-start.14
  23.7 0.0 copy-start.15
  23.7 0.3 copy.40
  24.0 0.2 convert_reduce_fusion
  24.3 0.1 multiply_reduce_fusion.1
  24.4 0.1 divide_convert_fusion.1
  24.5 0.2 fusion.2
  24.7 0.2 convert_reduce_fusion.2
  24.9 0.1 select_convert_fusion
  25.0 0.3 dynamic_update_slice.5
  25.4 0.0 copy-start
  25.4 1.0 fusion.12
  26.4 0.3 copy-done
  26.6 0.4 convolution_add_fusion
  27.0 1.3 broadcast_in_dim.85
  28.4 11.0 %all-to-all-start = ((bf16[32,16,1664]{2,1,0:T(8,128)(2,1)}), bf16[32,16,1664]{2,1,0:T(8,128)(2,1)S(1)}, u32[]{:S(2)}, u32[]{:S(2)}) async-start(bf16[32,16,1664]{2,1,0:T(8,128)(2,1)} %broadcast_in_dim.85), calls=%async_computation | async-start | bytes 3407872 | tf_op jit(solution)/shard_map/all_to_all | solution.py:399
  39.4 2.4 %collective-permute-start = (bf16[4,16,1536]{2,1,0:T(8,128)(2,1)S(1)}, bf16[4,16,1536]{2,1,0:T(8,128)(2,1)S(1)}, u32[]{:S(2)}, u32[]{:S(2)}) collective-permute-start(bf16[4,16,1536]{2,1,0:T(8,128)(2,1)S(1)} %fusion.13), channel_id=1, source_target_pairs={{0,1},{1,0},{2,3},{3,2},{4,5},{5,4},{6,7},{7,6},{8,9},{9,8},{10,11... | collective-permute-start | bytes 589832 | tf_op jit(solution)/shard_map/ppermute | solution.py:393
  41.7 0.1 pad_add_fusion.where_ref
  41.8 1.0 collective-permute-done.got_ref
  42.8 0.6 shard_map.148
  43.4 1.9 %collective-permute-start.1 = (bf16[16,1536]{1,0:T(8,128)(2,1)S(1)}, bf16[16,1536]{1,0:T(8,128)(2,1)S(1)}, u32[]{:S(2)}, u32[]{:S(2)}) collective-permute-start(bf16[16,1536]{1,0:T(8,128)(2,1)S(1)} %get-tuple-element.37), channel_id=1, source_target_pairs={{0,2},{2,4},{4,6},{6,0},{1,3},{3,5},{5,7},{7,1},{8,10},{10,12},{12... | collective-permute-start | bytes 147464 | tf_op jit(solution)/shard_map/ppermute | solution.py:404
  45.3 5.2 %collective-permute-start.2 = (bf16[16,1536]{1,0:T(8,128)(2,1)S(1)}, bf16[16,1536]{1,0:T(8,128)(2,1)S(1)}, u32[]{:S(2)}, u32[]{:S(2)}) collective-permute-start(bf16[16,1536]{1,0:T(8,128)(2,1)S(1)} %get-tuple-element.38), channel_id=1, source_target_pairs={{0,4},{2,6},{4,0},{6,2},{1,5},{3,7},{5,1},{7,3},{8,12},{10,14},{12... | collective-permute-start | bytes 147464 | tf_op jit(solution)/shard_map/ppermute | solution.py:404
  50.5 5.5 %collective-permute-start.3 = (bf16[16,1536]{1,0:T(8,128)(2,1)S(1)}, bf16[16,1536]{1,0:T(8,128)(2,1)S(1)}, u32[]{:S(2)}, u32[]{:S(2)}) collective-permute-start(bf16[16,1536]{1,0:T(8,128)(2,1)S(1)} %get-tuple-element.39), channel_id=1, source_target_pairs={{0,6},{2,0},{4,2},{6,4},{1,7},{3,1},{5,3},{7,5},{8,14},{10,8},{12,... | collective-permute-start | bytes 147464 | tf_op jit(solution)/shard_map/ppermute | solution.py:404
  57.9 0.0 collective-permute-done.1.one_ref
  58.0 0.1 shard_map.149
  58.1 22.6 %all_gather.10 = bf16[256,1664]{1,0:T(8,128)(2,1)S(1)} all-gather(bf16[16,1664]{1,0:T(8,128)(2,1)S(1)} %get-tuple-element.40), channel_id=1, replica_groups=mesh['x'=4,'z'=8,'ylo'=2,'yhi'=4,'core'=2] {'ylo','yhi','core'}, dimensions={0}, use_global_device_ids=true | all-gather | bytes 905216 | tf_op jit(solution)/shard_map/all_gather | solution.py:406
  80.7 2.0 %shard_map.150 = (bf16[128,1536]{1,0:T(8,128)(2,1)}, f32[8,128]{1,0:T(8,128)S(1)}) custom-call(s32[1]{0:T(128)} %bitcast.10.which_ref, f32[1]{0:T(128)S(6)} %copy.44.temper_ref, f32[1]{0:T(128)S(6)} %copy.45.offset_ref, f32[1]{0:T(128)S(6)} %copy.46.factor_ref, bf16[8,2,16,1664]{3,2,1,0:T(8,128)(2,1)S(1)} %bitcast.45, bf16[512,1664]{1,0:T(8,128)(2,1)S(1)} %bitcast.42), custom_call_target="tpu_custom_call" | custom-call | flops 402653184 | bytes 3000000 | tf_op jit(solution)/shard_map/pallas_call | solution.py:49
  82.7 3.5 %collective-permute-start.4 = (bf16[128,1536]{1,0:T(8,128)(2,1)}, bf16[128,1536]{1,0:T(8,128)(2,1)S(1)}, u32[]{:S(2)}, u32[]{:S(2)}) collective-permute-start(bf16[128,1536]{1,0:T(8,128)(2,1)} %get-tuple-element.42), channel_id=1, source_target_pairs={{0,1},{1,0},{2,3},{3,2},{4,5},{5,4},{6,7},{7,6},{8,9},{9,8},{10,11... | collective-permute-start | bytes 1179656 | tf_op jit(solution)/shard_map/ppermute | solution.py:410
  86.2 1.0 fusion
  87.2 0.1 reduce
  87.3 0.4 collective-permute-done.4.refs_0_
  87.7 2.0 %shard_map.151 = (bf16[128,1536]{1,0:T(8,128)(2,1)}, f32[8,128]{1,0:T(8,128)S(1)}) custom-call(s32[1]{0:T(128)} %bitcast.1.which_ref, f32[1]{0:T(128)S(6)} %copy.44.temper_ref, f32[1]{0:T(128)S(6)} %copy.45.offset_ref, f32[1]{0:T(128)S(6)} %copy.46.factor_ref, bf16[8,2,16,1664]{3,2,1,0:T(8,128)(2,1)S(1)} %bitcast.46, bf16[512,1664]{1,0:T(8,128)(2,1)S(1)} %bitcast.43, ...), custom_call_target="tpu_custom_call" | custom-call | flops 402653184 | bytes 3000000 | tf_op jit(solution)/shard_map/pallas_call | solution.py:49
  89.7 5.2 %all-to-all-start.1 = ((bf16[8,16,1536]{2,1,0:T(8,128)(2,1)}), bf16[8,16,1536]{2,1,0:T(8,128)(2,1)S(1)}, u32[]{:S(2)}, u32[]{:S(2)}) async-start(bf16[8,16,1536]{2,1,0:T(8,128)(2,1)} %bitcast.11), calls=%async_computation.1 | async-start | bytes 786432 | tf_op jit(solution)/shard_map/all_to_all | solution.py:418
  94.9 0.3 multiply_bitcast_fusion.gs_ref
  95.2 3.4 %collective-permute-start.5 = (bf16[128,384]{1,0:T(8,128)(2,1)S(1)}, bf16[128,384]{1,0:T(8,128)(2,1)S(1)}, u32[]{:S(2)}, u32[]{:S(2)}) collective-permute-start(bf16[128,384]{1,0:T(8,128)(2,1)S(1)} %get-tuple-element.50.hidden_ref), channel_id=1, source_target_pairs={{0,8},{8,0},{1,9},{9,1},{2,10},{10,2},{3,11},{11,3},{4,12},{12,4},... | collective-permute-start | bytes 294920 | tf_op jit(solution)/shard_map/ppermute | solution.py:416
  98.6 7.5 %all-to-all-done.1 = bf16[8,16,1536]{2,1,0:T(8,128)(2,1)S(1)} async-done(((bf16[8,16,1536]{2,1,0:T(8,128)(2,1)}), bf16[8,16,1536]{2,1,0:T(8,128)(2,1)S(1)}, u32[]{:S(2)}, u32[]{:S(2)}) %all-to-all-start.1) | async-done | bytes 393248 | tf_op jit(solution)/shard_map/all_to_all | solution.py:418
  106.2 0.1 convert_reduce_fusion.1
  106.2 0.0 copy-start.1
  106.2 0.1 multiply_reduce_fusion
  106.4 0.1 divide_convert_fusion
  106.5 1.0 collective-permute-done.5.other_ref
  107.5 23.4 %all_gather.11.grad_ref = bf16[256,1664]{1,0:T(8,128)(2,1)S(1)} all-gather(bf16[16,1664]{1,0:T(8,128)(2,1)S(1)} %pad_maximum_fusion.2), channel_id=1, replica_groups=mesh['x'=4,'z'=8,'ylo'=2,'yhi'=4,'core'=2] {'ylo','yhi','core'}, dimensions={0}, use_global_device_ids=true | all-gather | bytes 905216 | tf_op jit(solution)/shard_map/all_gather | solution.py:428
  130.9 0.3 broadcast_in_dim.86.gain_ref
  131.2 1.7 %shard_map.152 = (bf16[784,128]{1,0:T(8,128)(2,1)S(1)}, f32[4,192,128]{2,1,0:T(8,128)S(1)}, f32[8,128]{1,0:T(8,128)S(1)}) custom-call(s32[3]{0:T(128)S(1)} %pad_add_fusion.where_ref, bf16[2,128,1664]{2,1,0:T(8,128)(2,1)S(1)} %bitcast.44, bf16[384,1536]{1,0:T(8,128)(2,1)S(1)} %copy-done.1, f32[128,384]{1,0:T(8,128)S(1)} %get-tuple-element.79.pre_ref, ...), custom_call_target="tpu_custom_call" | custom-call | flops 301989888 | bytes 4000000 | tf_op jit(solution)/shard_map/pallas_call | solution.py:148
  132.9 0.0 copy-start.7
  132.9 1.7 %shard_map.154 = bf16[32,80,128]{2,1,0:T(8,128)(2,1)} custom-call(s32[1]{0:T(128)} %bitcast.ylo_ref, bf16[256,1664]{1,0:T(8,128)(2,1)S(1)} %all_gather.11.grad_ref, bf16[128,384]{1,0:T(8,128)(2,1)S(1)} %get-tuple-element.50.hidden_ref, bf16[128,384]{1,0:T(8,128)(2,1)S(1)} %collective-permute-done.5.other_ref), custom_call_target="tpu_custom_call" | custom-call | flops 301989888 | bytes 1700000 | tf_op jit(solution)/shard_map/pallas_call | solution.py:326
  134.6 9.5 %all-to-all-start.2 = ((bf16[32,80,128]{2,1,0:T(8,128)(2,1)}), bf16[32,80,128]{2,1,0:T(8,128)(2,1)S(1)}, u32[]{:S(2)}, u32[]{:S(2)}) async-start(bf16[32,80,128]{2,1,0:T(8,128)(2,1)} %shard_map.154), calls=%async_computation.2 | async-start | bytes 1310720 | tf_op jit(solution)/shard_map/all_to_all | solution.py:434
  144.1 0.1 dynamic_slice.15
  144.2 2.5 %collective-permute-start.6 = (bf16[784,128]{1,0:T(8,128)(2,1)S(1)}, bf16[784,128]{1,0:T(8,128)(2,1)S(1)}, u32[]{:S(2)}, u32[]{:S(2)}) collective-permute-start(bf16[784,128]{1,0:T(8,128)(2,1)S(1)} %get-tuple-element.56), channel_id=1, source_target_pairs={{0,1},{1,0},{2,3},{3,2},{4,5},{5,4},{6,7},{7,6},{8,9},{9,8},{10,11... | collective-permute-start | bytes 602120 | tf_op jit(solution)/shard_map/ppermute | solution.py:435
  146.7 1.0 collective-permute-done.6.got_ref
  147.8 0.6 shard_map.153
  148.4 5.5 %collective-permute-start.7 = (bf16[208,128]{1,0:T(8,128)(2,1)S(1)}, bf16[208,128]{1,0:T(8,128)(2,1)S(1)}, u32[]{:S(2)}, u32[]{:S(2)}) collective-permute-start(bf16[208,128]{1,0:T(8,128)(2,1)S(1)} %get-tuple-element.59), channel_id=1, source_target_pairs={{0,2},{2,4},{4,6},{6,0},{1,3},{3,5},{5,7},{7,1},{8,10},{10,12},{12... | collective-permute-start | bytes 159752 | tf_op jit(solution)/shard_map/ppermute | solution.py:437
  153.9 2.3 %collective-permute-start.8 = (bf16[208,128]{1,0:T(8,128)(2,1)S(1)}, bf16[208,128]{1,0:T(8,128)(2,1)S(1)}, u32[]{:S(2)}, u32[]{:S(2)}) collective-permute-start(bf16[208,128]{1,0:T(8,128)(2,1)S(1)} %get-tuple-element.60), channel_id=1, source_target_pairs={{0,4},{2,6},{4,0},{6,2},{1,5},{3,7},{5,1},{7,3},{8,12},{10,14},{12... | collective-permute-start | bytes 159752 | tf_op jit(solution)/shard_map/ppermute | solution.py:437
  156.2 4.8 %collective-permute-start.9 = (bf16[208,128]{1,0:T(8,128)(2,1)S(1)}, bf16[208,128]{1,0:T(8,128)(2,1)S(1)}, u32[]{:S(2)}, u32[]{:S(2)}) collective-permute-start(bf16[208,128]{1,0:T(8,128)(2,1)S(1)} %get-tuple-element.61), channel_id=1, source_target_pairs={{0,6},{2,0},{4,2},{6,4},{1,7},{3,1},{5,3},{7,5},{8,14},{10,8},{12,... | collective-permute-start | bytes 159752 | tf_op jit(solution)/shard_map/ppermute | solution.py:437
  161.0 0.1 broadcast_multiply_fusion.invgain_ref
  161.1 0.1 dynamic_slice.16
  161.2 0.1 copy.42
  161.4 1.9 %collective-permute-done.8.two_ref = bf16[208,128]{1,0:T(8,128)(2,1)S(1)} collective-permute-done((bf16[208,128]{1,0:T(8,128)(2,1)S(1)}, bf16[208,128]{1,0:T(8,128)(2,1)S(1)}, u32[]{:S(2)}, u32[]{:S(2)}) %collective-permute-start.8) | collective-permute-done | bytes 53280 | tf_op jit(solution)/shard_map/ppermute | solution.py:437
  163.2 1.2 collective-permute-done.9.three_ref
  164.4 0.8 shard_map.155
  (46 shorter events, 0.2 us)
Async XLA Ops:
  23.7 1.7 %copy-start.4 = (bf16[256,1536]{0,1:T(8,128)(2,1)}, bf16[256,1536]{0,1:T(8,128)(2,1)S(1)}, u32[]{:S(2)}) copy-start(bf16[256,1536]{0,1:T(8,128)(2,1)S(1)} %all_gather.9) | copy-start | bytes 2359300
  23.7 1.1 copy-start.12
  23.7 1.1 copy-start.13
  23.7 1.4 copy-start.11
  23.7 1.7 %copy-start.2 = (bf16[1536,384]{1,0:T(8,128)(2,1)S(1)}, bf16[1536,384]{1,0:T(8,128)(2,1)}, u32[]{:S(2)}) copy-start(bf16[1536,384]{1,0:T(8,128)(2,1)} %up_ref.1) | copy-start | bytes 3538948
  23.7 1.7 %copy-start.8 = (f32[1536]{0:T(1024)S(1)}, f32[1536]{0:T(1024)}, u32[]{:S(2)}) copy-start(f32[1536]{0:T(1024)} %param.14) | copy-start | bytes 18436
  23.7 1.7 copy-start.14
  23.7 1.6 copy-start.15
  24.5 1.9 %copy-start.9 = (f32[128]{0:T(128)}, f32[128]{0:T(128)S(1)}, u32[]{:S(2)}) copy-start(f32[128]{0:T(128)S(1)} %broadcast_multiply_fusion.1) | copy-start | bytes 1540
  25.4 1.3 copy-start
  28.4 52.4 %all-to-all-start = ((bf16[32,16,1664]{2,1,0:T(8,128)(2,1)}), bf16[32,16,1664]{2,1,0:T(8,128)(2,1)S(1)}, u32[]{:S(2)}, u32[]{:S(2)}) async-start(bf16[32,16,1664]{2,1,0:T(8,128)(2,1)} %broadcast_in_dim.85), calls=%async_computation | async-start | bytes 3407872 | tf_op jit(solution)/shard_map/all_to_all | solution.py:399
  39.4 3.4 %collective-permute-start = (bf16[4,16,1536]{2,1,0:T(8,128)(2,1)S(1)}, bf16[4,16,1536]{2,1,0:T(8,128)(2,1)S(1)}, u32[]{:S(2)}, u32[]{:S(2)}) collective-permute-start(bf16[4,16,1536]{2,1,0:T(8,128)(2,1)S(1)} %fusion.13), channel_id=1, source_target_pairs={{0,1},{1,0},{2,3},{3,2},{4,5},{5,4},{6,7},{7,6},{8,9},{9,8},{10,11... | collective-permute-start | bytes 589832 | tf_op jit(solution)/shard_map/ppermute | solution.py:393
  43.4 14.6 %collective-permute-start.1 = (bf16[16,1536]{1,0:T(8,128)(2,1)S(1)}, bf16[16,1536]{1,0:T(8,128)(2,1)S(1)}, u32[]{:S(2)}, u32[]{:S(2)}) collective-permute-start(bf16[16,1536]{1,0:T(8,128)(2,1)S(1)} %get-tuple-element.37), channel_id=1, source_target_pairs={{0,2},{2,4},{4,6},{6,0},{1,3},{3,5},{5,7},{7,1},{8,10},{10,12},{12... | collective-permute-start | bytes 147464 | tf_op jit(solution)/shard_map/ppermute | solution.py:404
  45.3 12.6 %collective-permute-start.2 = (bf16[16,1536]{1,0:T(8,128)(2,1)S(1)}, bf16[16,1536]{1,0:T(8,128)(2,1)S(1)}, u32[]{:S(2)}, u32[]{:S(2)}) collective-permute-start(bf16[16,1536]{1,0:T(8,128)(2,1)S(1)} %get-tuple-element.38), channel_id=1, source_target_pairs={{0,4},{2,6},{4,0},{6,2},{1,5},{3,7},{5,1},{7,3},{8,12},{10,14},{12... | collective-permute-start | bytes 147464 | tf_op jit(solution)/shard_map/ppermute | solution.py:404
  50.5 7.5 %collective-permute-start.3 = (bf16[16,1536]{1,0:T(8,128)(2,1)S(1)}, bf16[16,1536]{1,0:T(8,128)(2,1)S(1)}, u32[]{:S(2)}, u32[]{:S(2)}) collective-permute-start(bf16[16,1536]{1,0:T(8,128)(2,1)S(1)} %get-tuple-element.39), channel_id=1, source_target_pairs={{0,6},{2,0},{4,2},{6,4},{1,7},{3,1},{5,3},{7,5},{8,14},{10,8},{12,... | collective-permute-start | bytes 147464 | tf_op jit(solution)/shard_map/ppermute | solution.py:404
  80.7 5.4 %copy-start.5 = (bf16[256,1536]{0,1:T(8,128)(2,1)S(1)}, bf16[256,1536]{0,1:T(8,128)(2,1)}, u32[]{:S(2)}) copy-start(bf16[256,1536]{0,1:T(8,128)(2,1)} %copy-done.4) | copy-start | bytes 2359300
  80.7 5.5 %copy-start.10 = (f32[128]{0:T(128)S(1)}, f32[128]{0:T(128)}, u32[]{:S(2)}) copy-start(f32[128]{0:T(128)} %copy-done.9) | copy-start | bytes 1540
  82.7 5.0 %collective-permute-start.4 = (bf16[128,1536]{1,0:T(8,128)(2,1)}, bf16[128,1536]{1,0:T(8,128)(2,1)S(1)}, u32[]{:S(2)}, u32[]{:S(2)}) collective-permute-start(bf16[128,1536]{1,0:T(8,128)(2,1)} %get-tuple-element.42), channel_id=1, source_target_pairs={{0,1},{1,0},{2,3},{3,2},{4,5},{5,4},{6,7},{7,6},{8,9},{9,8},{10,11... | collective-permute-start | bytes 1179656 | tf_op jit(solution)/shard_map/ppermute | solution.py:410
  89.7 5.2 %copy-start.6 = (f32[128,1536]{0,1:T(8,128)S(1)}, f32[128,1536]{0,1:T(8,128)}, u32[]{:S(2)}) copy-start(f32[128,1536]{0,1:T(8,128)} %fusion) | copy-start | bytes 2359300
  89.7 16.5 %all-to-all-start.1 = ((bf16[8,16,1536]{2,1,0:T(8,128)(2,1)}), bf16[8,16,1536]{2,1,0:T(8,128)(2,1)S(1)}, u32[]{:S(2)}, u32[]{:S(2)}) async-start(bf16[8,16,1536]{2,1,0:T(8,128)(2,1)} %bitcast.11), calls=%async_computation.1 | async-start | bytes 786432 | tf_op jit(solution)/shard_map/all_to_all | solution.py:418
  95.2 12.3 %collective-permute-start.5 = (bf16[128,384]{1,0:T(8,128)(2,1)S(1)}, bf16[128,384]{1,0:T(8,128)(2,1)S(1)}, u32[]{:S(2)}, u32[]{:S(2)}) collective-permute-start(bf16[128,384]{1,0:T(8,128)(2,1)S(1)} %get-tuple-element.50.hidden_ref), channel_id=1, source_target_pairs={{0,8},{8,0},{1,9},{9,1},{2,10},{10,2},{3,11},{11,3},{4,12},{12,4},... | collective-permute-start | bytes 294920 | tf_op jit(solution)/shard_map/ppermute | solution.py:416
  106.2 25.0 %copy-start.3 = (bf16[1536,384]{1,0:T(8,128)(2,1)S(1)}, bf16[1536,384]{1,0:T(8,128)(2,1)}, u32[]{:S(2)}) copy-start(bf16[1536,384]{1,0:T(8,128)(2,1)} %up_ref.1) | copy-start | bytes 3538948
  106.2 24.9 %copy-start.1 = (bf16[384,1536]{1,0:T(8,128)(2,1)S(1)}, bf16[384,1536]{1,0:T(8,128)(2,1)}, u32[]{:S(2)}) copy-start(bf16[384,1536]{1,0:T(8,128)(2,1)} %down_ref.1) | copy-start | bytes 3538948
  132.9 13.8 %copy-start.7 = (bf16[128,192]{0,1:T(8,128)(2,1)S(1)}, bf16[128,192]{0,1:T(8,128)(2,1)}, u32[]{:S(2)}) copy-start(bf16[128,192]{0,1:T(8,128)(2,1)} %param.13) | copy-start | bytes 147460
  134.6 29.8 %all-to-all-start.2 = ((bf16[32,80,128]{2,1,0:T(8,128)(2,1)}), bf16[32,80,128]{2,1,0:T(8,128)(2,1)S(1)}, u32[]{:S(2)}, u32[]{:S(2)}) async-start(bf16[32,80,128]{2,1,0:T(8,128)(2,1)} %shard_map.154), calls=%async_computation.2 | async-start | bytes 1310720 | tf_op jit(solution)/shard_map/all_to_all | solution.py:434
  144.2 3.6 %collective-permute-start.6 = (bf16[784,128]{1,0:T(8,128)(2,1)S(1)}, bf16[784,128]{1,0:T(8,128)(2,1)S(1)}, u32[]{:S(2)}, u32[]{:S(2)}) collective-permute-start(bf16[784,128]{1,0:T(8,128)(2,1)S(1)} %get-tuple-element.56), channel_id=1, source_target_pairs={{0,1},{1,0},{2,3},{3,2},{4,5},{5,4},{6,7},{7,6},{8,9},{9,8},{10,11... | collective-permute-start | bytes 602120 | tf_op jit(solution)/shard_map/ppermute | solution.py:435
  148.4 13.0 %collective-permute-start.7 = (bf16[208,128]{1,0:T(8,128)(2,1)S(1)}, bf16[208,128]{1,0:T(8,128)(2,1)S(1)}, u32[]{:S(2)}, u32[]{:S(2)}) collective-permute-start(bf16[208,128]{1,0:T(8,128)(2,1)S(1)} %get-tuple-element.59), channel_id=1, source_target_pairs={{0,2},{2,4},{4,6},{6,0},{1,3},{3,5},{5,7},{7,1},{8,10},{10,12},{12... | collective-permute-start | bytes 159752 | tf_op jit(solution)/shard_map/ppermute | solution.py:437
  153.9 9.3 %collective-permute-start.8 = (bf16[208,128]{1,0:T(8,128)(2,1)S(1)}, bf16[208,128]{1,0:T(8,128)(2,1)S(1)}, u32[]{:S(2)}, u32[]{:S(2)}) collective-permute-start(bf16[208,128]{1,0:T(8,128)(2,1)S(1)} %get-tuple-element.60), channel_id=1, source_target_pairs={{0,4},{2,6},{4,0},{6,2},{1,5},{3,7},{5,1},{7,3},{8,12},{10,14},{12... | collective-permute-start | bytes 159752 | tf_op jit(solution)/shard_map/ppermute | solution.py:437
  156.2 8.2 %collective-permute-start.9 = (bf16[208,128]{1,0:T(8,128)(2,1)S(1)}, bf16[208,128]{1,0:T(8,128)(2,1)S(1)}, u32[]{:S(2)}, u32[]{:S(2)}) collective-permute-start(bf16[208,128]{1,0:T(8,128)(2,1)S(1)} %get-tuple-element.61), channel_id=1, source_target_pairs={{0,6},{2,0},{4,2},{6,4},{1,7},{3,1},{5,3},{7,5},{8,14},{10,8},{12,... | collective-permute-start | bytes 159752 | tf_op jit(solution)/shard_map/ppermute | solution.py:437

commit v7 on v6

--- a/solution.py
+++ b/solution.py
@@ -118,7 +118,10 @@
 ):
     across = (((1,), (1,)), ((), ()))
     core = where_ref[1]
-    grad = grad_ref[where_ref[0]][:, :WIDE]
+    first = where_ref[0] * 4
+    grad = jnp.concatenate(
+        [grad_ref[side, first + at, :, :WIDE] for at in range(4) for side in range(2)], axis=0
+    )
     grad_hidden = lax.dot_general(grad, down_ref[...], across, preferred_element_type=jnp.float32)
     grad_pre = (grad_hidden * gelu_slope(pre_ref[...])).astype(jnp.bfloat16)
     part = lax.dot_general(up_ref[...], grad_pre, across, preferred_element_type=jnp.float32)
@@ -159,7 +162,7 @@
         cost_estimate=pl.CostEstimate(
             flops=4 * ROWS * 384 * WIDE, bytes_accessed=4000000, transcendentals=0
         ),
-    )(where, grad_all.reshape(2, ROWS, WIDE + EXTRA), w_down, preact, w_up, gain_t, gs_t)
+    )(where, grad_all, w_down, preact, w_up, gain_t, gs_t)
 
 
 def chip_kernel(where_ref, own_ref, sums_ref, got_ref, one_ref, two_ref, three_ref, keep_ref, all_ref, hold_ref):
@@ -294,7 +297,9 @@
 
 def down_kernel(ylo_ref, grad_ref, hidden_ref, other_ref, out_ref):
     even = ylo_ref[0] == 0
-    rows = grad_ref[:, :WIDE]
+    rows = jnp.concatenate(
+        [grad_ref[side, at, :, :WIDE] for at in range(8) for side in range(2)], axis=0
+    )
     mine = hidden_ref[...]
     other = other_ref[...]
     hidden = jnp.concatenate(
@@ -310,7 +315,7 @@
         out_ref[:, piece * 24 : (piece + 1) * 24, :] = jnp.where(
             even, part[:, 0], part[:, 1]
         ).astype(jnp.bfloat16)
-    tail = grad_ref[:, WIDE:].astype(jnp.float32)
+    tail = grad_ref[:, :, :, WIDE:].astype(jnp.float32).reshape(256, EXTRA)
     total = jnp.sum(tail, axis=0, keepdims=True)
     first = total.astype(jnp.bfloat16).astype(jnp.float32)
     second = (total - first).astype(jnp.bfloat16).astype(jnp.float32)
@@ -425,7 +430,16 @@
     loss_block = jnp.pad(pieces(loss_part, 3), ((0, IMG - 3), (0, 0)))
     grad_send = jnp.concatenate([grad_low, loss_block], axis=1)
     grad_send, hidden_other = lax.optimization_barrier((grad_send, hidden_other))
-    grad_all = lax.all_gather(grad_send, RING, axis=0, tiled=True)
+    grad_chips = lax.all_to_all(
+        jnp.broadcast_to(grad_send[None], (8, IMG, WIDE + EXTRA)).reshape(ROWS, WIDE + EXTRA),
+        ("ylo", "yhi"),
+        split_axis=0,
+        concat_axis=0,
+        tiled=True,
+    )
+    grad_all = lax.all_gather(grad_chips, "core", axis=0, tiled=True).reshape(
+        2, 8, IMG, WIDE + EXTRA
+    )
     send, own_blocks, own_sums = back_rows(
         where, grad_all, w_down, preact, w_up, gain_t, gs_t
     )
@@ -438,7 +452,11 @@
     gain_own = lax.dynamic_slice_in_dim(ln_gain, col0, SLICE, 0)
     scaled_own = ((pooled.astype(jnp.float32) - average) * inverse).T
     inverse_t = jnp.broadcast_to(inverse.reshape(1, ROWS), (8, ROWS))
-    grad_own = lax.dynamic_slice(grad_all, (ylo * ROWS, col0), (ROWS, SLICE))
+    grad_own = (
+        lax.dynamic_slice(grad_all, (0, ylo * 4, 0, col0), (2, 4, IMG, SLICE))
+        .transpose(1, 0, 2, 3)
+        .reshape(ROWS, SLICE)
+    )
     grad_pooled, grad_down, loss = last_rows(
         sends[3], sends[4], gots, inverse_t, inverse_t[:1] * gain_own[:, None],
         inverse_t[:1] * scaled_own, grad_own.T, down_got,

time: 166 us -> 166 us (level)
  starting transfers between devices: 62.6 us -> 60.5 us
  waiting for transfers between devices: 14 us -> 16.1 us
    all_gather x1, blocking collectives: 23.4 us -> 6.49 us  [shards(): lax.all_gather(grad_chips, 'core', axis=0, tiled=True)]
    all_to_all x0 -> x1, blocking collectives: none -> 16.9 us  [shards(): lax.all_to_all(jnp.broadcast_to(grad_send[None], (8, IMG, WIDE + EXTRA))....]
    ppermute x6, starting transfers between devices: 25.2 us -> 23 us  [shards(): lax.ppermute(sends[step - 1], 'yhi', turn(step))]
    ppermute x6, waiting for transfers between devices: 3.07 us -> 5.18 us  [shards(): lax.ppermute(sends[step - 1], 'yhi', turn(step))]
where the time goes in v7:
time: 166 us; the launch traced here: 165 us
  blocking collectives  68.2 us (41%)
  starting transfers between devices  60.5 us (36%)
  waiting for transfers between devices  16.1 us (10%)
  Pallas kernels  9.42 us (6%)
  other arithmetic  3.67 us (2%)
  between operations  3.05 us (2%)
  local copies, waits for them, and re-layouts  2.84 us (2%)
    ppermute x6, starting transfers between devices, shards(): lax.ppermute(sends[step - 1], 'yhi', turn(step))  23 us
    all_gather x1, blocking collectives, shards(): img_all = lax.all_gather(img_send, RING, axis=0, tiled=True)  22.6 us
    all_gather x1, blocking collectives, shards(): lax.all_gather(jnp.concatenate([pooled, text_embed], axis=0), TENS, axis=...  22.2 us
    all_to_all x1, blocking collectives, shards(): lax.all_to_all(jnp.broadcast_to(grad_send[None], (8, IMG, WIDE + EXTRA))....  16.9 us
    all_to_all x1, starting transfers between devices, shards(): lax.all_to_all(txt_copies, ('x', 'z'), split_axis=0, concat_axis=0, tiled...  11 us
    all_to_all x1, starting transfers between devices, shards(): lax.all_to_all(down_send, ('x', 'z'), split_axis=0, concat_axis=0, tiled=...  9.51 us
    all_to_all x1, waiting for transfers between devices, shards(): lax.all_to_all(chip_part, ('ylo', 'yhi'), split_axis=0, concat_axis=0, ti...  7.53 us
    all_gather x1, blocking collectives, shards(): lax.all_gather(grad_chips, 'core', axis=0, tiled=True)  6.49 us
  transfers between devices with their start and end apart: 13, of which 7 were waited for; matrix products, arithmetic and copies ran while one was open for 1% of the time, Pallas kernels for 1%

profile of v7, /device:TPU:1, one launch (start us, length us, event | category | flops | bytes accessed | tf_op | source)
XLA Modules:
  0.0 165.2 jit_solution(10504169522923626535)
XLA Ops:
  0.6 0.8 pad_maximum_fusion
  1.5 22.2 %all_gather.9 = bf16[256,1536]{0,1:T(8,128)(2,1)S(1)} all-gather(bf16[256,192]{0,1:T(8,128)(2,1)S(1)} %pad_maximum_fusion), channel_id=1, replica_groups=mesh['x'=4,'z'=8,'ylo'=2,'yhi'=4,'core'=2] {'yhi','core'}, dimensions={1}, use_global_device_ids=true | all-gather | bytes 884736 | tf_op jit(solution)/shard_map/all_gather | solution.py:371
  23.7 0.0 copy-start.2
  23.7 0.0 copy-start.8
  23.7 0.0 copy-start.14
  23.7 0.0 copy-start.15
  23.7 0.3 copy.27
  24.0 0.2 convert_reduce_fusion
  24.3 0.1 multiply_reduce_fusion.1
  24.4 0.1 divide_convert_fusion.1
  24.5 0.2 fusion.2
  24.7 0.2 convert_reduce_fusion.2
  24.9 0.1 select_convert_fusion
  25.0 0.3 dynamic_update_slice.5
  25.4 0.0 copy-start
  25.4 1.0 fusion.12
  26.4 0.3 copy-done
  26.6 0.4 convolution_add_fusion
  27.0 1.3 broadcast_in_dim.91
  28.4 11.0 %all-to-all-start = ((bf16[32,16,1664]{2,1,0:T(8,128)(2,1)}), bf16[32,16,1664]{2,1,0:T(8,128)(2,1)S(1)}, u32[]{:S(2)}, u32[]{:S(2)}) async-start(bf16[32,16,1664]{2,1,0:T(8,128)(2,1)} %broadcast_in_dim.91), calls=%async_computation | async-start | bytes 3407872 | tf_op jit(solution)/shard_map/all_to_all | solution.py:404
  39.4 2.4 %collective-permute-start = (bf16[4,16,1536]{2,1,0:T(8,128)(2,1)S(1)}, bf16[4,16,1536]{2,1,0:T(8,128)(2,1)S(1)}, u32[]{:S(2)}, u32[]{:S(2)}) collective-permute-start(bf16[4,16,1536]{2,1,0:T(8,128)(2,1)S(1)} %fusion.13), channel_id=1, source_target_pairs={{0,1},{1,0},{2,3},{3,2},{4,5},{5,4},{6,7},{7,6},{8,9},{9,8},{10,11... | collective-permute-start | bytes 589832 | tf_op jit(solution)/shard_map/ppermute | solution.py:398
  41.7 0.1 pad_add_fusion.where_ref
  41.8 1.0 collective-permute-done.got_ref
  42.8 0.6 shard_map.148
  43.4 1.9 %collective-permute-start.1 = (bf16[16,1536]{1,0:T(8,128)(2,1)S(1)}, bf16[16,1536]{1,0:T(8,128)(2,1)S(1)}, u32[]{:S(2)}, u32[]{:S(2)}) collective-permute-start(bf16[16,1536]{1,0:T(8,128)(2,1)S(1)} %get-tuple-element.37), channel_id=1, source_target_pairs={{0,2},{2,4},{4,6},{6,0},{1,3},{3,5},{5,7},{7,1},{8,10},{10,12},{12... | collective-permute-start | bytes 147464 | tf_op jit(solution)/shard_map/ppermute | solution.py:409
  45.3 5.2 %collective-permute-start.2 = (bf16[16,1536]{1,0:T(8,128)(2,1)S(1)}, bf16[16,1536]{1,0:T(8,128)(2,1)S(1)}, u32[]{:S(2)}, u32[]{:S(2)}) collective-permute-start(bf16[16,1536]{1,0:T(8,128)(2,1)S(1)} %get-tuple-element.38), channel_id=1, source_target_pairs={{0,4},{2,6},{4,0},{6,2},{1,5},{3,7},{5,1},{7,3},{8,12},{10,14},{12... | collective-permute-start | bytes 147464 | tf_op jit(solution)/shard_map/ppermute | solution.py:409
  50.5 5.5 %collective-permute-start.3 = (bf16[16,1536]{1,0:T(8,128)(2,1)S(1)}, bf16[16,1536]{1,0:T(8,128)(2,1)S(1)}, u32[]{:S(2)}, u32[]{:S(2)}) collective-permute-start(bf16[16,1536]{1,0:T(8,128)(2,1)S(1)} %get-tuple-element.39), channel_id=1, source_target_pairs={{0,6},{2,0},{4,2},{6,4},{1,7},{3,1},{5,3},{7,5},{8,14},{10,8},{12,... | collective-permute-start | bytes 147464 | tf_op jit(solution)/shard_map/ppermute | solution.py:409
  58.0 0.1 shard_map.149
  58.1 22.6 %all_gather.10 = bf16[256,1664]{1,0:T(8,128)(2,1)S(1)} all-gather(bf16[16,1664]{1,0:T(8,128)(2,1)S(1)} %get-tuple-element.40), channel_id=1, replica_groups=mesh['x'=4,'z'=8,'ylo'=2,'yhi'=4,'core'=2] {'ylo','yhi','core'}, dimensions={0}, use_global_device_ids=true | all-gather | bytes 905216 | tf_op jit(solution)/shard_map/all_gather | solution.py:411
  80.7 2.0 %shard_map.150 = (bf16[128,1536]{1,0:T(8,128)(2,1)}, f32[8,128]{1,0:T(8,128)S(1)}) custom-call(s32[1]{0:T(128)} %bitcast.10.which_ref, f32[1]{0:T(128)S(6)} %copy.30.temper_ref, f32[1]{0:T(128)S(6)} %copy.31.offset_ref, f32[1]{0:T(128)S(6)} %copy.32.factor_ref, bf16[8,2,16,1664]{3,2,1,0:T(8,128)(2,1)S(1)} %bitcast.51, bf16[512,1664]{1,0:T(8,128)(2,1)S(1)} %bitcast.46), custom_call_target="tpu_custom_call" | custom-call | flops 402653184 | bytes 3000000 | tf_op jit(solution)/shard_map/pallas_call | solution.py:49
  82.7 3.5 %collective-permute-start.4 = (bf16[128,1536]{1,0:T(8,128)(2,1)}, bf16[128,1536]{1,0:T(8,128)(2,1)S(1)}, u32[]{:S(2)}, u32[]{:S(2)}) collective-permute-start(bf16[128,1536]{1,0:T(8,128)(2,1)} %get-tuple-element.42), channel_id=1, source_target_pairs={{0,1},{1,0},{2,3},{3,2},{4,5},{5,4},{6,7},{7,6},{8,9},{9,8},{10,11... | collective-permute-start | bytes 1179656 | tf_op jit(solution)/shard_map/ppermute | solution.py:415
  86.2 1.0 fusion
  87.2 0.1 reduce
  87.3 0.4 collective-permute-done.4.refs_0_
  87.7 2.0 %shard_map.151 = (bf16[128,1536]{1,0:T(8,128)(2,1)}, f32[8,128]{1,0:T(8,128)S(1)}) custom-call(s32[1]{0:T(128)} %bitcast.1.which_ref, f32[1]{0:T(128)S(6)} %copy.30.temper_ref, f32[1]{0:T(128)S(6)} %copy.31.offset_ref, f32[1]{0:T(128)S(6)} %copy.32.factor_ref, bf16[8,2,16,1664]{3,2,1,0:T(8,128)(2,1)S(1)} %bitcast.52, bf16[512,1664]{1,0:T(8,128)(2,1)S(1)} %bitcast.47, ...), custom_call_target="tpu_custom_call" | custom-call | flops 402653184 | bytes 3000000 | tf_op jit(solution)/shard_map/pallas_call | solution.py:49
  89.7 5.2 %all-to-all-start.1 = ((bf16[8,16,1536]{2,1,0:T(8,128)(2,1)}), bf16[8,16,1536]{2,1,0:T(8,128)(2,1)S(1)}, u32[]{:S(2)}, u32[]{:S(2)}) async-start(bf16[8,16,1536]{2,1,0:T(8,128)(2,1)} %bitcast.11), calls=%async_computation.1 | async-start | bytes 786432 | tf_op jit(solution)/shard_map/all_to_all | solution.py:423
  94.9 0.3 multiply_bitcast_fusion.gs_ref
  95.2 3.4 %collective-permute-start.5 = (bf16[128,384]{1,0:T(8,128)(2,1)S(1)}, bf16[128,384]{1,0:T(8,128)(2,1)S(1)}, u32[]{:S(2)}, u32[]{:S(2)}) collective-permute-start(bf16[128,384]{1,0:T(8,128)(2,1)S(1)} %get-tuple-element.50.hidden_ref), channel_id=1, source_target_pairs={{0,8},{8,0},{1,9},{9,1},{2,10},{10,2},{3,11},{11,3},{4,12},{12,4},... | collective-permute-start | bytes 294920 | tf_op jit(solution)/shard_map/ppermute | solution.py:421
  98.6 7.5 %all-to-all-done.1 = bf16[8,16,1536]{2,1,0:T(8,128)(2,1)S(1)} async-done(((bf16[8,16,1536]{2,1,0:T(8,128)(2,1)}), bf16[8,16,1536]{2,1,0:T(8,128)(2,1)S(1)}, u32[]{:S(2)}, u32[]{:S(2)}) %all-to-all-start.1) | async-done | bytes 393248 | tf_op jit(solution)/shard_map/all_to_all | solution.py:423
  106.2 0.1 convert_reduce_fusion.1
  106.2 0.1 multiply_reduce_fusion
  106.3 0.1 divide_convert_fusion
  106.4 1.0 collective-permute-done.5.other_ref
  107.5 0.0 copy-start.3
  107.5 16.9 %all_to_all.28 = bf16[8,16,1664]{2,1,0:T(8,128)(2,1)S(1)} all-to-all(bf16[8,16,1664]{2,1,0:T(8,128)(2,1)S(1)} %broadcast_in_dim.92), channel_id=1, replica_groups=mesh['x'=4,'z'=8,'ylo'=2,'yhi'=4,'core'=2] {'ylo','yhi'}, dimensions={0} | all-to-all | bytes 851968 | tf_op jit(solution)/shard_map/all_to_all | solution.py:433
  124.4 6.5 %all_gather.11 = bf16[256,1664]{1,0:T(8,128)(2,1)S(1)} all-gather(bf16[128,1664]{1,0:T(8,128)(2,1)S(1)} %bitcast.56), channel_id=1, replica_groups=mesh['x'=4,'z'=8,'ylo'=2,'yhi'=4,'core'=2] {'core'}, dimensions={0}, use_global_device_ids=true | all-gather | bytes 1277952 | tf_op jit(solution)/shard_map/all_gather | solution.py:440
  130.9 0.3 broadcast_in_dim.93.gain_ref
  131.2 1.7 %shard_map.152 = (bf16[784,128]{1,0:T(8,128)(2,1)S(1)}, f32[4,192,128]{2,1,0:T(8,128)S(1)}, f32[8,128]{1,0:T(8,128)S(1)}) custom-call(s32[3]{0:T(128)S(1)} %pad_add_fusion.where_ref, bf16[2,8,16,1664]{3,2,1,0:T(8,128)(2,1)S(1)} %bitcast.48, bf16[384,1536]{1,0:T(8,128)(2,1)S(1)} %copy-done.1, f32[128,384]{1,0:T(8,128)S(1)} %get-tuple-element.79.pre_ref, ...), custom_call_target="tpu_custom_call" | custom-call | flops 301989888 | bytes 4000000 | tf_op jit(solution)/shard_map/pallas_call | solution.py:151
  132.9 0.0 copy-start.7
  133.0 1.7 %shard_map.154 = bf16[32,80,128]{2,1,0:T(8,128)(2,1)} custom-call(s32[1]{0:T(128)} %bitcast.ylo_ref, bf16[2,8,16,1664]{3,2,1,0:T(8,128)(2,1)S(1)} %bitcast.49, bf16[128,384]{1,0:T(8,128)(2,1)S(1)} %get-tuple-element.50.hidden_ref, bf16[128,384]{1,0:T(8,128)(2,1)S(1)} %collective-permute-done.5.other_ref), custom_call_target="tpu_custom_call" | custom-call | flops 301989888 | bytes 1700000 | tf_op jit(solution)/shard_map/pallas_call | solution.py:331
  134.6 9.5 %all-to-all-start.3 = ((bf16[32,80,128]{2,1,0:T(8,128)(2,1)}), bf16[32,80,128]{2,1,0:T(8,128)(2,1)S(1)}, u32[]{:S(2)}, u32[]{:S(2)}) async-start(bf16[32,80,128]{2,1,0:T(8,128)(2,1)} %shard_map.154), calls=%async_computation.3 | async-start | bytes 1310720 | tf_op jit(solution)/shard_map/all_to_all | solution.py:448
  144.1 0.1 dynamic_slice.15
  144.2 2.6 %collective-permute-start.6 = (bf16[784,128]{1,0:T(8,128)(2,1)S(1)}, bf16[784,128]{1,0:T(8,128)(2,1)S(1)}, u32[]{:S(2)}, u32[]{:S(2)}) collective-permute-start(bf16[784,128]{1,0:T(8,128)(2,1)S(1)} %get-tuple-element.56), channel_id=1, source_target_pairs={{0,1},{1,0},{2,3},{3,2},{4,5},{5,4},{6,7},{7,6},{8,9},{9,8},{10,11... | collective-permute-start | bytes 602120 | tf_op jit(solution)/shard_map/ppermute | solution.py:449
  146.8 0.1 broadcast_multiply_fusion.invgain_ref
  146.9 1.0 collective-permute-done.6.got_ref
  147.9 0.6 shard_map.153
  148.5 2.0 %collective-permute-start.7 = (bf16[208,128]{1,0:T(8,128)(2,1)S(1)}, bf16[208,128]{1,0:T(8,128)(2,1)S(1)}, u32[]{:S(2)}, u32[]{:S(2)}) collective-permute-start(bf16[208,128]{1,0:T(8,128)(2,1)S(1)} %get-tuple-element.59), channel_id=1, source_target_pairs={{0,2},{2,4},{4,6},{6,0},{1,3},{3,5},{5,7},{7,1},{8,10},{10,12},{12... | collective-permute-start | bytes 159752 | tf_op jit(solution)/shard_map/ppermute | solution.py:451
  150.5 4.9 %collective-permute-start.8 = (bf16[208,128]{1,0:T(8,128)(2,1)S(1)}, bf16[208,128]{1,0:T(8,128)(2,1)S(1)}, u32[]{:S(2)}, u32[]{:S(2)}) collective-permute-start(bf16[208,128]{1,0:T(8,128)(2,1)S(1)} %get-tuple-element.60), channel_id=1, source_target_pairs={{0,4},{2,6},{4,0},{6,2},{1,5},{3,7},{5,1},{7,3},{8,12},{10,14},{12... | collective-permute-start | bytes 159752 | tf_op jit(solution)/shard_map/ppermute | solution.py:451
  155.3 3.6 %collective-permute-start.9 = (bf16[208,128]{1,0:T(8,128)(2,1)S(1)}, bf16[208,128]{1,0:T(8,128)(2,1)S(1)}, u32[]{:S(2)}, u32[]{:S(2)}) collective-permute-start(bf16[208,128]{1,0:T(8,128)(2,1)S(1)} %get-tuple-element.61), channel_id=1, source_target_pairs={{0,6},{2,0},{4,2},{6,4},{1,7},{3,1},{5,3},{7,5},{8,14},{10,8},{12,... | collective-permute-start | bytes 159752 | tf_op jit(solution)/shard_map/ppermute | solution.py:451
  159.0 0.1 dynamic-slice_bitcast_fusion
  159.1 0.1 copy.26
  159.2 0.1 collective-permute-done.8.two_ref
  159.3 5.1 %collective-permute-done.9.three_ref = bf16[208,128]{1,0:T(8,128)(2,1)S(1)} collective-permute-done((bf16[208,128]{1,0:T(8,128)(2,1)S(1)}, bf16[208,128]{1,0:T(8,128)(2,1)S(1)}, u32[]{:S(2)}, u32[]{:S(2)}) %collective-permute-start.9) | collective-permute-done | bytes 53280 | tf_op jit(solution)/shard_map/ppermute | solution.py:451
  164.4 0.8 shard_map.155
  (49 shorter events, 0.3 us)
Async XLA Ops:
  23.7 1.7 %copy-start.4 = (bf16[256,1536]{0,1:T(8,128)(2,1)}, bf16[256,1536]{0,1:T(8,128)(2,1)S(1)}, u32[]{:S(2)}) copy-start(bf16[256,1536]{0,1:T(8,128)(2,1)S(1)} %all_gather.9) | copy-start | bytes 2359300
  23.7 1.1 copy-start.12
  23.7 1.1 copy-start.13
  23.7 1.4 copy-start.11
  23.7 1.7 %copy-start.2 = (bf16[1536,384]{1,0:T(8,128)(2,1)S(1)}, bf16[1536,384]{1,0:T(8,128)(2,1)}, u32[]{:S(2)}) copy-start(bf16[1536,384]{1,0:T(8,128)(2,1)} %up_ref.1) | copy-start | bytes 3538948
  23.7 1.7 %copy-start.8 = (f32[1536]{0:T(1024)S(1)}, f32[1536]{0:T(1024)}, u32[]{:S(2)}) copy-start(f32[1536]{0:T(1024)} %param.14) | copy-start | bytes 18436
  23.7 1.7 copy-start.14
  23.7 1.6 copy-start.15
  24.5 1.9 %copy-start.9 = (f32[128]{0:T(128)}, f32[128]{0:T(128)S(1)}, u32[]{:S(2)}) copy-start(f32[128]{0:T(128)S(1)} %broadcast_multiply_fusion.1) | copy-start | bytes 1540
  25.4 1.3 copy-start
  28.4 52.4 %all-to-all-start = ((bf16[32,16,1664]{2,1,0:T(8,128)(2,1)}), bf16[32,16,1664]{2,1,0:T(8,128)(2,1)S(1)}, u32[]{:S(2)}, u32[]{:S(2)}) async-start(bf16[32,16,1664]{2,1,0:T(8,128)(2,1)} %broadcast_in_dim.91), calls=%async_computation | async-start | bytes 3407872 | tf_op jit(solution)/shard_map/all_to_all | solution.py:404
  39.4 3.4 %collective-permute-start = (bf16[4,16,1536]{2,1,0:T(8,128)(2,1)S(1)}, bf16[4,16,1536]{2,1,0:T(8,128)(2,1)S(1)}, u32[]{:S(2)}, u32[]{:S(2)}) collective-permute-start(bf16[4,16,1536]{2,1,0:T(8,128)(2,1)S(1)} %fusion.13), channel_id=1, source_target_pairs={{0,1},{1,0},{2,3},{3,2},{4,5},{5,4},{6,7},{7,6},{8,9},{9,8},{10,11... | collective-permute-start | bytes 589832 | tf_op jit(solution)/shard_map/ppermute | solution.py:398
  43.4 14.6 %collective-permute-start.1 = (bf16[16,1536]{1,0:T(8,128)(2,1)S(1)}, bf16[16,1536]{1,0:T(8,128)(2,1)S(1)}, u32[]{:S(2)}, u32[]{:S(2)}) collective-permute-start(bf16[16,1536]{1,0:T(8,128)(2,1)S(1)} %get-tuple-element.37), channel_id=1, source_target_pairs={{0,2},{2,4},{4,6},{6,0},{1,3},{3,5},{5,7},{7,1},{8,10},{10,12},{12... | collective-permute-start | bytes 147464 | tf_op jit(solution)/shard_map/ppermute | solution.py:409
  45.3 12.6 %collective-permute-start.2 = (bf16[16,1536]{1,0:T(8,128)(2,1)S(1)}, bf16[16,1536]{1,0:T(8,128)(2,1)S(1)}, u32[]{:S(2)}, u32[]{:S(2)}) collective-permute-start(bf16[16,1536]{1,0:T(8,128)(2,1)S(1)} %get-tuple-element.38), channel_id=1, source_target_pairs={{0,4},{2,6},{4,0},{6,2},{1,5},{3,7},{5,1},{7,3},{8,12},{10,14},{12... | collective-permute-start | bytes 147464 | tf_op jit(solution)/shard_map/ppermute | solution.py:409
  50.5 7.5 %collective-permute-start.3 = (bf16[16,1536]{1,0:T(8,128)(2,1)S(1)}, bf16[16,1536]{1,0:T(8,128)(2,1)S(1)}, u32[]{:S(2)}, u32[]{:S(2)}) collective-permute-start(bf16[16,1536]{1,0:T(8,128)(2,1)S(1)} %get-tuple-element.39), channel_id=1, source_target_pairs={{0,6},{2,0},{4,2},{6,4},{1,7},{3,1},{5,3},{7,5},{8,14},{10,8},{12,... | collective-permute-start | bytes 147464 | tf_op jit(solution)/shard_map/ppermute | solution.py:409
  80.7 5.4 %copy-start.5 = (bf16[256,1536]{0,1:T(8,128)(2,1)S(1)}, bf16[256,1536]{0,1:T(8,128)(2,1)}, u32[]{:S(2)}) copy-start(bf16[256,1536]{0,1:T(8,128)(2,1)} %copy-done.4) | copy-start | bytes 2359300
  80.7 5.5 %copy-start.10 = (f32[128]{0:T(128)S(1)}, f32[128]{0:T(128)}, u32[]{:S(2)}) copy-start(f32[128]{0:T(128)} %copy-done.9) | copy-start | bytes 1540
  82.7 5.0 %collective-permute-start.4 = (bf16[128,1536]{1,0:T(8,128)(2,1)}, bf16[128,1536]{1,0:T(8,128)(2,1)S(1)}, u32[]{:S(2)}, u32[]{:S(2)}) collective-permute-start(bf16[128,1536]{1,0:T(8,128)(2,1)} %get-tuple-element.42), channel_id=1, source_target_pairs={{0,1},{1,0},{2,3},{3,2},{4,5},{5,4},{6,7},{7,6},{8,9},{9,8},{10,11... | collective-permute-start | bytes 1179656 | tf_op jit(solution)/shard_map/ppermute | solution.py:415
  89.7 5.2 %copy-start.6 = (f32[128,1536]{0,1:T(8,128)S(1)}, f32[128,1536]{0,1:T(8,128)}, u32[]{:S(2)}) copy-start(f32[128,1536]{0,1:T(8,128)} %fusion) | copy-start | bytes 2359300
  89.7 16.5 %all-to-all-start.1 = ((bf16[8,16,1536]{2,1,0:T(8,128)(2,1)}), bf16[8,16,1536]{2,1,0:T(8,128)(2,1)S(1)}, u32[]{:S(2)}, u32[]{:S(2)}) async-start(bf16[8,16,1536]{2,1,0:T(8,128)(2,1)} %bitcast.11), calls=%async_computation.1 | async-start | bytes 786432 | tf_op jit(solution)/shard_map/all_to_all | solution.py:423
  95.2 12.3 %collective-permute-start.5 = (bf16[128,384]{1,0:T(8,128)(2,1)S(1)}, bf16[128,384]{1,0:T(8,128)(2,1)S(1)}, u32[]{:S(2)}, u32[]{:S(2)}) collective-permute-start(bf16[128,384]{1,0:T(8,128)(2,1)S(1)} %get-tuple-element.50.hidden_ref), channel_id=1, source_target_pairs={{0,8},{8,0},{1,9},{9,1},{2,10},{10,2},{3,11},{11,3},{4,12},{12,4},... | collective-permute-start | bytes 294920 | tf_op jit(solution)/shard_map/ppermute | solution.py:421
  107.5 23.7 %copy-start.3 = (bf16[1536,384]{1,0:T(8,128)(2,1)S(1)}, bf16[1536,384]{1,0:T(8,128)(2,1)}, u32[]{:S(2)}) copy-start(bf16[1536,384]{1,0:T(8,128)(2,1)} %up_ref.1) | copy-start | bytes 3538948
  124.4 6.8 %copy-start.1 = (bf16[384,1536]{1,0:T(8,128)(2,1)S(1)}, bf16[384,1536]{1,0:T(8,128)(2,1)}, u32[]{:S(2)}) copy-start(bf16[384,1536]{1,0:T(8,128)(2,1)} %down_ref.1) | copy-start | bytes 3538948
  132.9 11.3 %copy-start.7 = (bf16[128,192]{0,1:T(8,128)(2,1)S(1)}, bf16[128,192]{0,1:T(8,128)(2,1)}, u32[]{:S(2)}) copy-start(bf16[128,192]{0,1:T(8,128)(2,1)} %param.13) | copy-start | bytes 147460
  134.6 29.7 %all-to-all-start.3 = ((bf16[32,80,128]{2,1,0:T(8,128)(2,1)}), bf16[32,80,128]{2,1,0:T(8,128)(2,1)S(1)}, u32[]{:S(2)}, u32[]{:S(2)}) async-start(bf16[32,80,128]{2,1,0:T(8,128)(2,1)} %shard_map.154), calls=%async_computation.3 | async-start | bytes 1310720 | tf_op jit(solution)/shard_map/all_to_all | solution.py:448
  144.2 3.6 %collective-permute-start.6 = (bf16[784,128]{1,0:T(8,128)(2,1)S(1)}, bf16[784,128]{1,0:T(8,128)(2,1)S(1)}, u32[]{:S(2)}, u32[]{:S(2)}) collective-permute-start(bf16[784,128]{1,0:T(8,128)(2,1)S(1)} %get-tuple-element.56), channel_id=1, source_target_pairs={{0,1},{1,0},{2,3},{3,2},{4,5},{5,4},{6,7},{7,6},{8,9},{9,8},{10,11... | collective-permute-start | bytes 602120 | tf_op jit(solution)/shard_map/ppermute | solution.py:449
  148.5 10.7 %collective-permute-start.7 = (bf16[208,128]{1,0:T(8,128)(2,1)S(1)}, bf16[208,128]{1,0:T(8,128)(2,1)S(1)}, u32[]{:S(2)}, u32[]{:S(2)}) collective-permute-start(bf16[208,128]{1,0:T(8,128)(2,1)S(1)} %get-tuple-element.59), channel_id=1, source_target_pairs={{0,2},{2,4},{4,6},{6,0},{1,3},{3,5},{5,7},{7,1},{8,10},{10,12},{12... | collective-permute-start | bytes 159752 | tf_op jit(solution)/shard_map/ppermute | solution.py:451
  150.5 8.8 %collective-permute-start.8 = (bf16[208,128]{1,0:T(8,128)(2,1)S(1)}, bf16[208,128]{1,0:T(8,128)(2,1)S(1)}, u32[]{:S(2)}, u32[]{:S(2)}) collective-permute-start(bf16[208,128]{1,0:T(8,128)(2,1)S(1)} %get-tuple-element.60), channel_id=1, source_target_pairs={{0,4},{2,6},{4,0},{6,2},{1,5},{3,7},{5,1},{7,3},{8,12},{10,14},{12... | collective-permute-start | bytes 159752 | tf_op jit(solution)/shard_map/ppermute | solution.py:451
  155.3 9.0 %collective-permute-start.9 = (bf16[208,128]{1,0:T(8,128)(2,1)S(1)}, bf16[208,128]{1,0:T(8,128)(2,1)S(1)}, u32[]{:S(2)}, u32[]{:S(2)}) collective-permute-start(bf16[208,128]{1,0:T(8,128)(2,1)S(1)} %get-tuple-element.61), channel_id=1, source_target_pairs={{0,6},{2,0},{4,2},{6,4},{1,7},{3,1},{5,3},{7,5},{8,14},{10,8},{12,... | collective-permute-start | bytes 159752 | tf_op jit(solution)/shard_map/ppermute | solution.py:451

commit v8 on v7

--- a/solution.py
+++ b/solution.py
@@ -406,7 +406,7 @@
     ).reshape(4 * ROWS, WIDE + EXTRA)
     where = jnp.stack([lax.axis_index("ylo"), core, yhi]).astype(jnp.int32)
     sends = fore_chip(where, part, core_got)
-    gots = [lax.ppermute(sends[step - 1], "yhi", turn(step)) for step in range(1, 4)]
+    gots = [lax.ppermute(sends[step - 1], "yhi", turn(step)) for step in (2, 1, 3)]
     img_send, img_unit, img_norm = img_rows(sends[3], gots, own, id_columns(image_ids, row0))
     img_all = lax.all_gather(img_send, RING, axis=0, tiled=True)
 
@@ -448,7 +448,7 @@
     down_got = lax.all_to_all(down_send, ("x", "z"), split_axis=0, concat_axis=0, tiled=True)
     got = lax.ppermute(send, "core", [(0, 1), (1, 0)])
     sends = chip_rows(where, own_blocks, own_sums, got)
-    gots = [lax.ppermute(sends[step - 1], "yhi", turn(step)) for step in range(1, 4)]
+    gots = [lax.ppermute(sends[step - 1], "yhi", turn(step)) for step in (2, 1, 3)]
     gain_own = lax.dynamic_slice_in_dim(ln_gain, col0, SLICE, 0)
     scaled_own = ((pooled.astype(jnp.float32) - average) * inverse).T
     inverse_t = jnp.broadcast_to(inverse.reshape(1, ROWS), (8, ROWS))

time: 166 us -> 165 us (level); the launches traced: 165 us -> 162 us
  waiting for transfers between devices: 16.1 us -> 13.4 us
    ppermute x6, waiting for transfers between devices: 5.18 us -> 2.49 us  [shards(): lax.ppermute(sends[step - 1], 'yhi', turn(step))]
  transfers between devices with their start and end apart: 13 -> 13, of which waited for: 7 -> 6; matrix products, arithmetic and copies ran while one was open for 1% -> 1% of each run, Pallas kernels for 1% -> 1%
where the time goes in v8:
time: 165 us; the launch traced here: 162 us
  blocking collectives  68.2 us (41%)
  starting transfers between devices  60.5 us (37%)
  waiting for transfers between devices  13.4 us (8%)
  Pallas kernels  9.42 us (6%)
  other arithmetic  3.67 us (2%)
  between operations  3.06 us (2%)
  local copies, waits for them, and re-layouts  2.84 us (2%)
    ppermute x6, starting transfers between devices, shards(): lax.ppermute(sends[step - 1], 'yhi', turn(step))  23 us
    all_gather x1, blocking collectives, shards(): img_all = lax.all_gather(img_send, RING, axis=0, tiled=True)  22.6 us
    all_gather x1, blocking collectives, shards(): lax.all_gather(jnp.concatenate([pooled, text_embed], axis=0), TENS, axis=...  22.2 us
    all_to_all x1, blocking collectives, shards(): lax.all_to_all(jnp.broadcast_to(grad_send[None], (8, IMG, WIDE + EXTRA))....  16.9 us
    all_to_all x1, starting transfers between devices, shards(): lax.all_to_all(txt_copies, ('x', 'z'), split_axis=0, concat_axis=0, tiled...  11 us
    all_to_all x1, starting transfers between devices, shards(): lax.all_to_all(down_send, ('x', 'z'), split_axis=0, concat_axis=0, tiled=...  9.5 us
    all_to_all x1, waiting for transfers between devices, shards(): lax.all_to_all(chip_part, ('ylo', 'yhi'), split_axis=0, concat_axis=0, ti...  7.52 us
    all_gather x1, blocking collectives, shards(): lax.all_gather(grad_chips, 'core', axis=0, tiled=True)  6.49 us
  transfers between devices with their start and end apart: 13, of which 6 were waited for; matrix products, arithmetic and copies ran while one was open for 1% of the time, Pallas kernels for 1%

profile of v8, /device:TPU:1, one launch (start us, length us, event | category | flops | bytes accessed | tf_op | source)
XLA Modules:
  0.0 162.5 jit_solution(13449144914715153338)
XLA Ops:
  0.6 0.8 pad_maximum_fusion
  1.5 22.2 %all_gather.9 = bf16[256,1536]{0,1:T(8,128)(2,1)S(1)} all-gather(bf16[256,192]{0,1:T(8,128)(2,1)S(1)} %pad_maximum_fusion), channel_id=1, replica_groups=mesh['x'=4,'z'=8,'ylo'=2,'yhi'=4,'core'=2] {'yhi','core'}, dimensions={1}, use_global_device_ids=true | all-gather | bytes 884736 | tf_op jit(solution)/shard_map/all_gather | solution.py:371
  23.7 0.0 copy-start.2
  23.7 0.0 copy-start.8
  23.7 0.0 copy-start.14
  23.7 0.0 copy-start.15
  23.7 0.3 copy.27
  24.0 0.2 convert_reduce_fusion
  24.3 0.1 multiply_reduce_fusion.1
  24.4 0.1 divide_convert_fusion.1
  24.5 0.2 fusion.2
  24.7 0.2 convert_reduce_fusion.2
  24.9 0.1 select_convert_fusion
  25.0 0.3 dynamic_update_slice.5
  25.4 0.0 copy-start
  25.4 1.0 fusion.12
  26.4 0.3 copy-done
  26.6 0.4 convolution_add_fusion
  27.0 1.3 broadcast_in_dim.91
  28.4 11.0 %all-to-all-start = ((bf16[32,16,1664]{2,1,0:T(8,128)(2,1)}), bf16[32,16,1664]{2,1,0:T(8,128)(2,1)S(1)}, u32[]{:S(2)}, u32[]{:S(2)}) async-start(bf16[32,16,1664]{2,1,0:T(8,128)(2,1)} %broadcast_in_dim.91), calls=%async_computation | async-start | bytes 3407872 | tf_op jit(solution)/shard_map/all_to_all | solution.py:404
  39.4 2.4 %collective-permute-start = (bf16[4,16,1536]{2,1,0:T(8,128)(2,1)S(1)}, bf16[4,16,1536]{2,1,0:T(8,128)(2,1)S(1)}, u32[]{:S(2)}, u32[]{:S(2)}) collective-permute-start(bf16[4,16,1536]{2,1,0:T(8,128)(2,1)S(1)} %fusion.13), channel_id=1, source_target_pairs={{0,1},{1,0},{2,3},{3,2},{4,5},{5,4},{6,7},{7,6},{8,9},{9,8},{10,11... | collective-permute-start | bytes 589832 | tf_op jit(solution)/shard_map/ppermute | solution.py:398
  41.7 0.1 pad_add_fusion.where_ref
  41.8 1.0 collective-permute-done.got_ref
  42.8 0.6 shard_map.148
  43.4 5.2 %collective-permute-start.1 = (bf16[16,1536]{1,0:T(8,128)(2,1)S(1)}, bf16[16,1536]{1,0:T(8,128)(2,1)S(1)}, u32[]{:S(2)}, u32[]{:S(2)}) collective-permute-start(bf16[16,1536]{1,0:T(8,128)(2,1)S(1)} %get-tuple-element.37), channel_id=1, source_target_pairs={{0,4},{2,6},{4,0},{6,2},{1,5},{3,7},{5,1},{7,3},{8,12},{10,14},{12... | collective-permute-start | bytes 147464 | tf_op jit(solution)/shard_map/ppermute | solution.py:409
  48.6 1.9 %collective-permute-start.2 = (bf16[16,1536]{1,0:T(8,128)(2,1)S(1)}, bf16[16,1536]{1,0:T(8,128)(2,1)S(1)}, u32[]{:S(2)}, u32[]{:S(2)}) collective-permute-start(bf16[16,1536]{1,0:T(8,128)(2,1)S(1)} %get-tuple-element.38), channel_id=1, source_target_pairs={{0,2},{2,4},{4,6},{6,0},{1,3},{3,5},{5,7},{7,1},{8,10},{10,12},{12... | collective-permute-start | bytes 147464 | tf_op jit(solution)/shard_map/ppermute | solution.py:409
  50.5 5.5 %collective-permute-start.3 = (bf16[16,1536]{1,0:T(8,128)(2,1)S(1)}, bf16[16,1536]{1,0:T(8,128)(2,1)S(1)}, u32[]{:S(2)}, u32[]{:S(2)}) collective-permute-start(bf16[16,1536]{1,0:T(8,128)(2,1)S(1)} %get-tuple-element.39), channel_id=1, source_target_pairs={{0,6},{2,0},{4,2},{6,4},{1,7},{3,1},{5,3},{7,5},{8,14},{10,8},{12,... | collective-permute-start | bytes 147464 | tf_op jit(solution)/shard_map/ppermute | solution.py:409
  57.9 0.0 collective-permute-done.1.one_ref
  58.0 0.1 shard_map.149
  58.1 22.6 %all_gather.10 = bf16[256,1664]{1,0:T(8,128)(2,1)S(1)} all-gather(bf16[16,1664]{1,0:T(8,128)(2,1)S(1)} %get-tuple-element.40), channel_id=1, replica_groups=mesh['x'=4,'z'=8,'ylo'=2,'yhi'=4,'core'=2] {'ylo','yhi','core'}, dimensions={0}, use_global_device_ids=true | all-gather | bytes 905216 | tf_op jit(solution)/shard_map/all_gather | solution.py:411
  80.8 2.0 %shard_map.150 = (bf16[128,1536]{1,0:T(8,128)(2,1)}, f32[8,128]{1,0:T(8,128)S(1)}) custom-call(s32[1]{0:T(128)} %bitcast.10.which_ref, f32[1]{0:T(128)S(6)} %copy.30.temper_ref, f32[1]{0:T(128)S(6)} %copy.31.offset_ref, f32[1]{0:T(128)S(6)} %copy.32.factor_ref, bf16[8,2,16,1664]{3,2,1,0:T(8,128)(2,1)S(1)} %bitcast.51, bf16[512,1664]{1,0:T(8,128)(2,1)S(1)} %bitcast.46), custom_call_target="tpu_custom_call" | custom-call | flops 402653184 | bytes 3000000 | tf_op jit(solution)/shard_map/pallas_call | solution.py:49
  82.7 3.5 %collective-permute-start.4 = (bf16[128,1536]{1,0:T(8,128)(2,1)}, bf16[128,1536]{1,0:T(8,128)(2,1)S(1)}, u32[]{:S(2)}, u32[]{:S(2)}) collective-permute-start(bf16[128,1536]{1,0:T(8,128)(2,1)} %get-tuple-element.42), channel_id=1, source_target_pairs={{0,1},{1,0},{2,3},{3,2},{4,5},{5,4},{6,7},{7,6},{8,9},{9,8},{10,11... | collective-permute-start | bytes 1179656 | tf_op jit(solution)/shard_map/ppermute | solution.py:415
  86.2 1.0 fusion
  87.2 0.1 reduce
  87.3 0.4 collective-permute-done.4.refs_0_
  87.7 2.0 %shard_map.151 = (bf16[128,1536]{1,0:T(8,128)(2,1)}, f32[8,128]{1,0:T(8,128)S(1)}) custom-call(s32[1]{0:T(128)} %bitcast.1.which_ref, f32[1]{0:T(128)S(6)} %copy.30.temper_ref, f32[1]{0:T(128)S(6)} %copy.31.offset_ref, f32[1]{0:T(128)S(6)} %copy.32.factor_ref, bf16[8,2,16,1664]{3,2,1,0:T(8,128)(2,1)S(1)} %bitcast.52, bf16[512,1664]{1,0:T(8,128)(2,1)S(1)} %bitcast.47, ...), custom_call_target="tpu_custom_call" | custom-call | flops 402653184 | bytes 3000000 | tf_op jit(solution)/shard_map/pallas_call | solution.py:49
  89.7 5.2 %all-to-all-start.1 = ((bf16[8,16,1536]{2,1,0:T(8,128)(2,1)}), bf16[8,16,1536]{2,1,0:T(8,128)(2,1)S(1)}, u32[]{:S(2)}, u32[]{:S(2)}) async-start(bf16[8,16,1536]{2,1,0:T(8,128)(2,1)} %bitcast.11), calls=%async_computation.1 | async-start | bytes 786432 | tf_op jit(solution)/shard_map/all_to_all | solution.py:423
  94.9 0.3 multiply_bitcast_fusion.gs_ref
  95.2 3.4 %collective-permute-start.5 = (bf16[128,384]{1,0:T(8,128)(2,1)S(1)}, bf16[128,384]{1,0:T(8,128)(2,1)S(1)}, u32[]{:S(2)}, u32[]{:S(2)}) collective-permute-start(bf16[128,384]{1,0:T(8,128)(2,1)S(1)} %get-tuple-element.50.hidden_ref), channel_id=1, source_target_pairs={{0,8},{8,0},{1,9},{9,1},{2,10},{10,2},{3,11},{11,3},{4,12},{12,4},... | collective-permute-start | bytes 294920 | tf_op jit(solution)/shard_map/ppermute | solution.py:421
  98.6 7.5 %all-to-all-done.1 = bf16[8,16,1536]{2,1,0:T(8,128)(2,1)S(1)} async-done(((bf16[8,16,1536]{2,1,0:T(8,128)(2,1)}), bf16[8,16,1536]{2,1,0:T(8,128)(2,1)S(1)}, u32[]{:S(2)}, u32[]{:S(2)}) %all-to-all-start.1) | async-done | bytes 393248 | tf_op jit(solution)/shard_map/all_to_all | solution.py:423
  106.2 0.1 convert_reduce_fusion.1
  106.2 0.1 multiply_reduce_fusion
  106.3 0.1 divide_convert_fusion
  106.4 1.0 collective-permute-done.5.other_ref
  107.5 0.0 copy-start.3
  107.5 16.9 %all_to_all.28 = bf16[8,16,1664]{2,1,0:T(8,128)(2,1)S(1)} all-to-all(bf16[8,16,1664]{2,1,0:T(8,128)(2,1)S(1)} %broadcast_in_dim.92), channel_id=1, replica_groups=mesh['x'=4,'z'=8,'ylo'=2,'yhi'=4,'core'=2] {'ylo','yhi'}, dimensions={0} | all-to-all | bytes 851968 | tf_op jit(solution)/shard_map/all_to_all | solution.py:433
  124.4 6.5 %all_gather.11 = bf16[256,1664]{1,0:T(8,128)(2,1)S(1)} all-gather(bf16[128,1664]{1,0:T(8,128)(2,1)S(1)} %bitcast.56), channel_id=1, replica_groups=mesh['x'=4,'z'=8,'ylo'=2,'yhi'=4,'core'=2] {'core'}, dimensions={0}, use_global_device_ids=true | all-gather | bytes 1277952 | tf_op jit(solution)/shard_map/all_gather | solution.py:440
  130.9 0.3 broadcast_in_dim.93.gain_ref
  131.2 1.7 %shard_map.152 = (bf16[784,128]{1,0:T(8,128)(2,1)S(1)}, f32[4,192,128]{2,1,0:T(8,128)S(1)}, f32[8,128]{1,0:T(8,128)S(1)}) custom-call(s32[3]{0:T(128)S(1)} %pad_add_fusion.where_ref, bf16[2,8,16,1664]{3,2,1,0:T(8,128)(2,1)S(1)} %bitcast.48, bf16[384,1536]{1,0:T(8,128)(2,1)S(1)} %copy-done.1, f32[128,384]{1,0:T(8,128)S(1)} %get-tuple-element.79.pre_ref, ...), custom_call_target="tpu_custom_call" | custom-call | flops 301989888 | bytes 4000000 | tf_op jit(solution)/shard_map/pallas_call | solution.py:151
  132.9 0.0 copy-start.7
  133.0 1.7 %shard_map.154 = bf16[32,80,128]{2,1,0:T(8,128)(2,1)} custom-call(s32[1]{0:T(128)} %bitcast.ylo_ref, bf16[2,8,16,1664]{3,2,1,0:T(8,128)(2,1)S(1)} %bitcast.49, bf16[128,384]{1,0:T(8,128)(2,1)S(1)} %get-tuple-element.50.hidden_ref, bf16[128,384]{1,0:T(8,128)(2,1)S(1)} %collective-permute-done.5.other_ref), custom_call_target="tpu_custom_call" | custom-call | flops 301989888 | bytes 1700000 | tf_op jit(solution)/shard_map/pallas_call | solution.py:331
  134.6 9.5 %all-to-all-start.3 = ((bf16[32,80,128]{2,1,0:T(8,128)(2,1)}), bf16[32,80,128]{2,1,0:T(8,128)(2,1)S(1)}, u32[]{:S(2)}, u32[]{:S(2)}) async-start(bf16[32,80,128]{2,1,0:T(8,128)(2,1)} %shard_map.154), calls=%async_computation.3 | async-start | bytes 1310720 | tf_op jit(solution)/shard_map/all_to_all | solution.py:448
  144.1 0.1 dynamic_slice.15
  144.2 2.6 %collective-permute-start.6 = (bf16[784,128]{1,0:T(8,128)(2,1)S(1)}, bf16[784,128]{1,0:T(8,128)(2,1)S(1)}, u32[]{:S(2)}, u32[]{:S(2)}) collective-permute-start(bf16[784,128]{1,0:T(8,128)(2,1)S(1)} %get-tuple-element.56), channel_id=1, source_target_pairs={{0,1},{1,0},{2,3},{3,2},{4,5},{5,4},{6,7},{7,6},{8,9},{9,8},{10,11... | collective-permute-start | bytes 602120 | tf_op jit(solution)/shard_map/ppermute | solution.py:449
  146.8 0.1 broadcast_multiply_fusion.invgain_ref
  146.9 1.0 collective-permute-done.6.got_ref
  147.9 0.6 shard_map.153
  148.5 3.1 %collective-permute-start.7 = (bf16[208,128]{1,0:T(8,128)(2,1)S(1)}, bf16[208,128]{1,0:T(8,128)(2,1)S(1)}, u32[]{:S(2)}, u32[]{:S(2)}) collective-permute-start(bf16[208,128]{1,0:T(8,128)(2,1)S(1)} %get-tuple-element.59), channel_id=1, source_target_pairs={{0,4},{2,6},{4,0},{6,2},{1,5},{3,7},{5,1},{7,3},{8,12},{10,14},{12... | collective-permute-start | bytes 159752 | tf_op jit(solution)/shard_map/ppermute | solution.py:451
  151.5 3.8 %collective-permute-start.8 = (bf16[208,128]{1,0:T(8,128)(2,1)S(1)}, bf16[208,128]{1,0:T(8,128)(2,1)S(1)}, u32[]{:S(2)}, u32[]{:S(2)}) collective-permute-start(bf16[208,128]{1,0:T(8,128)(2,1)S(1)} %get-tuple-element.60), channel_id=1, source_target_pairs={{0,2},{2,4},{4,6},{6,0},{1,3},{3,5},{5,7},{7,1},{8,10},{10,12},{12... | collective-permute-start | bytes 159752 | tf_op jit(solution)/shard_map/ppermute | solution.py:451
  155.3 3.6 %collective-permute-start.9 = (bf16[208,128]{1,0:T(8,128)(2,1)S(1)}, bf16[208,128]{1,0:T(8,128)(2,1)S(1)}, u32[]{:S(2)}, u32[]{:S(2)}) collective-permute-start(bf16[208,128]{1,0:T(8,128)(2,1)S(1)} %get-tuple-element.61), channel_id=1, source_target_pairs={{0,6},{2,0},{4,2},{6,4},{1,7},{3,1},{5,3},{7,5},{8,14},{10,8},{12,... | collective-permute-start | bytes 159752 | tf_op jit(solution)/shard_map/ppermute | solution.py:451
  159.0 0.1 dynamic-slice_bitcast_fusion
  159.1 0.1 copy.26
  159.2 2.5 %collective-permute-done.9.three_ref = bf16[208,128]{1,0:T(8,128)(2,1)S(1)} collective-permute-done((bf16[208,128]{1,0:T(8,128)(2,1)S(1)}, bf16[208,128]{1,0:T(8,128)(2,1)S(1)}, u32[]{:S(2)}, u32[]{:S(2)}) %collective-permute-start.9) | collective-permute-done | bytes 53280 | tf_op jit(solution)/shard_map/ppermute | solution.py:451
  161.7 0.8 shard_map.155
  (49 shorter events, 0.3 us)
Async XLA Ops:
  23.7 1.7 %copy-start.4 = (bf16[256,1536]{0,1:T(8,128)(2,1)}, bf16[256,1536]{0,1:T(8,128)(2,1)S(1)}, u32[]{:S(2)}) copy-start(bf16[256,1536]{0,1:T(8,128)(2,1)S(1)} %all_gather.9) | copy-start | bytes 2359300
  23.7 1.1 copy-start.12
  23.7 1.1 copy-start.13
  23.7 1.4 copy-start.11
  23.7 1.7 %copy-start.2 = (bf16[1536,384]{1,0:T(8,128)(2,1)S(1)}, bf16[1536,384]{1,0:T(8,128)(2,1)}, u32[]{:S(2)}) copy-start(bf16[1536,384]{1,0:T(8,128)(2,1)} %up_ref.1) | copy-start | bytes 3538948
  23.7 1.7 %copy-start.8 = (f32[1536]{0:T(1024)S(1)}, f32[1536]{0:T(1024)}, u32[]{:S(2)}) copy-start(f32[1536]{0:T(1024)} %param.14) | copy-start | bytes 18436
  23.7 1.7 %copy-start.14 = (f32[1536]{0:T(1024)S(1)}, f32[1536]{0:T(1024)}, u32[]{:S(2)}) copy-start(f32[1536]{0:T(1024)} %param.15) | copy-start | bytes 18436
  23.7 1.6 %copy-start.15 = (f32[384]{0:T(512)S(1)}, f32[384]{0:T(512)}, u32[]{:S(2)}) copy-start(f32[384]{0:T(512)} %param.17) | copy-start | bytes 4612
  24.5 1.9 %copy-start.9 = (f32[128]{0:T(128)}, f32[128]{0:T(128)S(1)}, u32[]{:S(2)}) copy-start(f32[128]{0:T(128)S(1)} %broadcast_multiply_fusion.1) | copy-start | bytes 1540
  25.4 1.3 copy-start
  28.4 52.4 %all-to-all-start = ((bf16[32,16,1664]{2,1,0:T(8,128)(2,1)}), bf16[32,16,1664]{2,1,0:T(8,128)(2,1)S(1)}, u32[]{:S(2)}, u32[]{:S(2)}) async-start(bf16[32,16,1664]{2,1,0:T(8,128)(2,1)} %broadcast_in_dim.91), calls=%async_computation | async-start | bytes 3407872 | tf_op jit(solution)/shard_map/all_to_all | solution.py:404
  39.4 3.4 %collective-permute-start = (bf16[4,16,1536]{2,1,0:T(8,128)(2,1)S(1)}, bf16[4,16,1536]{2,1,0:T(8,128)(2,1)S(1)}, u32[]{:S(2)}, u32[]{:S(2)}) collective-permute-start(bf16[4,16,1536]{2,1,0:T(8,128)(2,1)S(1)} %fusion.13), channel_id=1, source_target_pairs={{0,1},{1,0},{2,3},{3,2},{4,5},{5,4},{6,7},{7,6},{8,9},{9,8},{10,11... | collective-permute-start | bytes 589832 | tf_op jit(solution)/shard_map/ppermute | solution.py:398
  43.4 14.6 %collective-permute-start.1 = (bf16[16,1536]{1,0:T(8,128)(2,1)S(1)}, bf16[16,1536]{1,0:T(8,128)(2,1)S(1)}, u32[]{:S(2)}, u32[]{:S(2)}) collective-permute-start(bf16[16,1536]{1,0:T(8,128)(2,1)S(1)} %get-tuple-element.37), channel_id=1, source_target_pairs={{0,4},{2,6},{4,0},{6,2},{1,5},{3,7},{5,1},{7,3},{8,12},{10,14},{12... | collective-permute-start | bytes 147464 | tf_op jit(solution)/shard_map/ppermute | solution.py:409
  48.6 9.4 %collective-permute-start.2 = (bf16[16,1536]{1,0:T(8,128)(2,1)S(1)}, bf16[16,1536]{1,0:T(8,128)(2,1)S(1)}, u32[]{:S(2)}, u32[]{:S(2)}) collective-permute-start(bf16[16,1536]{1,0:T(8,128)(2,1)S(1)} %get-tuple-element.38), channel_id=1, source_target_pairs={{0,2},{2,4},{4,6},{6,0},{1,3},{3,5},{5,7},{7,1},{8,10},{10,12},{12... | collective-permute-start | bytes 147464 | tf_op jit(solution)/shard_map/ppermute | solution.py:409
  50.5 7.5 %collective-permute-start.3 = (bf16[16,1536]{1,0:T(8,128)(2,1)S(1)}, bf16[16,1536]{1,0:T(8,128)(2,1)S(1)}, u32[]{:S(2)}, u32[]{:S(2)}) collective-permute-start(bf16[16,1536]{1,0:T(8,128)(2,1)S(1)} %get-tuple-element.39), channel_id=1, source_target_pairs={{0,6},{2,0},{4,2},{6,4},{1,7},{3,1},{5,3},{7,5},{8,14},{10,8},{12,... | collective-permute-start | bytes 147464 | tf_op jit(solution)/shard_map/ppermute | solution.py:409
  80.7 5.4 %copy-start.5 = (bf16[256,1536]{0,1:T(8,128)(2,1)S(1)}, bf16[256,1536]{0,1:T(8,128)(2,1)}, u32[]{:S(2)}) copy-start(bf16[256,1536]{0,1:T(8,128)(2,1)} %copy-done.4) | copy-start | bytes 2359300
  80.7 5.5 %copy-start.10 = (f32[128]{0:T(128)S(1)}, f32[128]{0:T(128)}, u32[]{:S(2)}) copy-start(f32[128]{0:T(128)} %copy-done.9) | copy-start | bytes 1540
  82.7 5.0 %collective-permute-start.4 = (bf16[128,1536]{1,0:T(8,128)(2,1)}, bf16[128,1536]{1,0:T(8,128)(2,1)S(1)}, u32[]{:S(2)}, u32[]{:S(2)}) collective-permute-start(bf16[128,1536]{1,0:T(8,128)(2,1)} %get-tuple-element.42), channel_id=1, source_target_pairs={{0,1},{1,0},{2,3},{3,2},{4,5},{5,4},{6,7},{7,6},{8,9},{9,8},{10,11... | collective-permute-start | bytes 1179656 | tf_op jit(solution)/shard_map/ppermute | solution.py:415
  89.7 5.2 %copy-start.6 = (f32[128,1536]{0,1:T(8,128)S(1)}, f32[128,1536]{0,1:T(8,128)}, u32[]{:S(2)}) copy-start(f32[128,1536]{0,1:T(8,128)} %fusion) | copy-start | bytes 2359300
  89.7 16.5 %all-to-all-start.1 = ((bf16[8,16,1536]{2,1,0:T(8,128)(2,1)}), bf16[8,16,1536]{2,1,0:T(8,128)(2,1)S(1)}, u32[]{:S(2)}, u32[]{:S(2)}) async-start(bf16[8,16,1536]{2,1,0:T(8,128)(2,1)} %bitcast.11), calls=%async_computation.1 | async-start | bytes 786432 | tf_op jit(solution)/shard_map/all_to_all | solution.py:423
  95.2 12.3 %collective-permute-start.5 = (bf16[128,384]{1,0:T(8,128)(2,1)S(1)}, bf16[128,384]{1,0:T(8,128)(2,1)S(1)}, u32[]{:S(2)}, u32[]{:S(2)}) collective-permute-start(bf16[128,384]{1,0:T(8,128)(2,1)S(1)} %get-tuple-element.50.hidden_ref), channel_id=1, source_target_pairs={{0,8},{8,0},{1,9},{9,1},{2,10},{10,2},{3,11},{11,3},{4,12},{12,4},... | collective-permute-start | bytes 294920 | tf_op jit(solution)/shard_map/ppermute | solution.py:421
  107.5 23.7 %copy-start.3 = (bf16[1536,384]{1,0:T(8,128)(2,1)S(1)}, bf16[1536,384]{1,0:T(8,128)(2,1)}, u32[]{:S(2)}) copy-start(bf16[1536,384]{1,0:T(8,128)(2,1)} %up_ref.1) | copy-start | bytes 3538948
  124.4 6.8 %copy-start.1 = (bf16[384,1536]{1,0:T(8,128)(2,1)S(1)}, bf16[384,1536]{1,0:T(8,128)(2,1)}, u32[]{:S(2)}) copy-start(bf16[384,1536]{1,0:T(8,128)(2,1)} %down_ref.1) | copy-start | bytes 3538948
  132.9 11.3 %copy-start.7 = (bf16[128,192]{0,1:T(8,128)(2,1)S(1)}, bf16[128,192]{0,1:T(8,128)(2,1)}, u32[]{:S(2)}) copy-start(bf16[128,192]{0,1:T(8,128)(2,1)} %param.13) | copy-start | bytes 147460
  134.6 27.1 %all-to-all-start.3 = ((bf16[32,80,128]{2,1,0:T(8,128)(2,1)}), bf16[32,80,128]{2,1,0:T(8,128)(2,1)S(1)}, u32[]{:S(2)}, u32[]{:S(2)}) async-start(bf16[32,80,128]{2,1,0:T(8,128)(2,1)} %shard_map.154), calls=%async_computation.3 | async-start | bytes 1310720 | tf_op jit(solution)/shard_map/all_to_all | solution.py:448
  144.2 3.6 %collective-permute-start.6 = (bf16[784,128]{1,0:T(8,128)(2,1)S(1)}, bf16[784,128]{1,0:T(8,128)(2,1)S(1)}, u32[]{:S(2)}, u32[]{:S(2)}) collective-permute-start(bf16[784,128]{1,0:T(8,128)(2,1)S(1)} %get-tuple-element.56), channel_id=1, source_target_pairs={{0,1},{1,0},{2,3},{3,2},{4,5},{5,4},{6,7},{7,6},{8,9},{9,8},{10,11... | collective-permute-start | bytes 602120 | tf_op jit(solution)/shard_map/ppermute | solution.py:449
  148.5 10.7 %collective-permute-start.7 = (bf16[208,128]{1,0:T(8,128)(2,1)S(1)}, bf16[208,128]{1,0:T(8,128)(2,1)S(1)}, u32[]{:S(2)}, u32[]{:S(2)}) collective-permute-start(bf16[208,128]{1,0:T(8,128)(2,1)S(1)} %get-tuple-element.59), channel_id=1, source_target_pairs={{0,4},{2,6},{4,0},{6,2},{1,5},{3,7},{5,1},{7,3},{8,12},{10,14},{12... | collective-permute-start | bytes 159752 | tf_op jit(solution)/shard_map/ppermute | solution.py:451
  151.5 7.6 %collective-permute-start.8 = (bf16[208,128]{1,0:T(8,128)(2,1)S(1)}, bf16[208,128]{1,0:T(8,128)(2,1)S(1)}, u32[]{:S(2)}, u32[]{:S(2)}) collective-permute-start(bf16[208,128]{1,0:T(8,128)(2,1)S(1)} %get-tuple-element.60), channel_id=1, source_target_pairs={{0,2},{2,4},{4,6},{6,0},{1,3},{3,5},{5,7},{7,1},{8,10},{10,12},{12... | collective-permute-start | bytes 159752 | tf_op jit(solution)/shard_map/ppermute | solution.py:451
  155.3 6.3 %collective-permute-start.9 = (bf16[208,128]{1,0:T(8,128)(2,1)S(1)}, bf16[208,128]{1,0:T(8,128)(2,1)S(1)}, u32[]{:S(2)}, u32[]{:S(2)}) collective-permute-start(bf16[208,128]{1,0:T(8,128)(2,1)S(1)} %get-tuple-element.61), channel_id=1, source_target_pairs={{0,6},{2,0},{4,2},{6,4},{1,7},{3,1},{5,3},{7,5},{8,14},{10,8},{12,... | collective-permute-start | bytes 159752 | tf_op jit(solution)/shard_map/ppermute | solution.py:451
